TPU v7x, 32 devices: a whole 2x2x4 slice. The times are simulated.
32 devices in a mesh: row: 4 (over y, x), blk: 8 (over z, core).
Axes of the slice: x: 2, y: 2, z: 4, core: 2. Of those that a mesh axis runs over, the one named last changes fastest.
Arguments:
- hidden_in: bfloat16 [4, 1024, 2048], P('row', 'blk'), may hold values from -6 to 6
- segment_ids: int32 [4, 1024], P('row', 'blk'), may hold values from 0 to 1, as said below
- expert_ids: int32 [4, 1024, 8], P('row', 'blk'), may hold values from 0 to 15, all different within a row; in each aligned block of 128 rows (0 to 127, 128 to 255, ..., all dimensions but the last counted through in order) at most 96 rows name the same one
- attention_gain: bfloat16 [2048], P(('row', 'blk')), may hold values from 0.5 to 1.5
- query_gain: bfloat16 [2048], P(('row', 'blk')), may hold values from 0.5 to 1.5
- key_gain: bfloat16 [2048], P(('row', 'blk')), may hold values from 0.5 to 1.5
- expert_gain: bfloat16 [2048], P(('row', 'blk')), may hold values from 0.5 to 1.5
- query_weight: bfloat16 [2048, 2048], P(('row', 'blk')), may hold values from -0.125 to 0.125
- key_weight: bfloat16 [2048, 2048], P(('row', 'blk')), may hold values from -0.125 to 0.125
- value_weight: bfloat16 [2048, 2048], P(('row', 'blk')), may hold values from -0.125 to 0.125
- output_weight: bfloat16 [2048, 2048], P(('row', 'blk')), may hold values from -1 to 1
- router_weight: bfloat16 [2048, 16], P(('row', 'blk')), may hold values from -0.0625 to 0.0625
- gate_weight: bfloat16 [32, 2048, 512], P(('row', 'blk')), may hold values from -0.125 to 0.125
- up_weight: bfloat16 [32, 2048, 512], P(('row', 'blk')), may hold values from -0.125 to 0.125
- down_weight: bfloat16 [32, 512, 2048], P(('row', 'blk')), may hold values from -0.75 to 0.75
- grad_out: bfloat16 [4, 1024, 2048], P('row', 'blk'), may hold values from -6 to 6
Outputs:
- layer_out: bfloat16 [4, 1024, 2048], P('row', 'blk')
- input_grad: float32 [4, 1024, 2048], P('row', 'blk')
- grad_attention_gain: float32 [2048], P(('row', 'blk'))
- grad_query_gain: float32 [2048], P(('row', 'blk'))
- grad_key_gain: float32 [2048], P(('row', 'blk'))
- grad_expert_gain: float32 [2048], P(('row', 'blk'))
- grad_query_weight: float32 [2048, 2048], P(('row', 'blk'))
- grad_key_weight: float32 [2048, 2048], P(('row', 'blk'))
- grad_value_weight: float32 [2048, 2048], P(('row', 'blk'))
- grad_output_weight: float32 [2048, 2048], P(('row', 'blk'))
- grad_router_weight: float32 [2048, 16], P(('row', 'blk'))
- grad_gate_weight: float32 [32, 2048, 512], P(('row', 'blk'))
- grad_up_weight: float32 [32, 2048, 512], P(('row', 'blk'))
- grad_down_weight: float32 [32, 512, 2048], P(('row', 'blk'))
Inputs may be any that keep to these rules, and one draw needn't show every extreme that they name: `segment_ids`: within a packed row the ids never fall. Each row is either one document or two documents, each of 256 to 768 tokens; in every draw some row is one document. `expert_ids`: each token names 8 different experts. Among the 128 tokens of one device (aligned blocks of a packed row) no expert is named by more than 96 tokens, and in every draw some expert is named by exactly 96 tokens of some device.
All inputs are finite; a program needn't handle non-finite values.
Results may differ from a plain program's by a relative error of at most 0.028.
Values may be sent and summed in bfloat16 or wider, within the bound.
A program may use at most 256 MiB of HBM per device.

v0:
```python
import math

import jax
import jax.numpy as jnp
from jax import lax
from jax.sharding import PartitionSpec as P

HEADS = 16
HEAD_DIM = 128
TOP_K = 8


epsilon = 1e-05
masked_score = -1e30


def passed_along(block, axis, distance):
    devices = range(lax.axis_size(axis))
    route = [((i - distance) % len(devices), i) for i in devices]
    return lax.ppermute(block, axis, route)


def rms_scale(values, norm_gain):
    return (
        values * lax.rsqrt(jnp.mean(values * values, axis=-1, keepdims=True) + epsilon) * norm_gain
    )


def rotate_heads(values, positions):
    half_width = values.shape[-1] // 2
    frequency = jnp.exp(
        -math.log(10000.0) * 2.0 * jnp.arange(half_width, dtype=jnp.float32) / values.shape[-1]
    )
    angles = positions.astype(jnp.float32)[:, None, None] * frequency[None, None, :]
    cosine = jnp.cos(angles)
    sine_part = jnp.sin(angles)
    leading = values[..., :half_width]
    trailing = values[..., half_width:]
    return jnp.concatenate(
        [leading * cosine - trailing * sine_part, trailing * cosine + leading * sine_part], axis=-1
    )


def both_halves(slot_rows, experts_all, capacity):
    row_width = slot_rows.shape[-1]
    spread = jnp.broadcast_to(
        slot_rows.reshape(experts_all, 1, capacity, row_width),
        (experts_all, 2, capacity, row_width),
    )
    return spread.reshape(2 * experts_all, capacity, row_width)


def add_halves(returned, experts_all, capacity):
    row_width = returned.shape[-1]
    return jnp.sum(
        returned.reshape(experts_all, 2, capacity, row_width).astype(jnp.float32), axis=1
    ).reshape(experts_all * capacity, row_width)


def contract_rows(left_side, right_side):
    return lax.dot_general(
        left_side, right_side, (((0,), (0,)), ((), ())), preferred_element_type=jnp.float32
    )


def contract_cols(left_side, right_side):
    return lax.dot_general(
        left_side, right_side, (((1,), (1,)), ((), ())), preferred_element_type=jnp.float32
    )


def body(
    hidden_in,
    segment_ids,
    expert_ids,
    attention_gain,
    query_gain,
    key_gain,
    expert_gain,
    query_weight,
    key_weight,
    value_weight,
    output_weight,
    router_weight,
    gate_weight,
    up_weight,
    down_weight,
    grad_out,
):
    tokens_here = hidden_in.shape[1]
    model_width = hidden_in.shape[2]
    experts_all = router_weight.shape[1]
    capacity = 3 * tokens_here * TOP_K // (2 * experts_all)
    blocks = lax.axis_size("blk")
    block_index = lax.axis_index("blk")
    score_scale = HEAD_DIM ** (-0.5)
    positions = block_index * tokens_here + jnp.arange(tokens_here, dtype=jnp.int32)
    own_segments = segment_ids[0]
    routes = expert_ids[0]
    gathered = (
        lax.all_gather(attention_gain, ("row", "blk"), axis=0, tiled=True),
        lax.all_gather(query_gain, ("row", "blk"), axis=0, tiled=True),
        lax.all_gather(key_gain, ("row", "blk"), axis=0, tiled=True),
        lax.all_gather(expert_gain, ("row", "blk"), axis=0, tiled=True),
        lax.all_gather(query_weight, ("row", "blk"), axis=0, tiled=True),
        lax.all_gather(key_weight, ("row", "blk"), axis=0, tiled=True),
        lax.all_gather(value_weight, ("row", "blk"), axis=0, tiled=True),
        lax.all_gather(output_weight, ("row", "blk"), axis=0, tiled=True),
        lax.all_gather(router_weight, ("row", "blk"), axis=0, tiled=True),
    )
    gain_attn = gathered[0].astype(jnp.float32)
    gain_query = gathered[1].astype(jnp.float32)
    gain_key = gathered[2].astype(jnp.float32)
    gain_expert = gathered[3].astype(jnp.float32)
    full_query = gathered[4]
    full_key = gathered[5]
    full_value = gathered[6]
    full_output = gathered[7]
    full_router = gathered[8]
    residual_in = hidden_in[0].astype(jnp.float32)
    normed_low = rms_scale(residual_in, gain_attn).astype(jnp.bfloat16)
    query_pre = jnp.dot(normed_low, full_query, preferred_element_type=jnp.float32)
    key_pre = jnp.dot(normed_low, full_key, preferred_element_type=jnp.float32)
    value_low = jnp.dot(normed_low, full_value, preferred_element_type=jnp.float32).astype(
        jnp.bfloat16
    )

    def head_shape(values, norm_gain):
        return rotate_heads(
            rms_scale(values, norm_gain).reshape(tokens_here, HEADS, HEAD_DIM), positions
        )

    query_rot, query_back = jax.vjp(head_shape, query_pre, gain_query)
    key_rot, key_back = jax.vjp(head_shape, key_pre, gain_key)
    query_low = query_rot.astype(jnp.bfloat16)
    key_low = key_rot.astype(jnp.bfloat16).reshape(tokens_here, model_width)
    run_max = jnp.full((HEADS, tokens_here), masked_score, jnp.float32)
    key_piece = lax.all_gather(key_low, "blk", axis=0, tiled=True)
    value_piece = lax.all_gather(value_low, "blk", axis=0, tiled=True)
    segment_piece = lax.all_gather(own_segments, "blk", axis=0, tiled=True)
    key_count = key_piece.shape[0]
    key_heads = key_piece.reshape(key_count, HEADS, HEAD_DIM)
    value_heads = value_piece.reshape(key_count, HEADS, HEAD_DIM)
    key_positions = jnp.arange(key_count, dtype=jnp.int32)
    allowed = (key_positions[None, :] <= positions[:, None]) & (
        segment_piece[None, :] == own_segments[:, None]
    )
    scores = (
        jnp.einsum("qhd,khd->hqk", query_low, key_heads, preferred_element_type=jnp.float32)
        * score_scale
    )
    scores = jnp.where(allowed[None], scores, masked_score)
    new_max = jnp.maximum(run_max, jnp.max(scores, axis=-1))
    weights = jnp.where(allowed[None], jnp.exp(scores - new_max[:, :, None]), 0.0)
    run_total = jnp.sum(weights, axis=-1)
    run_acc = jnp.einsum(
        "hqk,khd->hqd",
        weights.astype(jnp.bfloat16),
        value_heads,
        preferred_element_type=jnp.float32,
    )
    run_max, run_total, run_acc = (new_max, run_total, run_acc)
    log_total = run_max + jnp.log(run_total)
    attended = jnp.transpose(run_acc / run_total[:, :, None], (1, 0, 2)).reshape(
        tokens_here, model_width
    )
    attended_low = attended.astype(jnp.bfloat16)
    residual_mid = residual_in + jnp.dot(
        attended_low, full_output, preferred_element_type=jnp.float32
    )
    expert_in = rms_scale(residual_mid, gain_expert).astype(jnp.bfloat16)
    logits = jnp.dot(expert_in, full_router, preferred_element_type=jnp.float32)
    route_hot = (
        routes[:, :, None] == jnp.arange(experts_all, dtype=jnp.int32)[None, None, :]
    ).astype(jnp.float32)
    picked = jnp.sum(route_hot * logits[:, None, :], axis=-1)
    gate_probs = jax.nn.softmax(picked, axis=-1)
    flat_routes = routes.reshape(-1)
    pair_count = flat_routes.shape[0]
    route_ones = (flat_routes[:, None] == jnp.arange(experts_all, dtype=jnp.int32)[None, :]).astype(
        jnp.int32
    )
    earlier = jnp.cumsum(route_ones, axis=0) - route_ones
    places = jnp.sum(earlier * route_ones, axis=1)
    slot_of_pair = flat_routes * capacity + places
    pair_of_slot = (
        jnp.zeros((experts_all * capacity,), jnp.int32)
        .at[slot_of_pair]
        .set(jnp.arange(pair_count, dtype=jnp.int32))
    )
    slot_live = jnp.zeros((experts_all * capacity,), jnp.int32).at[slot_of_pair].set(1) > 0
    token_of_slot = pair_of_slot // TOP_K
    send_rows = jnp.where(slot_live[:, None], expert_in[token_of_slot], 0)
    dispatched = both_halves(send_rows, experts_all, capacity)
    gate_local = gate_weight[0]
    up_local = up_weight[0]
    down_local = down_weight[0]
    arrived = lax.all_to_all(dispatched, ("row", "blk"), split_axis=0, concat_axis=0, tiled=True)
    sources = arrived.shape[0]
    slot_count = arrived.shape[1]
    flat_rows = arrived.reshape(sources * slot_count, model_width)
    gate_pre = jnp.dot(flat_rows, gate_local, preferred_element_type=jnp.float32)
    up_pre = jnp.dot(flat_rows, up_local, preferred_element_type=jnp.float32)
    hidden_low = (jax.nn.silu(gate_pre) * up_pre).astype(jnp.bfloat16)
    part_out = jnp.dot(hidden_low, down_local, preferred_element_type=jnp.float32).astype(
        jnp.bfloat16
    )
    returned = lax.all_to_all(
        part_out.reshape(sources, slot_count, model_width),
        ("row", "blk"),
        split_axis=0,
        concat_axis=0,
        tiled=True,
    )
    returned, kept_rows = (returned, arrived)
    combined = add_halves(returned, experts_all, capacity)
    pair_out = combined[slot_of_pair].reshape(tokens_here, TOP_K, model_width)
    moe_out = jnp.sum(gate_probs[:, :, None] * pair_out, axis=1)
    layer_out = (residual_mid + moe_out).astype(jnp.bfloat16)
    upstream = grad_out[0].astype(jnp.float32)
    grad_gates = jnp.sum(pair_out * upstream[:, None, :], axis=-1)
    grad_pairs = (
        (gate_probs[:, :, None] * upstream[:, None, :])
        .astype(jnp.bfloat16)
        .reshape(pair_count, model_width)
    )
    grad_slots = jnp.where(slot_live[:, None], grad_pairs[pair_of_slot], 0)
    grad_send = both_halves(grad_slots, experts_all, capacity)
    expert_rows, expert_grads = (
        lax.all_to_all(dispatched, ("row", "blk"), split_axis=0, concat_axis=0, tiled=True),
        lax.all_to_all(grad_send, ("row", "blk"), split_axis=0, concat_axis=0, tiled=True),
    )
    flat_rows = expert_rows.reshape(-1, model_width)
    flat_grads = expert_grads.reshape(-1, model_width)
    gate_pre = jnp.dot(flat_rows, gate_local, preferred_element_type=jnp.float32)
    up_pre = jnp.dot(flat_rows, up_local, preferred_element_type=jnp.float32)
    gate_sigmoid = jax.nn.sigmoid(gate_pre)
    silu_value = jax.nn.silu(gate_pre)
    hidden_low = (silu_value * up_pre).astype(jnp.bfloat16)
    grad_hidden = contract_cols(flat_grads, down_local)
    grad_down_local = contract_rows(hidden_low, flat_grads)
    grad_gate_pre = (
        grad_hidden * up_pre * gate_sigmoid * (1.0 + gate_pre * (1.0 - gate_sigmoid))
    ).astype(jnp.bfloat16)
    grad_up_pre = (grad_hidden * silu_value).astype(jnp.bfloat16)
    grad_gate_local = contract_rows(flat_rows, grad_gate_pre)
    grad_up_local = contract_rows(flat_rows, grad_up_pre)
    grad_rows = (
        contract_cols(grad_gate_pre, gate_local) + contract_cols(grad_up_pre, up_local)
    ).astype(jnp.bfloat16)
    returned_grads = lax.all_to_all(
        grad_rows.reshape(expert_rows.shape),
        ("row", "blk"),
        split_axis=0,
        concat_axis=0,
        tiled=True,
    )
    grad_slots_in = add_halves(returned_grads, experts_all, capacity)
    grad_expert_in = jnp.sum(
        grad_slots_in[slot_of_pair].reshape(tokens_here, TOP_K, model_width), axis=1
    )
    grad_picked = gate_probs * (
        grad_gates - jnp.sum(gate_probs * grad_gates, axis=-1, keepdims=True)
    )
    grad_logits = jnp.sum(route_hot * grad_picked[:, :, None], axis=1).astype(jnp.bfloat16)
    grad_expert_in = grad_expert_in + contract_cols(grad_logits, full_router)
    grad_router = contract_rows(expert_in, grad_logits)
    ignored, norm_two_back = jax.vjp(rms_scale, residual_mid, gain_expert)
    grad_mid_norm, grad_gain_expert = norm_two_back(grad_expert_in)
    grad_mid = upstream + grad_mid_norm
    grad_proj = grad_mid.astype(jnp.bfloat16)
    grad_output_w = contract_rows(attended_low, grad_proj)
    grad_attended = (
        contract_cols(grad_proj, full_output)
        .astype(jnp.bfloat16)
        .reshape(tokens_here, HEADS, HEAD_DIM)
    )
    row_delta = jnp.sum(
        grad_attended.astype(jnp.float32) * attended.reshape(tokens_here, HEADS, HEAD_DIM), axis=-1
    ).T

    def key_block_grads(key_piece, value_piece, segment_piece, key_start):
        key_count = key_piece.shape[0]
        key_heads = key_piece.reshape(key_count, HEADS, HEAD_DIM)
        value_heads = value_piece.reshape(key_count, HEADS, HEAD_DIM)
        key_positions = key_start + jnp.arange(key_count, dtype=jnp.int32)
        allowed = (key_positions[None, :] <= positions[:, None]) & (
            segment_piece[None, :] == own_segments[:, None]
        )
        scores = (
            jnp.einsum("qhd,khd->hqk", query_low, key_heads, preferred_element_type=jnp.float32)
            * score_scale
        )
        probabilities = jnp.where(allowed[None], jnp.exp(scores - log_total[:, :, None]), 0.0)
        grad_value = jnp.einsum(
            "hqk,qhd->khd",
            probabilities.astype(jnp.bfloat16),
            grad_attended,
            preferred_element_type=jnp.float32,
        )
        grad_probs = jnp.einsum(
            "qhd,khd->hqk", grad_attended, value_heads, preferred_element_type=jnp.float32
        )
        grad_scores = (probabilities * (grad_probs - row_delta[:, :, None])).astype(jnp.bfloat16)
        grad_query = (
            jnp.einsum("hqk,khd->qhd", grad_scores, key_heads, preferred_element_type=jnp.float32)
            * score_scale
        )
        grad_key = (
            jnp.einsum("hqk,qhd->khd", grad_scores, query_low, preferred_element_type=jnp.float32)
            * score_scale
        )
        return (
            grad_query,
            grad_key.reshape(key_count, model_width),
            grad_value.reshape(key_count, model_width),
        )

    def turn(step_index, loop_state):
        key_piece, value_piece, segment_piece, grad_key_acc, grad_value_acc, grad_query_acc = (
            loop_state
        )
        anchor = (block_index + step_index) % blocks
        grad_query, grad_key, grad_value = key_block_grads(
            key_piece, value_piece, segment_piece, anchor * tokens_here
        )
        key_piece, value_piece, segment_piece = passed_along(
            (key_piece, value_piece, segment_piece), "blk", -1
        )
        grad_key_acc, grad_value_acc = (
            passed_along((grad_key_acc + grad_key).astype(jnp.bfloat16), "blk", -1).astype(
                jnp.float32
            ),
            passed_along((grad_value_acc + grad_value).astype(jnp.bfloat16), "blk", -1).astype(
                jnp.float32
            ),
        )
        return (
            key_piece,
            value_piece,
            segment_piece,
            grad_key_acc,
            grad_value_acc,
            grad_query_acc + grad_query,
        )

    first_state = (
        key_low,
        value_low,
        own_segments,
        jnp.zeros((tokens_here, model_width), jnp.float32),
        jnp.zeros((tokens_here, model_width), jnp.float32),
        jnp.zeros((tokens_here, HEADS, HEAD_DIM), jnp.float32),
    )
    final_state = lax.fori_loop(0, blocks, turn, first_state)
    grad_key_home = final_state[3]
    grad_value_home = final_state[4]
    grad_query_all = final_state[5]
    grad_query_pre, grad_gain_query = query_back(grad_query_all)
    grad_key_pre, grad_gain_key = key_back(grad_key_home.reshape(tokens_here, HEADS, HEAD_DIM))
    grad_query_low = grad_query_pre.astype(jnp.bfloat16)
    grad_key_low = grad_key_pre.astype(jnp.bfloat16)
    grad_value_low = grad_value_home.astype(jnp.bfloat16)
    grad_query_w = contract_rows(normed_low, grad_query_low)
    grad_key_w = contract_rows(normed_low, grad_key_low)
    grad_value_w = contract_rows(normed_low, grad_value_low)
    grad_normed = (
        contract_cols(grad_query_low, full_query)
        + contract_cols(grad_key_low, full_key)
        + contract_cols(grad_value_low, full_value)
    )
    ignored_two, norm_one_back = jax.vjp(rms_scale, residual_in, gain_attn)
    grad_in_norm, grad_gain_attn = norm_one_back(grad_normed)
    input_grad = grad_mid + grad_in_norm
    summed = (
        lax.psum_scatter(grad_gain_attn, ("row", "blk"), scatter_dimension=0, tiled=True),
        lax.psum_scatter(grad_gain_query, ("row", "blk"), scatter_dimension=0, tiled=True),
        lax.psum_scatter(grad_gain_key, ("row", "blk"), scatter_dimension=0, tiled=True),
        lax.psum_scatter(grad_gain_expert, ("row", "blk"), scatter_dimension=0, tiled=True),
        lax.psum_scatter(grad_query_w, ("row", "blk"), scatter_dimension=0, tiled=True),
        lax.psum_scatter(grad_key_w, ("row", "blk"), scatter_dimension=0, tiled=True),
        lax.psum_scatter(grad_value_w, ("row", "blk"), scatter_dimension=0, tiled=True),
        lax.psum_scatter(grad_output_w, ("row", "blk"), scatter_dimension=0, tiled=True),
        lax.psum_scatter(grad_router, ("row", "blk"), scatter_dimension=0, tiled=True),
    )
    return (
        layer_out[None],
        input_grad[None],
        summed[0],
        summed[1],
        summed[2],
        summed[3],
        summed[4],
        summed[5],
        summed[6],
        summed[7],
        summed[8],
        grad_gate_local[None],
        grad_up_local[None],
        grad_down_local[None],
    )


def solution(mesh):
    return jax.shard_map(
        body,
        mesh=mesh,
        in_specs=(
            P("row", "blk", None),
            P("row", "blk"),
            P("row", "blk", None),
            P(("row", "blk")),
            P(("row", "blk")),
            P(("row", "blk")),
            P(("row", "blk")),
            P(("row", "blk"), None),
            P(("row", "blk"), None),
            P(("row", "blk"), None),
            P(("row", "blk"), None),
            P(("row", "blk"), None),
            P(("row", "blk"), None, None),
            P(("row", "blk"), None, None),
            P(("row", "blk"), None, None),
            P("row", "blk", None),
        ),
        out_specs=(
            P("row", "blk", None),
            P("row", "blk", None),
            P(("row", "blk")),
            P(("row", "blk")),
            P(("row", "blk")),
            P(("row", "blk")),
            P(("row", "blk"), None),
            P(("row", "blk"), None),
            P(("row", "blk"), None),
            P(("row", "blk"), None),
            P(("row", "blk"), None),
            P(("row", "blk"), None, None),
            P(("row", "blk"), None, None),
            P(("row", "blk"), None, None),
        ),
        check_vma=False,
    )
```

profile of v0, /device:TPU:0, one launch (start us, length us, event | category | flops | bytes accessed | tf_op | source)
XLA Modules:
  0.0 2660.1 jit_solution(15039476677945121050)
XLA Ops:
  12.9 42.7 %all-reduce.13 = (bf16[2048]{0:T(1024)(128)(2,1)S(1)}, bf16[2048]{0:T(1024)(128)(2,1)S(1)}, bf16[2048]{0:T(1024)(128)(2,1)S(1)}, bf16[2048]{0:T(1024)(128)(2,1)S(1)}) all-reduce(bf16[2048]{0:T(1024)(128)(2,1)S(1)} %dynamic-update-slice, bf16[2048]{0:T(1024)(128)(2,1)S(1)} %dynamic-update-slice.1, ...), channel_id=1, replica_groups=mesh['row'=4,'blk'=8] {'row','blk'}, use_global_device_ids=true, to_apply=%add.4 | all-reduce | flops 8192 | bytes 32768
  56.8 34.8 %all-gather.15.cloned.1.call-done = bf16[2048,2048]{1,0:T(8,128)(2,1)} async-done(((bf16[64,2048]{1,0:T(8,128)(2,1)}), bf16[2048,2048]{1,0:T(8,128)(2,1)}) %all-gather.15.cloned.1.call-update) | async-done | bytes 8388624 | tf_op jit(solution)/shard_map/all_gather | solution.py:107
  91.6 5.7 convolution_convert_fusion.2
  97.8 72.7 %all-gather.11.cloned.1.call-done = bf16[2048,2048]{1,0:T(8,128)(2,1)} async-done(((bf16[64,2048]{1,0:T(8,128)(2,1)}), bf16[2048,2048]{1,0:T(8,128)(2,1)}) %all-gather.11.cloned.1.call-update) | async-done | bytes 8388624 | tf_op jit(solution)/shard_map/all_gather | solution.py:106
  170.5 4.8 multiply_reduce_fusion.6
  177.6 71.9 %all-gather.9.cloned.1.call-done = bf16[2048,2048]{1,0:T(8,128)(2,1)} async-done(((bf16[64,2048]{1,0:T(8,128)(2,1)}), bf16[2048,2048]{1,0:T(8,128)(2,1)}) %all-gather.9.cloned.1.call-update) | async-done | bytes 8388624 | tf_op jit(solution)/shard_map/all_gather | solution.py:105
  249.5 4.9 multiply_reduce_fusion.7
  263.2 4.5 reduce-window.6
  268.2 4.3 scatter_custom_fusion.1
  276.9 40.4 %all-gather.1 = bf16[32,64,16]{1,2,0:T(8,128)(2,1)S(1)} all-gather(bf16[1,64,16]{1,2,0:T(8,128)(2,1)S(1)} %bitcast.306), channel_id=1, replica_groups=mesh['row'=4,'blk'=8] {'row','blk'}, dimensions={0}, use_global_device_ids=true | all-gather | bytes 67584 | tf_op jit(solution)/shard_map/all_gather | solution.py:109
  317.5 9.2 all-gather
  329.6 6.6 copy.171
  336.2 10.0 all-gather.13.cloned.1.call-done
  357.5 67.1 %all-gather.19.cloned.1.call-done = bf16[2048,2048]{1,0:T(8,128)(2,1)} async-done(((bf16[64,2048]{1,0:T(8,128)(2,1)}), bf16[2048,2048]{1,0:T(8,128)(2,1)}) %all-gather.19.cloned.1.call-update) | async-done | bytes 8388624 | tf_op jit(solution)/shard_map/all_gather | solution.py:108
  424.6 4.7 multiply_reduce_fusion.5
  431.7 7.2 gather_fusion
  442.3 15.4 gather_fusion.2
  457.8 5.4 broadcast_select_fusion
  464.8 278.0 %all_to_all.21 = bf16[32,96,2048]{2,1,0:T(8,128)(2,1)} all-to-all(bf16[32,96,2048]{2,1,0:T(8,128)(2,1)S(1)} %bitcast.272), channel_id=1, replica_groups=mesh['row'=4,'blk'=8] {'row','blk'}, dimensions={0} | all-to-all | bytes 25165824 | tf_op jit(solution)/shard_map/all_to_all | solution.py:198
  742.8 5.5 broadcast_in_dim.191
  752.1 12.2 fusion.38
  764.2 11.3 fusion.42
  775.6 251.3 %all-to-all-done.2 = bf16[32,96,2048]{2,1,0:T(8,128)(2,1)} async-done(((bf16[32,96,2048]{2,1,0:T(8,128)(2,1)}), bf16[32,96,2048]{2,1,0:T(8,128)(2,1)}, u32[]{:S(2)}, u32[]{:S(2)}) %all-to-all-start.2) | async-done | bytes 12582944 | tf_op jit(solution)/shard_map/all_to_all | solution.py:231
  1026.9 17.7 multiply_convert_fusion
  1044.6 9.9 convolution_convert_fusion
  1058.4 13.7 fusion.40
  1072.1 16.0 add_convert_fusion
  1088.1 245.1 %all-to-all-done.1 = bf16[32,96,2048]{2,1,0:T(8,128)(2,1)} async-done(((bf16[32,96,2048]{2,1,0:T(8,128)(2,1)}), bf16[32,96,2048]{2,1,0:T(8,128)(2,1)}, u32[]{:S(2)}, u32[]{:S(2)}) %all-to-all-start.1) | async-done | bytes 12582944 | tf_op jit(solution)/shard_map/all_to_all | solution.py:208
  1337.1 13.2 convert_reduce_fusion.1
  1350.3 13.6 gather_fusion.1
  1364.0 5.3 fusion.22
  1370.8 251.9 %all-to-all-done.3 = bf16[32,96,2048]{2,1,0:T(8,128)(2,1)} async-done(((bf16[32,96,2048]{2,1,0:T(8,128)(2,1)}), bf16[32,96,2048]{2,1,0:T(8,128)(2,1)}, u32[]{:S(2)}, u32[]{:S(2)}) %all-to-all-start.3) | async-done | bytes 12582944 | tf_op jit(solution)/shard_map/all_to_all | solution.py:251
  1622.7 12.8 convert_reduce_fusion
  1635.5 13.6 gather_fusion.3
  1649.2 5.5 bitcast_reduce_fusion
  1656.5 8.1 fusion.68
  1666.2 7.0 convolution_convert_fusion.1
  1674.9 405.7 %while.26 = (s32[]{:T(128)}, bf16[128,2048]{1,0:T(8,128)(2,1)S(1)}, bf16[128,2048]{1,0:T(8,128)(2,1)S(1)}, s32[128]{0:T(128)S(1)}, f32[128,2048]{0,1:T(8,128)}, ...) while((s32[]{:T(128)}, bf16[128,2048]{1,0:T(8,128)(2,1)S(1)}, ...), condition=%wide.region_24.25_spmd.clone, body=%wide.region_23.24_spmd.clone.sunk | while | flops 340574464 | bytes 46193328 | solution.py:355
  1685.5 13.1 collective-permute-done.3
  1700.7 14.8 collective-permute-done.4
  1717.5 31.6 %collective-permute-done.2 = s32[128]{0:T(128)S(1)} collective-permute-done((s32[128]{0:T(128)S(1)}, s32[128]{0:T(128)S(1)}, u32[]{:S(2)}, u32[]{:S(2)}) %collective-permute-start.2) | collective-permute-done | bytes 544 | tf_op jit(solution)/shard_map/while/body/eval_jaxpr/ppermute | solution.py:20
  1766.4 11.5 collective-permute-done.3
  1780.0 14.8 collective-permute-done.4
  1796.8 31.6 %collective-permute-done.2 = s32[128]{0:T(128)S(1)} collective-permute-done((s32[128]{0:T(128)S(1)}, s32[128]{0:T(128)S(1)}, u32[]{:S(2)}, u32[]{:S(2)}) %collective-permute-start.2) | collective-permute-done | bytes 544 | tf_op jit(solution)/shard_map/while/body/eval_jaxpr/ppermute | solution.py:20
  1845.6 11.5 collective-permute-done.3
  1859.2 14.8 collective-permute-done.4
  1876.1 31.6 %collective-permute-done.2 = s32[128]{0:T(128)S(1)} collective-permute-done((s32[128]{0:T(128)S(1)}, s32[128]{0:T(128)S(1)}, u32[]{:S(2)}, u32[]{:S(2)}) %collective-permute-start.2) | collective-permute-done | bytes 544 | tf_op jit(solution)/shard_map/while/body/eval_jaxpr/ppermute | solution.py:20
  1933.1 9.1 collective-permute-done.2
  1967.7 9.1 collective-permute-done.2
  2002.3 9.1 collective-permute-done.2
  2036.9 9.1 collective-permute-done.2
  2071.5 9.1 collective-permute-done.2
  2080.7 9.4 fusion.65
  2095.9 4.4 multiply_add_fusion.1
  2101.3 8.2 fusion.95
  2114.6 8.2 fusion.97
  2122.9 12.2 convolution_bitcast_fusion
  2135.0 11.2 convolution_bitcast_fusion.1
  2146.3 8.5 convolution_bitcast_fusion.2
  2154.8 6.5 fusion.109
  2168.4 41.4 %all-reduce.12 = (f32[2048]{0:T(1024)S(1)}, f32[2048]{0:T(1024)S(1)}, f32[2048]{0:T(1024)S(1)}, f32[2048]{0:T(1024)S(1)}) all-reduce(f32[2048]{0:T(1024)S(1)} %get-tuple-element.476, f32[2048]{0:T(1024)S(1)} %get-tuple-element.474, f32[2048]{0:T(1024)S(1)} %get-tuple-element.472, ...), channel_id=3, replica_groups=mesh['row'=4,'blk'=8] {'row','blk'}, use_global_device_ids=true, to_apply=%region_29.30.clone | all-reduce | flops 8192 | bytes 65536
  2216.4 62.2 %reduce-scatter.12.cloned.1.call-done = f32[64,2048]{1,0:T(8,128)} async-done(((f32[2048,2048]{1,0:T(8,128)}), f32[64,2048]{1,0:T(8,128)}) %reduce-scatter.12.cloned.1.call-update) | async-done | bytes 524304 | tf_op jit(solution)/shard_map/reduce_scatter | solution.py:382
  2278.6 187.2 %reduce-scatter.10.cloned.1.call-done = f32[64,2048]{1,0:T(8,128)} async-done(((f32[2048,2048]{1,0:T(8,128)}), f32[64,2048]{1,0:T(8,128)}) %reduce-scatter.10.cloned.1.call-update) | async-done | bytes 524304 | tf_op jit(solution)/shard_map/reduce_scatter | solution.py:381
  2465.8 187.4 %reduce-scatter.8.cloned.1.call-done = f32[64,2048]{1,0:T(8,128)} async-done(((f32[2048,2048]{1,0:T(8,128)}), f32[64,2048]{1,0:T(8,128)}) %reduce-scatter.8.cloned.1.call-update) | async-done | bytes 524304 | tf_op jit(solution)/shard_map/reduce_scatter | solution.py:380
  (609 shorter events, 271.4 us)
Async XLA Ops:
  7.2 1019.7 %copy-start = (bf16[1,512,2048]{2,1,0:T(8,128)(2,1)S(1)}, bf16[1,512,2048]{2,1,0:T(8,128)(2,1)}, u32[]{:S(2)}) copy-start(bf16[1,512,2048]{2,1,0:T(8,128)(2,1)} %param.32) | copy-start | bytes 6291460
  7.2 84.4 %all-gather.15.cloned.1.call-start = ((), (), s32[]{:S(2)}) async-start(), calls=%async_computation.12 | async-start | bytes 8650752 | tf_op jit(solution)/shard_map/all_gather | solution.py:107
  7.9 162.6 %all-gather.11.cloned.1.call-start = ((), (), s32[]{:S(2)}) async-start(), calls=%async_computation.10 | async-start | bytes 8650752 | tf_op jit(solution)/shard_map/all_gather | solution.py:106
  8.7 240.8 %all-gather.9.cloned.1.call-start = ((), (), s32[]{:S(2)}) async-start(), calls=%async_computation.9 | async-start | bytes 8650752 | tf_op jit(solution)/shard_map/all_gather | solution.py:105
  9.4 320.2 %all-gather.17.cloned.1.call-start = ((), (), s32[]{:S(2)}) async-start(), calls=%async_computation.13 | async-start | bytes 4718592 | tf_op jit(solution)/shard_map/all_gather | solution.py:139
  55.6 193.9 %copy-start.34 = (f32[2048]{0:T(1024)}, f32[2048]{0:T(1024)S(1)}, u32[]{:S(2)}) copy-start(f32[2048]{0:T(1024)S(1)} %convert_element_type.189) | copy-start | bytes 24580
  56.8 192.7 %copy-start.54 = (f32[128]{0:T(128)}, f32[128]{0:T(128)S(1)}, u32[]{:S(2)}) copy-start(f32[128]{0:T(128)S(1)} %fusion.86) | copy-start | bytes 1540
  97.3 248.8 %all-gather.13.cloned.1.call-start = ((), (), s32[]{:S(2)}) async-start(), calls=%async_computation.11 | async-start | bytes 4718592 | tf_op jit(solution)/shard_map/all_gather | solution.py:138
  97.8 158.8 %copy-start.38 = (f32[128,64]{1,0:T(8,128)}, f32[128,64]{1,0:T(8,128)S(1)}, u32[]{:S(2)}) copy-start(f32[128,64]{1,0:T(8,128)S(1)} %get-tuple-element.541) | copy-start | bytes 98308
  97.8 158.8 %copy-start.40 = (f32[128,64]{1,0:T(8,128)}, f32[128,64]{1,0:T(8,128)S(1)}, u32[]{:S(2)}) copy-start(f32[128,64]{1,0:T(8,128)S(1)} %get-tuple-element.542) | copy-start | bytes 98308
  262.0 162.6 %all-gather.19.cloned.1.call-start = ((), (), s32[]{:S(2)}) async-start(), calls=%async_computation.14 | async-start | bytes 8650752 | tf_op jit(solution)/shard_map/all_gather | solution.py:108
  262.9 166.5 %copy-start.52 = (f32[2048]{0:T(1024)}, f32[2048]{0:T(1024)S(1)}, u32[]{:S(2)}) copy-start(f32[2048]{0:T(1024)S(1)} %convert_element_type.199) | copy-start | bytes 24580
  748.3 278.6 %all-to-all-start.2 = ((bf16[32,96,2048]{2,1,0:T(8,128)(2,1)}), bf16[32,96,2048]{2,1,0:T(8,128)(2,1)}, u32[]{:S(2)}, u32[]{:S(2)}) async-start(bf16[32,96,2048]{2,1,0:T(8,128)(2,1)} %bitcast.271), calls=%async_computation.2 | async-start | bytes 25165824 | tf_op jit(solution)/shard_map/all_to_all | solution.py:231
  1054.4 278.7 %all-to-all-start.1 = ((bf16[32,96,2048]{2,1,0:T(8,128)(2,1)}), bf16[32,96,2048]{2,1,0:T(8,128)(2,1)}, u32[]{:S(2)}, u32[]{:S(2)}) async-start(bf16[32,96,2048]{2,1,0:T(8,128)(2,1)} %bitcast.283), calls=%async_computation.1 | async-start | bytes 25165824 | tf_op jit(solution)/shard_map/all_to_all | solution.py:208
  1333.2 289.6 %all-to-all-start.3 = ((bf16[32,96,2048]{2,1,0:T(8,128)(2,1)}), bf16[32,96,2048]{2,1,0:T(8,128)(2,1)}, u32[]{:S(2)}, u32[]{:S(2)}) async-start(bf16[32,96,2048]{2,1,0:T(8,128)(2,1)} %bitcast.282), calls=%async_computation.3 | async-start | bytes 25165824 | tf_op jit(solution)/shard_map/all_to_all | solution.py:251
  1337.1 877.9 %reduce-scatter.16.cloned.1.call-start = ((), (), s32[]{:S(2)}) async-start(), calls=%async_computation.19 | async-start | bytes 1081344
  1370.8 845.6 %reduce-scatter.14.cloned.1.call-start = ((), (), s32[]{:S(2)}) async-start(), calls=%async_computation.18 | async-start | bytes 17301504 | tf_op jit(solution)/shard_map/reduce_scatter | solution.py:383
  1664.7 613.9 %reduce-scatter.12.cloned.1.call-start = ((), (), s32[]{:S(2)}) async-start(), calls=%async_computation.17 | async-start | bytes 17301504 | tf_op jit(solution)/shard_map/reduce_scatter | solution.py:382
  1674.9 405.7 %copy-start.5 = (bf16[1,128,2048]{2,1,0:T(8,128)(2,1)S(1)}, bf16[1,128,2048]{2,1,0:T(8,128)(2,1)}, u32[]{:S(2)}) copy-start(bf16[1,128,2048]{2,1,0:T(8,128)(2,1)} %param.18) | copy-start | bytes 1572868
  1674.9 405.7 %copy-start.35 = (f32[2048]{0:T(1024)S(1)}, f32[2048]{0:T(1024)}, u32[]{:S(2)}) copy-start(f32[2048]{0:T(1024)} %copy-done.34) | copy-start | bytes 24580
  1674.9 405.7 %copy-start.55 = (f32[128]{0:T(128)S(1)}, f32[128]{0:T(128)}, u32[]{:S(2)}) copy-start(f32[128]{0:T(128)} %copy-done.54) | copy-start | bytes 1540
  1680.6 18.0 collective-permute-start.3
  1683.0 32.4 %collective-permute-start.4 = (bf16[128,2048]{0,1:T(8,128)(2,1)}, bf16[128,2048]{0,1:T(8,128)(2,1)}, u32[]{:S(2)}, u32[]{:S(2)}) collective-permute-start(bf16[128,2048]{0,1:T(8,128)(2,1)} %fusion.193), channel_id=1, source_target_pairs={{1,0},{2,1},{3,2},{4,3},{5,4},{6,5},{7,6},{0,7},{9,8},{10,9},{11,1... | collective-permute-start | bytes 1572872 | tf_op jit(solution)/shard_map/while/body/eval_jaxpr/ppermute | solution.py:20
  1683.0 66.1 %collective-permute-start.1 = (bf16[128,2048]{1,0:T(8,128)(2,1)}, bf16[128,2048]{1,0:T(8,128)(2,1)S(1)}, u32[]{:S(2)}, u32[]{:S(2)}) collective-permute-start(bf16[128,2048]{1,0:T(8,128)(2,1)} %copy-done.9), channel_id=1, source_target_pairs={{1,0},{2,1},{3,2},{4,3},{5,4},{6,5},{7,6},{0,7},{9,8},{10,9},{11,1... | collective-permute-start | bytes 1572872 | tf_op jit(solution)/shard_map/while/body/eval_jaxpr/ppermute | solution.py:20
  1683.0 66.1 %collective-permute-start = (bf16[128,2048]{1,0:T(8,128)(2,1)}, bf16[128,2048]{1,0:T(8,128)(2,1)S(1)}, u32[]{:S(2)}, u32[]{:S(2)}) collective-permute-start(bf16[128,2048]{1,0:T(8,128)(2,1)} %copy-done.10), channel_id=1, source_target_pairs={{1,0},{2,1},{3,2},{4,3},{5,4},{6,5},{7,6},{0,7},{9,8},{10,9},{11,1... | collective-permute-start | bytes 1572872 | tf_op jit(solution)/shard_map/while/body/eval_jaxpr/ppermute | solution.py:20
  1683.0 66.1 %collective-permute-start.2 = (s32[128]{0:T(128)S(1)}, s32[128]{0:T(128)S(1)}, u32[]{:S(2)}, u32[]{:S(2)}) collective-permute-start(s32[128]{0:T(128)S(1)} %copy.236), channel_id=1, source_target_pairs={{1,0},{2,1},{3,2},{4,3},{5,4},{6,5},{7,6},{0,7},{9,8},{10,9},{11,1... | collective-permute-start | bytes 1544 | tf_op jit(solution)/shard_map/while/body/eval_jaxpr/ppermute | solution.py:20
  1756.2 21.7 collective-permute-start.3
  1763.5 31.2 %collective-permute-start.4 = (bf16[128,2048]{0,1:T(8,128)(2,1)}, bf16[128,2048]{0,1:T(8,128)(2,1)}, u32[]{:S(2)}, u32[]{:S(2)}) collective-permute-start(bf16[128,2048]{0,1:T(8,128)(2,1)} %fusion.193), channel_id=1, source_target_pairs={{1,0},{2,1},{3,2},{4,3},{5,4},{6,5},{7,6},{0,7},{9,8},{10,9},{11,1... | collective-permute-start | bytes 1572872 | tf_op jit(solution)/shard_map/while/body/eval_jaxpr/ppermute | solution.py:20
  1763.6 64.8 %collective-permute-start.1 = (bf16[128,2048]{1,0:T(8,128)(2,1)}, bf16[128,2048]{1,0:T(8,128)(2,1)S(1)}, u32[]{:S(2)}, u32[]{:S(2)}) collective-permute-start(bf16[128,2048]{1,0:T(8,128)(2,1)} %copy-done.9), channel_id=1, source_target_pairs={{1,0},{2,1},{3,2},{4,3},{5,4},{6,5},{7,6},{0,7},{9,8},{10,9},{11,1... | collective-permute-start | bytes 1572872 | tf_op jit(solution)/shard_map/while/body/eval_jaxpr/ppermute | solution.py:20
  1763.6 64.8 %collective-permute-start = (bf16[128,2048]{1,0:T(8,128)(2,1)}, bf16[128,2048]{1,0:T(8,128)(2,1)S(1)}, u32[]{:S(2)}, u32[]{:S(2)}) collective-permute-start(bf16[128,2048]{1,0:T(8,128)(2,1)} %copy-done.10), channel_id=1, source_target_pairs={{1,0},{2,1},{3,2},{4,3},{5,4},{6,5},{7,6},{0,7},{9,8},{10,9},{11,1... | collective-permute-start | bytes 1572872 | tf_op jit(solution)/shard_map/while/body/eval_jaxpr/ppermute | solution.py:20
  1763.7 64.8 %collective-permute-start.2 = (s32[128]{0:T(128)S(1)}, s32[128]{0:T(128)S(1)}, u32[]{:S(2)}, u32[]{:S(2)}) collective-permute-start(s32[128]{0:T(128)S(1)} %copy.236), channel_id=1, source_target_pairs={{1,0},{2,1},{3,2},{4,3},{5,4},{6,5},{7,6},{0,7},{9,8},{10,9},{11,1... | collective-permute-start | bytes 1544 | tf_op jit(solution)/shard_map/while/body/eval_jaxpr/ppermute | solution.py:20
  1835.5 21.6 collective-permute-start.3
  1842.8 31.2 %collective-permute-start.4 = (bf16[128,2048]{0,1:T(8,128)(2,1)}, bf16[128,2048]{0,1:T(8,128)(2,1)}, u32[]{:S(2)}, u32[]{:S(2)}) collective-permute-start(bf16[128,2048]{0,1:T(8,128)(2,1)} %fusion.193), channel_id=1, source_target_pairs={{1,0},{2,1},{3,2},{4,3},{5,4},{6,5},{7,6},{0,7},{9,8},{10,9},{11,1... | collective-permute-start | bytes 1572872 | tf_op jit(solution)/shard_map/while/body/eval_jaxpr/ppermute | solution.py:20
  1842.9 64.8 %collective-permute-start.1 = (bf16[128,2048]{1,0:T(8,128)(2,1)}, bf16[128,2048]{1,0:T(8,128)(2,1)S(1)}, u32[]{:S(2)}, u32[]{:S(2)}) collective-permute-start(bf16[128,2048]{1,0:T(8,128)(2,1)} %copy-done.9), channel_id=1, source_target_pairs={{1,0},{2,1},{3,2},{4,3},{5,4},{6,5},{7,6},{0,7},{9,8},{10,9},{11,1... | collective-permute-start | bytes 1572872 | tf_op jit(solution)/shard_map/while/body/eval_jaxpr/ppermute | solution.py:20
  1842.9 64.7 %collective-permute-start = (bf16[128,2048]{1,0:T(8,128)(2,1)}, bf16[128,2048]{1,0:T(8,128)(2,1)S(1)}, u32[]{:S(2)}, u32[]{:S(2)}) collective-permute-start(bf16[128,2048]{1,0:T(8,128)(2,1)} %copy-done.10), channel_id=1, source_target_pairs={{1,0},{2,1},{3,2},{4,3},{5,4},{6,5},{7,6},{0,7},{9,8},{10,9},{11,1... | collective-permute-start | bytes 1572872 | tf_op jit(solution)/shard_map/while/body/eval_jaxpr/ppermute | solution.py:20
  1842.9 64.7 %collective-permute-start.2 = (s32[128]{0:T(128)S(1)}, s32[128]{0:T(128)S(1)}, u32[]{:S(2)}, u32[]{:S(2)}) collective-permute-start(s32[128]{0:T(128)S(1)} %copy.236), channel_id=1, source_target_pairs={{1,0},{2,1},{3,2},{4,3},{5,4},{6,5},{7,6},{0,7},{9,8},{10,9},{11,1... | collective-permute-start | bytes 1544 | tf_op jit(solution)/shard_map/while/body/eval_jaxpr/ppermute | solution.py:20
  1914.7 10.7 collective-permute-start.3
  1922.0 9.0 collective-permute-start.4
  1922.1 20.2 collective-permute-start.1
  1922.1 20.2 collective-permute-start
  1922.1 20.1 collective-permute-start.2
  1949.3 10.7 collective-permute-start.3
  1956.6 9.0 collective-permute-start.4
  1956.6 20.2 collective-permute-start.1
  1956.7 20.2 collective-permute-start
  1956.7 20.1 collective-permute-start.2
  1983.9 10.7 collective-permute-start.3
  1991.1 9.0 collective-permute-start.4
  1991.2 20.2 collective-permute-start.1
  1991.3 20.2 collective-permute-start
  1991.3 20.1 collective-permute-start.2
  2018.5 10.7 collective-permute-start.3
  2025.7 9.0 collective-permute-start.4
  2025.8 20.2 collective-permute-start.1
  2025.9 20.2 collective-permute-start
  2025.9 20.1 collective-permute-start.2
  2053.1 10.7 collective-permute-start.3
  2060.3 9.0 collective-permute-start.4
  2060.4 20.2 collective-permute-start.1
  2060.4 20.2 collective-permute-start
  2060.5 20.1 collective-permute-start.2
  2090.2 375.6 %reduce-scatter.10.cloned.1.call-start = ((), (), s32[]{:S(2)}) async-start(), calls=%async_computation.16 | async-start | bytes 17301504 | tf_op jit(solution)/shard_map/reduce_scatter | solution.py:381
  2109.6 543.6 %reduce-scatter.8.cloned.1.call-start = ((), (), s32[]{:S(2)}) async-start(), calls=%async_computation.15 | async-start | bytes 17301504 | tf_op jit(solution)/shard_map/reduce_scatter | solution.py:380
  2161.4 491.8 %copy-start.1 = (bf16[1,512,2048]{2,1,0:T(8,128)(2,1)S(1)}, bf16[1,512,2048]{2,1,0:T(8,128)(2,1)}, u32[]{:S(2)}) copy-start(bf16[1,512,2048]{2,1,0:T(8,128)(2,1)} %param.32) | copy-start | bytes 6291460
  (129 other events, 2207.3 us)
Sparse Core Ops, SparseCore 0:
  11.0 80.5 all-gather.14
  94.6 75.8 all-gather.10
  173.5 75.9 all-gather.8
  251.0 46.3 all-gather.16
  299.4 46.7 all-gather.12
  349.0 75.5 all-gather.18
  1370.9 167.3 reduce-scatter.15
  1664.8 251.6 reduce-scatter.13
  2090.2 188.3 reduce-scatter.11
  2281.4 184.3 reduce-scatter.9
  2468.8 184.3 reduce-scatter.7
where the time goes:
time: 2670 us; the launch traced here: 2660 us
  waiting for transfers between devices  1690 us (63%)
  blocking collectives  412 us (15%)
  matrix products  250 us (9%)
  other arithmetic  144 us (5%)
  local copies, waits for them, and re-layouts  112 us (4%)
  starting transfers between devices  39.3 us (1%)
    all_to_all x1, blocking collectives, body(): lax.all_to_all(dispatched, ('row', 'blk'), split_axis=0, concat_axis=0, t...  278 us
    all_to_all x1, waiting for transfers between devices, body(): lax.all_to_all(grad_rows.reshape(expert_rows.shape), ('row', 'blk'), spli...  252 us
    all_to_all x1, waiting for transfers between devices, body(): lax.all_to_all(grad_send, ('row', 'blk'), split_axis=0, concat_axis=0, ti...  251 us
    all_to_all x1, waiting for transfers between devices, body(): lax.all_to_all(part_out.reshape(sources, slot_count, model_width), ('row'...  245 us
    ppermute x40, waiting for transfers between devices, passed_along(): return lax.ppermute(block, axis, route)  241 us
    reduce_scatter x1, waiting for transfers between devices, body(): lax.psum_scatter(grad_query_w, ('row', 'blk'), scatter_dimension=0, tiled...  187 us
    reduce_scatter x1, waiting for transfers between devices, body(): lax.psum_scatter(grad_key_w, ('row', 'blk'), scatter_dimension=0, tiled=T...  187 us
    unnamed x2, blocking collectives  84.1 us
  transfers between devices with their start and end apart: 54, of which 35 were waited for; matrix products, arithmetic and copies ran while one was open for 16% of the time, Pallas kernels for 0%

commit v1 on v0

v1 whole, which is shorter than its diff:
```python
import math

import jax
import jax.numpy as jnp
from jax import lax
from jax.sharding import PartitionSpec as P

HEADS = 16
HEAD_DIM = 128
TOP_K = 8

epsilon = 1e-05
masked_score = -1e30
BOTH = ("row", "blk")
bf16 = jnp.bfloat16
f32 = jnp.float32


def mm(a, b):
    return jnp.dot(a, b, preferred_element_type=f32)


def mm_tn(a, b):
    return lax.dot_general(a, b, (((0,), (0,)), ((), ())), preferred_element_type=f32)


def mm_nt(a, b):
    return lax.dot_general(a, b, (((1,), (1,)), ((), ())), preferred_element_type=f32)


def rope_tables(count):
    half = HEAD_DIM // 2
    frequency = jnp.exp(
        -math.log(10000.0) * 2.0 * jnp.arange(half, dtype=f32) / HEAD_DIM
    )
    angles = jnp.arange(count, dtype=f32)[:, None] * frequency[None, :]
    return jnp.cos(angles)[:, None, :], jnp.sin(angles)[:, None, :]


def rope(values, cosine, sine):
    half = HEAD_DIM // 2
    a, b = values[..., :half], values[..., half:]
    return jnp.concatenate([a * cosine - b * sine, b * cosine + a * sine], axis=-1)


def norm_back(v, r, g, c, mean_vgc):
    return r * g * c - v * (r * r * r) * mean_vgc


def body(
    hidden_in,
    segment_ids,
    expert_ids,
    attention_gain,
    query_gain,
    key_gain,
    expert_gain,
    query_weight,
    key_weight,
    value_weight,
    output_weight,
    router_weight,
    gate_weight,
    up_weight,
    down_weight,
    grad_out,
):
    tokens = hidden_in.shape[1]
    width = hidden_in.shape[2]
    experts = router_weight.shape[1]
    rows, blocks = lax.axis_size("row"), lax.axis_size("blk")
    devices = rows * blocks
    seq = tokens * blocks
    head_cols = width // blocks
    heads_here = HEADS // blocks
    blk = lax.axis_index("blk")
    me = lax.axis_index("row") * blocks + blk
    scale = HEAD_DIM**-0.5

    small = jnp.concatenate(
        [
            router_weight,
            attention_gain[:, None],
            query_gain[:, None],
            key_gain[:, None],
            expert_gain[:, None],
        ],
        axis=1,
    )
    small = lax.all_gather(small, BOTH, axis=0, tiled=True)
    router = small[:, :experts]
    gains = small[:, experts:].astype(f32)
    gain_attn, gain_expert = gains[:, 0], gains[:, 3]
    own_q_gain = lax.dynamic_slice_in_dim(gains[:, 1], blk * head_cols, head_cols)
    own_k_gain = lax.dynamic_slice_in_dim(gains[:, 2], blk * head_cols, head_cols)

    x = hidden_in[0].astype(f32)
    r_attn = lax.rsqrt(jnp.mean(x * x, axis=-1, keepdims=True) + epsilon)
    normed = (x * r_attn * gain_attn).astype(bf16)
    normed_row = lax.all_gather(normed, "blk", axis=0, tiled=True)
    segments = lax.all_gather(segment_ids[0], "blk", axis=0, tiled=True)

    stacked = jnp.stack([query_weight, key_weight, value_weight], axis=0)
    wrows = stacked.shape[1]
    stacked = stacked.reshape(3, wrows, blocks, head_cols).transpose(2, 1, 0, 3)
    stacked = stacked.reshape(blocks, wrows, 3 * head_cols)
    cols = lax.all_to_all(stacked, "blk", split_axis=0, concat_axis=0, tiled=True)
    cols = cols.reshape(blocks * wrows, 3 * head_cols)
    qkv_cols = lax.all_gather(cols, "row", axis=0, tiled=True)
    full_output = lax.all_gather(output_weight, BOTH, axis=0, tiled=True)

    qkv = mm(normed_row, qkv_cols)
    query_pre = qkv[:, :head_cols]
    key_pre = qkv[:, head_cols : 2 * head_cols]
    value = qkv[:, 2 * head_cols :].astype(bf16)
    squares = jnp.stack(
        [jnp.sum(query_pre * query_pre, axis=-1), jnp.sum(key_pre * key_pre, axis=-1)]
    )
    squares = lax.psum(squares, "blk") / width
    r_q = lax.rsqrt(squares[0] + epsilon)[:, None]
    r_k = lax.rsqrt(squares[1] + epsilon)[:, None]
    cosine, sine = rope_tables(seq)

    def heads(v):
        return v.reshape(seq, heads_here, HEAD_DIM)

    query = rope(heads(query_pre * r_q * own_q_gain), cosine, sine).astype(bf16)
    key = rope(heads(key_pre * r_k * own_k_gain), cosine, sine).astype(bf16)
    value = heads(value)
    places = jnp.arange(seq, dtype=jnp.int32)
    allowed = (places[None, :] <= places[:, None]) & (
        segments[None, :] == segments[:, None]
    )
    scores = jnp.einsum("qhd,khd->hqk", query, key, preferred_element_type=f32) * scale
    scores = jnp.where(allowed[None], scores, masked_score)
    top = jnp.max(scores, axis=-1, keepdims=True)
    weights = jnp.where(allowed[None], jnp.exp(scores - top), 0.0)
    total = jnp.sum(weights, axis=-1, keepdims=True)
    probs = weights / total
    probs_low = probs.astype(bf16)
    attended = jnp.einsum("hqk,khd->qhd", probs_low, value, preferred_element_type=f32)
    attended_low_cols = attended.astype(bf16).reshape(blocks, tokens, head_cols)
    attended_low = lax.all_to_all(
        attended_low_cols, "blk", split_axis=0, concat_axis=0, tiled=True
    )
    attended_low = attended_low.transpose(1, 0, 2).reshape(tokens, width)

    residual_mid = x + mm(attended_low, full_output)
    r_exp = lax.rsqrt(
        jnp.mean(residual_mid * residual_mid, axis=-1, keepdims=True) + epsilon
    )
    expert_in = (residual_mid * r_exp * gain_expert).astype(bf16)
    logits = mm(expert_in, router)
    routes = expert_ids[0]
    routed = jnp.any(
        routes[:, :, None] == jnp.arange(experts, dtype=jnp.int32)[None, None, :],
        axis=1,
    )
    top_logit = jnp.max(
        jnp.where(routed, logits, masked_score), axis=-1, keepdims=True
    )
    gates = jnp.where(routed, jnp.exp(logits - top_logit), 0.0)
    gates = gates / jnp.sum(gates, axis=-1, keepdims=True)

    gate_local, up_local, down_local = gate_weight[0], up_weight[0], down_weight[0]
    parts = devices * tokens // 2048
    step = tokens // parts
    all_gates = lax.all_gather(gates, BOTH, axis=0, tiled=False)
    own_gate = jnp.sum(
        jnp.where(
            jnp.arange(experts, dtype=jnp.int32)[None, None, :] == me // 2,
            all_gates,
            0.0,
        ),
        axis=-1,
    )

    def expert_part(sums, items):
        own_rows, own_upstream, gate_col = items
        got = lax.all_gather(own_rows, BOTH, axis=0, tiled=True)
        up_stream = lax.all_gather(own_upstream, BOTH, axis=0, tiled=True)
        gate_col = gate_col.reshape(devices * step, 1)
        gate_pre = mm(got, gate_local)
        up_pre = mm(got, up_local)
        sig = jax.nn.sigmoid(gate_pre)
        silu = gate_pre * sig
        hidden = (silu * up_pre).astype(bf16)
        part_f = mm(hidden, down_local).astype(bf16).astype(f32)
        up_f = up_stream.astype(f32)
        dots = jnp.sum(part_f * up_f, axis=-1).reshape(devices, step)
        mixed = (gate_col * part_f).astype(bf16)
        out = lax.psum_scatter(mixed, BOTH, scatter_dimension=0, tiled=True)
        grad_part = (gate_col * up_f).astype(bf16)
        grad_hidden = mm_nt(grad_part, down_local)
        grad_gate_pre = (
            grad_hidden * up_pre * sig * (1.0 + gate_pre * (1.0 - sig))
        ).astype(bf16)
        grad_up_pre = (grad_hidden * silu).astype(bf16)
        grad_rows = (
            mm_nt(grad_gate_pre, gate_local) + mm_nt(grad_up_pre, up_local)
        ).astype(bf16)
        back = lax.psum_scatter(grad_rows, BOTH, scatter_dimension=0, tiled=True)
        sums = (
            sums[0] + mm_tn(got, grad_gate_pre),
            sums[1] + mm_tn(got, grad_up_pre),
            sums[2] + mm_tn(hidden, grad_part),
        )
        return sums, (out, back, dots)

    sums = (
        jnp.zeros(gate_local.shape, f32),
        jnp.zeros(up_local.shape, f32),
        jnp.zeros(down_local.shape, f32),
    )
    items = (
        expert_in.reshape(parts, step, width),
        grad_out[0].reshape(parts, step, width),
        own_gate.reshape(devices, parts, step).transpose(1, 0, 2),
    )
    if parts > 2:
        sums, (outs, backs, dots) = lax.scan(expert_part, sums, items)
    else:
        made = []
        for part in range(parts):
            sums, result = expert_part(sums, tuple(item[part] for item in items))
            made.append(result)
        outs, backs, dots = (jnp.stack(some) for some in zip(*made))
    grad_gate_local, grad_up_local, grad_down_local = sums
    dots = dots.transpose(1, 0, 2).reshape(devices, tokens)
    outs = outs.reshape(tokens, width)
    backs = backs.reshape(tokens, width)
    dots = lax.all_to_all(dots, BOTH, split_axis=0, concat_axis=0, tiled=True)
    grad_gates = jnp.sum(dots.reshape(experts, 2, tokens), axis=1).T
    moe_out = outs.astype(f32)
    layer_out = (residual_mid + moe_out).astype(bf16)
    upstream = grad_out[0].astype(f32)
    grad_picked = gates * (
        grad_gates - jnp.sum(gates * grad_gates, axis=-1, keepdims=True)
    )
    grad_logits = jnp.where(routed, grad_picked, 0.0).astype(bf16)
    grad_expert_in = backs.astype(f32) + mm_nt(
        grad_logits, router
    )
    grad_router = mm_tn(expert_in, grad_logits)
    grad_gain_expert = jnp.sum(grad_expert_in * residual_mid * r_exp, axis=0)
    grad_mid = upstream + norm_back(
        residual_mid,
        r_exp,
        gain_expert,
        grad_expert_in,
        jnp.mean(residual_mid * gain_expert * grad_expert_in, axis=-1, keepdims=True),
    )
    grad_proj = grad_mid.astype(bf16)
    grad_output_w = mm_tn(attended_low, grad_proj).astype(bf16)
    grad_output_w = lax.psum_scatter(
        grad_output_w, BOTH, scatter_dimension=0, tiled=True
    ).astype(f32)
    grad_attended = mm_nt(grad_proj, full_output).astype(bf16)
    grad_attended = grad_attended.reshape(tokens, blocks, head_cols).transpose(1, 0, 2)
    grad_attended = lax.all_to_all(
        grad_attended, "blk", split_axis=0, concat_axis=0, tiled=True
    )
    grad_attended = grad_attended.reshape(seq, heads_here, HEAD_DIM)
    row_delta = jnp.sum(grad_attended.astype(f32) * attended, axis=-1).T
    grad_probs = jnp.einsum(
        "qhd,khd->hqk", grad_attended, value, preferred_element_type=f32
    )
    grad_scores = (probs * (grad_probs - row_delta[:, :, None])).astype(bf16)
    grad_value = jnp.einsum(
        "hqk,qhd->khd", probs_low, grad_attended, preferred_element_type=f32
    ).astype(bf16)
    grad_query = (
        jnp.einsum("hqk,khd->qhd", grad_scores, key, preferred_element_type=f32) * scale
    )
    grad_key = (
        jnp.einsum("hqk,qhd->khd", grad_scores, query, preferred_element_type=f32)
        * scale
    )
    grad_query = rope(grad_query, cosine, -sine).reshape(seq, head_cols)
    grad_key = rope(grad_key, cosine, -sine).reshape(seq, head_cols)
    means = jnp.stack(
        [
            jnp.sum(query_pre * own_q_gain * grad_query, axis=-1),
            jnp.sum(key_pre * own_k_gain * grad_key, axis=-1),
        ]
    )
    means = lax.psum(means, "blk") / width
    grad_q_gain = jnp.sum(grad_query * query_pre * r_q, axis=0)
    grad_k_gain = jnp.sum(grad_key * key_pre * r_k, axis=0)
    grad_query_pre = norm_back(query_pre, r_q, own_q_gain, grad_query, means[0][:, None])
    grad_key_pre = norm_back(key_pre, r_k, own_k_gain, grad_key, means[1][:, None])
    grad_qkv = jnp.concatenate(
        [
            grad_query_pre.astype(bf16),
            grad_key_pre.astype(bf16),
            grad_value.reshape(seq, head_cols),
        ],
        axis=1,
    )
    grad_w = mm_tn(normed_row, grad_qkv).astype(bf16)
    grad_w = lax.psum_scatter(grad_w, "row", scatter_dimension=0, tiled=True)
    grad_w = grad_w.reshape(blocks, wrows, 3 * head_cols)
    grad_w = lax.all_to_all(grad_w, "blk", split_axis=0, concat_axis=0, tiled=True)
    grad_w = grad_w.reshape(blocks, wrows, 3, head_cols).transpose(2, 1, 0, 3)
    grad_w = grad_w.reshape(3, wrows, width).astype(f32)
    grad_normed = mm_nt(grad_qkv, qkv_cols).astype(bf16)
    grad_normed = lax.psum_scatter(
        grad_normed, "blk", scatter_dimension=0, tiled=True
    ).astype(f32)
    grad_gain_attn = jnp.sum(grad_normed * x * r_attn, axis=0)
    input_grad = grad_mid + norm_back(
        x,
        r_attn,
        gain_attn,
        grad_normed,
        jnp.mean(x * gain_attn * grad_normed, axis=-1, keepdims=True),
    )

    def placed(vector):
        return lax.dynamic_update_slice_in_dim(
            jnp.zeros((width,), f32), vector, blk * head_cols, axis=0
        )

    small_grads = jnp.concatenate(
        [
            grad_router,
            grad_gain_attn[:, None],
            placed(grad_q_gain)[:, None],
            placed(grad_k_gain)[:, None],
            grad_gain_expert[:, None],
        ],
        axis=1,
    )
    small_grads = lax.psum_scatter(small_grads, BOTH, scatter_dimension=0, tiled=True)
    return (
        layer_out[None],
        input_grad[None],
        small_grads[:, experts],
        small_grads[:, experts + 1],
        small_grads[:, experts + 2],
        small_grads[:, experts + 3],
        grad_w[0],
        grad_w[1],
        grad_w[2],
        grad_output_w,
        small_grads[:, :experts],
        grad_gate_local[None],
        grad_up_local[None],
        grad_down_local[None],
    )


def solution(mesh):
    tokens3 = P("row", "blk", None)
    vector, matrix, cube = P(BOTH), P(BOTH, None), P(BOTH, None, None)
    return jax.shard_map(
        body,
        mesh=mesh,
        in_specs=(
            tokens3,
            P("row", "blk"),
            tokens3,
            vector,
            vector,
            vector,
            vector,
            matrix,
            matrix,
            matrix,
            matrix,
            matrix,
            cube,
            cube,
            cube,
            tokens3,
        ),
        out_specs=(
            tokens3,
            tokens3,
            vector,
            vector,
            vector,
            vector,
            matrix,
            matrix,
            matrix,
            matrix,
            matrix,
            cube,
            cube,
            cube,
        ),
        check_vma=False,
    )
```

time: 2670 us -> 1730 us (0.65)
  waiting for transfers between devices: 1690 us -> 1140 us
  blocking collectives: 412 us -> 171 us
  other arithmetic: 144 us -> 60.6 us
    all_to_all x3, waiting for transfers between devices: 748 us -> 34.4 us  [the longest x1 15 us: body(): lax.all_to_all(grad_attended, 'blk', split_axis=0, concat_axis=0, tiled=T...]
    reduce_scatter x4 -> x7, waiting for transfers between devices: 437 us -> 712 us  [the longest x2 301 us: expert_part(): out = lax.psum_scatter(mixed, BOTH, scatter_dimension=0, tiled=True)]
    ppermute x40 -> x0, waiting for transfers between devices: 241 us -> none  [passed_along(): return lax.ppermute(block, axis, route)]
    all_to_all x1 -> x2, blocking collectives: 278 us -> 54.1 us  [the longest x1 27.2 us: body(): lax.all_to_all(stacked, 'blk', split_axis=0, concat_axis=0, tiled=True)]
    unnamed x12 -> x16, waiting for transfers between devices: 2.7 us -> 103 us
    unnamed x2 -> x0, blocking collectives: 84.1 us -> none
    gather x4 -> x0, local copies, waits for them, and re-layouts: 49.8 us -> none  [the longest x1 15.4 us: body(): grad_slots = jnp.where(slot_live[:, None], grad_pairs[pair_of_slot], 0)]
    convert_element_type x43 -> x9, other arithmetic: 73.9 us -> 29.6 us  [the longest x2 19.6 us: expert_part(): mixed = (gate_col * part_f).astype(bf16)]
  transfers between devices with their start and end apart: 54 -> 18, of which waited for: 35 -> 17; matrix products, arithmetic and copies ran while one was open for 16% -> 15% of each run, Pallas kernels for 0% -> 0%
where the time goes in v1:
time: 1730 us; the launch traced here: 1720 us
  waiting for transfers between devices  1140 us (66%)
  matrix products  224 us (13%)
  blocking collectives  171 us (10%)
  local copies, waits for them, and re-layouts  95.6 us (6%)
  other arithmetic  60.6 us (4%)
    reduce_scatter x2, waiting for transfers between devices, expert_part(): out = lax.psum_scatter(mixed, BOTH, scatter_dimension=0, tiled=True)  301 us
    reduce_scatter x2, waiting for transfers between devices, expert_part(): back = lax.psum_scatter(grad_rows, BOTH, scatter_dimension=0, tiled=True)  225 us
    reduce_scatter x1, waiting for transfers between devices, body(): lax.psum_scatter(grad_output_w, BOTH, scatter_dimension=0, tiled=True)  146 us
    all_gather x2, waiting for transfers between devices, expert_part(): up_stream = lax.all_gather(own_upstream, BOTH, axis=0, tiled=True)  137 us
    all_gather x2, waiting for transfers between devices, expert_part(): got = lax.all_gather(own_rows, BOTH, axis=0, tiled=True)  122 us
    unnamed x16, waiting for transfers between devices  103 us
    dot_general x9, matrix products, mm_nt(): lax.dot_general(a, b, (((1,), (1,)), ((), ())), preferred_element_type=f32)  80.7 us
    dot_general x9, matrix products, mm(): return jnp.dot(a, b, preferred_element_type=f32)  59.9 us
  transfers between devices with their start and end apart: 18, of which 17 were waited for; matrix products, arithmetic and copies ran while one was open for 15% of the time, Pallas kernels for 0%

profile of v1, /device:TPU:0, one launch (start us, length us, event | category | flops | bytes accessed | tf_op | source)
XLA Modules:
  0.0 1724.1 jit_solution(17276174775528114960)
XLA Ops:
  11.7 2.8 maximum_bitcast_fusion
  14.5 2.6 reshape.307
  17.1 27.2 %all_to_all.29 = bf16[8,64,768]{2,1,0:T(8,128)(2,1)} all-to-all(bf16[8,64,768]{2,1,0:T(8,128)(2,1)S(1)} %reshape.307), channel_id=1, replica_groups=mesh['row'=4,'blk'=8] {'blk'}, dimensions={0} | all-to-all | bytes 1572864 | tf_op jit(solution)/shard_map/all_to_all | solution.py:107
  44.5 40.8 %all-gather.4 = bf16[32,64,20]{1,2,0:T(8,128)(2,1)S(1)} all-gather(bf16[1,64,20]{1,2,0:T(8,128)(2,1)S(1)} %bitcast.311), channel_id=1, replica_groups=mesh['row'=4,'blk'=8] {'row','blk'}, dimensions={0}, use_global_device_ids=true | all-gather | bytes 84480 | tf_op jit(solution)/shard_map/all_gather | solution.py:90
  89.6 8.7 all-gather
  98.3 2.8 fusion.74
  102.7 34.5 %all-gather.13.cloned.1.call-done = bf16[1024,2048]{1,0:T(8,128)(2,1)} async-done(((bf16[128,2048]{1,0:T(8,128)(2,1)}), bf16[1024,2048]{1,0:T(8,128)(2,1)}) %all-gather.13.cloned.1.call-update) | async-done | bytes 4194320 | tf_op jit(solution)/shard_map/all_gather | solution.py:100
  137.2 6.2 fusion.102
  145.5 15.1 psum.14
  160.7 2.7 multiply_multiply_fusion.1
  176.2 4.0 subtract_convert_fusion.1
  180.2 10.0 fusion.100
  190.2 4.8 fusion.22
  197.4 26.9 %all_to_all.30 = bf16[8,128,256]{1,2,0:T(8,128)(2,1)S(1)} all-to-all(bf16[8,128,256]{1,2,0:T(8,128)(2,1)S(1)} %copy.182), channel_id=1, replica_groups=mesh['row'=4,'blk'=8] {'blk'}, dimensions={0} | all-to-all | bytes 1048576 | tf_op jit(solution)/shard_map/all_to_all | solution.py:143
  225.7 4.8 multiply_reduce_fusion.3
  233.3 70.5 %all-gather.23.cloned.1.call-done = bf16[1,2048,2048]{2,1,0:T(8,128)(2,1)} async-done(((bf16[1,64,2048]{2,1,0:T(8,128)(2,1)}), bf16[1,2048,2048]{2,1,0:T(8,128)(2,1)}) %all-gather.23.cloned.1.call-update) | async-done | bytes 8388624 | tf_op jit(solution)/shard_map/all_gather | solution.py:181
  303.8 12.2 copy.185
  316.1 66.6 %all-gather.25.cloned.1.call-done = bf16[1,2048,2048]{2,1,0:T(8,128)(2,1)} async-done(((bf16[1,64,2048]{2,1,0:T(8,128)(2,1)}), bf16[1,2048,2048]{2,1,0:T(8,128)(2,1)}) %all-gather.25.cloned.1.call-update) | async-done | bytes 8388624 | tf_op jit(solution)/shard_map/all_gather | solution.py:181
  382.7 12.3 copy.186
  395.2 66.9 %all-gather.21.cloned.1.call-done = bf16[2048,2048]{1,0:T(8,128)(2,1)} async-done(((bf16[64,2048]{1,0:T(8,128)(2,1)}), bf16[2048,2048]{1,0:T(8,128)(2,1)}) %all-gather.21.cloned.1.call-update) | async-done | bytes 8388624 | tf_op jit(solution)/shard_map/all_gather | solution.py:180
  462.1 7.7 fusion.39
  469.8 6.4 multiply_convert_fusion.5
  476.3 10.3 fusion.6
  486.6 55.1 %all-gather.19.cloned.1.call-done = bf16[2048,2048]{1,0:T(8,128)(2,1)} async-done(((bf16[64,2048]{1,0:T(8,128)(2,1)}), bf16[2048,2048]{1,0:T(8,128)(2,1)}) %all-gather.19.cloned.1.call-update) | async-done | bytes 8388624 | tf_op jit(solution)/shard_map/all_gather | solution.py:180
  541.7 7.7 fusion.41
  549.4 6.4 multiply_convert_fusion.6
  555.8 10.2 fusion.4
  566.9 3.2 all-to-all-start.2
  570.2 7.0 all-to-all-done.2
  577.3 38.0 %all-gather.1 = f32[4096,16]{0,1:T(8,128)S(1)} all-gather(f32[128,16]{0,1:T(8,128)S(1)} %get-tuple-element.29), channel_id=3, replica_groups=mesh['row'=4,'blk'=8] {'row','blk'}, dimensions={0}, use_global_device_ids=true | all-gather | bytes 270336 | tf_op jit(solution)/shard_map/all_gather | solution.py:168
  615.7 12.9 multiply_convert_fusion.1
  628.6 8.2 fusion.35
  636.8 14.9 add_convert_fusion
  651.9 13.5 multiply_convert_fusion.3
  665.4 8.3 fusion.37
  673.8 11.0 add_convert_fusion.1
  684.8 9.8 fusion.1
  694.6 12.4 copy.217
  707.1 9.8 fusion.2
  716.9 12.4 copy.219
  729.3 71.3 %reduce-scatter.17.cloned.1.call-done = bf16[64,2048]{1,0:T(8,128)(2,1)} async-done(((bf16[2048,2048]{1,0:T(8,128)(2,1)}), bf16[64,2048]{1,0:T(8,128)(2,1)}) %reduce-scatter.17.cloned.1.call-update) | async-done | bytes 262160 | tf_op jit(solution)/shard_map/reduce_scatter | solution.py:202
  800.6 153.2 %reduce-scatter.15.cloned.1.call-done = bf16[64,2048]{1,0:T(8,128)(2,1)} async-done(((bf16[2048,2048]{1,0:T(8,128)(2,1)}), bf16[64,2048]{1,0:T(8,128)(2,1)}) %reduce-scatter.15.cloned.1.call-update) | async-done | bytes 262160 | tf_op jit(solution)/shard_map/reduce_scatter | solution.py:202
  955.5 149.5 %reduce-scatter.25.cloned.1.call-done = bf16[64,2048]{1,0:T(8,128)(2,1)} async-done(((bf16[2048,2048]{1,0:T(8,128)(2,1)}), bf16[64,2048]{1,0:T(8,128)(2,1)}) %reduce-scatter.25.cloned.1.call-update) | async-done | bytes 262160 | tf_op jit(solution)/shard_map/reduce_scatter | solution.py:192
  1105.0 151.6 %reduce-scatter.27.cloned.1.call-done = bf16[64,2048]{1,0:T(8,128)(2,1)} async-done(((bf16[2048,2048]{1,0:T(8,128)(2,1)}), bf16[64,2048]{1,0:T(8,128)(2,1)}) %reduce-scatter.27.cloned.1.call-update) | async-done | bytes 262160 | tf_op jit(solution)/shard_map/reduce_scatter | solution.py:192
  1259.9 6.3 convolution_convert_fusion.5
  1267.2 3.6 all-to-all-start.3
  1271.1 15.0 all-to-all-done.3
  1286.7 4.6 convolution_convert_fusion.6
  1291.5 4.8 multiply_convert_fusion
  1311.0 14.8 psum.15
  1329.0 5.0 convolution_convert_fusion.3
  1335.4 7.4 convolution_convert_fusion.4
  1343.2 39.2 %reduce-scatter.19.cloned.1.call-done = bf16[128,2048]{1,0:T(8,128)(2,1)} async-done(((bf16[1024,2048]{1,0:T(8,128)(2,1)}), bf16[128,2048]{1,0:T(8,128)(2,1)}) %reduce-scatter.19.cloned.1.call-update) | async-done | bytes 524304 | tf_op jit(solution)/shard_map/reduce_scatter | solution.py:307
  1385.3 5.7 convolution_convert_fusion.2
  1391.0 10.7 fusion.7
  1401.7 7.7 fusion.104
  1409.5 4.6 fusion.103
  1414.1 6.1 add_bitcast_fusion.2
  1420.3 6.1 add_bitcast_fusion.1
  1427.5 4.8 all-to-all-start.4
  1432.3 10.3 add_bitcast_fusion
  1442.6 12.4 all-to-all-done.4
  1464.3 101.0 %reduce-scatter.29.cloned.1.call-done = f32[64,20]{1,0:T(8,128)} async-done(((f32[2048,20]{1,0:T(8,128)}), f32[64,20]{1,0:T(8,128)}) %reduce-scatter.29.cloned.1.call-update) | async-done | bytes 5136
  1570.0 145.5 %reduce-scatter.23.cloned.1.call-done = bf16[64,2048]{1,0:T(8,128)(2,1)} async-done(((bf16[2048,2048]{1,0:T(8,128)(2,1)}), bf16[64,2048]{1,0:T(8,128)(2,1)}) %reduce-scatter.23.cloned.1.call-update) | async-done | bytes 262160 | tf_op jit(solution)/shard_map/reduce_scatter | solution.py:255
  (302 shorter events, 79.9 us)
Async XLA Ops:
  7.2 469.1 %copy-start = (bf16[1,512,2048]{2,1,0:T(8,128)(2,1)S(1)}, bf16[1,512,2048]{2,1,0:T(8,128)(2,1)}, u32[]{:S(2)}) copy-start(bf16[1,512,2048]{2,1,0:T(8,128)(2,1)} %param.30) | copy-start | bytes 6291460
  7.2 95.5 %all-gather.15.cloned.1.call-start = ((), (), s32[]{:S(2)}) async-start(), calls=%async_computation.14 | async-start | bytes 3932160 | tf_op jit(solution)/shard_map/all_gather | solution.py:109
  10.2 34.2 %copy-start.52 = (bf16[64,16]{0,1:T(8,128)(2,1)S(1)}, bf16[64,16]{0,1:T(8,128)(2,1)}, u32[]{:S(2)}) copy-start(bf16[64,16]{0,1:T(8,128)(2,1)} %param.27) | copy-start | bytes 6148
  10.2 34.2 %copy-start.56 = (bf16[64]{0:T(256)(128)(2,1)S(1)}, bf16[64]{0:T(256)(128)(2,1)}, u32[]{:S(2)}) copy-start(bf16[64]{0:T(256)(128)(2,1)} %param.19) | copy-start | bytes 388
  10.2 34.2 %copy-start.57 = (bf16[64]{0:T(256)(128)(2,1)S(1)}, bf16[64]{0:T(256)(128)(2,1)}, u32[]{:S(2)}) copy-start(bf16[64]{0:T(256)(128)(2,1)} %param.20) | copy-start | bytes 388
  10.3 34.2 %copy-start.58 = (bf16[64]{0:T(256)(128)(2,1)S(1)}, bf16[64]{0:T(256)(128)(2,1)}, u32[]{:S(2)}) copy-start(bf16[64]{0:T(256)(128)(2,1)} %param.21) | copy-start | bytes 388
  10.3 34.2 %copy-start.59 = (bf16[64]{0:T(256)(128)(2,1)S(1)}, bf16[64]{0:T(256)(128)(2,1)}, u32[]{:S(2)}) copy-start(bf16[64]{0:T(256)(128)(2,1)} %param.22) | copy-start | bytes 388
  11.3 74.2 %copy-start.6 = (bf16[1,128,2048]{2,1,0:T(8,128)(2,1)S(1)}, bf16[1,128,2048]{2,1,0:T(8,128)(2,1)}, u32[]{:S(2)}) copy-start(bf16[1,128,2048]{2,1,0:T(8,128)(2,1)} %param.16) | copy-start | bytes 1572868
  14.5 75.1 %copy-start.60 = (s32[1,128]{1,0:T(1,128)S(1)}, s32[1,128]{1,0:T(1,128)}, u32[]{:S(2)}) copy-start(s32[1,128]{1,0:T(1,128)} %param.17) | copy-start | bytes 1540
  44.3 43.7 %copy-start.25 = (bf16[1,128,2048]{2,1,0:T(8,128)(2,1)S(1)}, bf16[1,128,2048]{2,1,0:T(8,128)(2,1)}, u32[]{:S(2)}) copy-start(bf16[1,128,2048]{2,1,0:T(8,128)(2,1)} %param.31) | copy-start | bytes 1572868
  44.3 92.9 %all-gather.13.cloned.1.call-start = ((), (), s32[]{:S(2)}) async-start(), calls=%async_computation.13 | async-start | bytes 4718592 | tf_op jit(solution)/shard_map/all_gather | solution.py:100
  85.5 309.4 %copy-start.26 = (bf16[2048,20]{0,1:T(8,128)(2,1)}, bf16[2048,20]{0,1:T(8,128)(2,1)S(1)}, u32[]{:S(2)}) copy-start(bf16[2048,20]{0,1:T(8,128)(2,1)S(1)} %reshape.334) | copy-start | bytes 245764
  86.2 57.2 %copy-start.48 = (f32[128]{0:T(128)}, f32[128]{0:T(128)S(1)}, u32[]{:S(2)}) copy-start(f32[128]{0:T(128)S(1)} %get-tuple-element.76) | copy-start | bytes 1540
  86.3 57.2 %copy-start.34 = (f32[2048,1]{0,1:T(1,128)}, f32[2048,1]{0,1:T(1,128)S(1)}, u32[]{:S(2)}) copy-start(f32[2048,1]{0,1:T(1,128)S(1)} %get-tuple-element.70) | copy-start | bytes 24580
  86.3 144.8 %copy-start.36 = (f32[2048,1]{0,1:T(1,128)}, f32[2048,1]{0,1:T(1,128)S(1)}, u32[]{:S(2)}) copy-start(f32[2048,1]{0,1:T(1,128)S(1)} %get-tuple-element.67) | copy-start | bytes 24580
  87.3 138.4 %all-gather.17.cloned.1.call-start = ((), (), s32[]{:S(2)}) async-start(), calls=%async_computation.15 | async-start | bytes 8650752 | tf_op jit(solution)/shard_map/all_gather | solution.py:110
  88.0 215.8 %all-gather.23.cloned.1.call-start = ((), (), s32[]{:S(2)}) async-start(), calls=%async_computation.23 | async-start | bytes 8650752 | tf_op jit(solution)/shard_map/all_gather | solution.py:181
  89.0 293.7 %all-gather.25.cloned.1.call-start = ((), (), s32[]{:S(2)}) async-start(), calls=%async_computation.24 | async-start | bytes 8650752 | tf_op jit(solution)/shard_map/all_gather | solution.py:181
  89.5 372.6 %all-gather.21.cloned.1.call-start = ((), (), s32[]{:S(2)}) async-start(), calls=%async_computation.17 | async-start | bytes 8650752 | tf_op jit(solution)/shard_map/all_gather | solution.py:180
  98.3 62.4 %copy-start.42 = (f32[256,1]{0,1:T(1,128)}, f32[256,1]{0,1:T(1,128)S(1)}, u32[]{:S(2)}) copy-start(f32[256,1]{0,1:T(1,128)S(1)} %get-tuple-element.99) | copy-start | bytes 3076
  98.3 62.4 %copy-start.44 = (f32[256,1]{0,1:T(1,128)}, f32[256,1]{0,1:T(1,128)S(1)}, u32[]{:S(2)}) copy-start(f32[256,1]{0,1:T(1,128)S(1)} %get-tuple-element.100) | copy-start | bytes 3076
  101.1 75.0 %copy-start.13 = (f32[1024,64]{1,0:T(8,128)}, f32[1024,64]{1,0:T(8,128)S(1)}, u32[]{:S(2)}) copy-start(f32[1024,64]{1,0:T(8,128)S(1)} %get-tuple-element.79) | copy-start | bytes 786436
  160.7 8.4 copy-start.38
  160.7 8.4 copy-start.40
  231.0 85.0 %copy-start.50 = (f32[128]{0:T(128)}, f32[128]{0:T(128)S(1)}, u32[]{:S(2)}) copy-start(f32[128]{0:T(128)S(1)} %get-tuple-element.81) | copy-start | bytes 1540
  231.6 163.4 %copy-start.11 = (bf16[128,2048]{1,0:T(8,128)(2,1)}, bf16[128,2048]{1,0:T(8,128)(2,1)S(1)}, u32[]{:S(2)}) copy-start(bf16[128,2048]{1,0:T(8,128)(2,1)S(1)} %multiply_convert_fusion.7) | copy-start | bytes 1572868
  232.5 309.2 %all-gather.19.cloned.1.call-start = ((), (), s32[]{:S(2)}) async-start(), calls=%async_computation.16 | async-start | bytes 8650752 | tf_op jit(solution)/shard_map/all_gather | solution.py:180
  476.2 10.3 copy-start.79
  555.8 10.2 copy-start.77
  566.9 10.3 all-to-all-start.2
  570.1 230.4 %reduce-scatter.17.cloned.1.call-start = ((), (), s32[]{:S(2)}) async-start(), calls=%async_computation.19 | async-start | bytes 8650752 | tf_op jit(solution)/shard_map/reduce_scatter | solution.py:202
  615.7 12.9 copy-start.64
  628.6 8.2 copy-start.69
  651.8 302.0 %reduce-scatter.15.cloned.1.call-start = ((), (), s32[]{:S(2)}) async-start(), calls=%async_computation.18 | async-start | bytes 8650752 | tf_op jit(solution)/shard_map/reduce_scatter | solution.py:202
  651.9 13.5 copy-start.65
  665.4 8.3 copy-start.71
  665.4 8.3 copy-start.68
  684.8 420.2 %reduce-scatter.25.cloned.1.call-start = ((), (), s32[]{:S(2)}) async-start(), calls=%async_computation.25 | async-start | bytes 8650752 | tf_op jit(solution)/shard_map/reduce_scatter | solution.py:192
  707.0 549.6 %reduce-scatter.27.cloned.1.call-start = ((), (), s32[]{:S(2)}) async-start(), calls=%async_computation.26 | async-start | bytes 8650752 | tf_op jit(solution)/shard_map/reduce_scatter | solution.py:192
  729.2 225.7 %copy-start.5 = (f32[128,2048]{1,0:T(8,128)S(1)}, f32[128,2048]{1,0:T(8,128)}, u32[]{:S(2)}) copy-start(f32[128,2048]{1,0:T(8,128)} %copy-done.4) | copy-start | bytes 3145732
  729.2 225.7 %copy-start.27 = (bf16[2048,20]{0,1:T(8,128)(2,1)S(1)}, bf16[2048,20]{0,1:T(8,128)(2,1)}, u32[]{:S(2)}) copy-start(bf16[2048,20]{0,1:T(8,128)(2,1)} %copy-done.26) | copy-start | bytes 245764
  729.2 225.7 %copy-start.37 = (f32[2048,1]{0,1:T(1,128)S(1)}, f32[2048,1]{0,1:T(1,128)}, u32[]{:S(2)}) copy-start(f32[2048,1]{0,1:T(1,128)} %copy-done.36) | copy-start | bytes 24580
  729.2 225.7 %copy-start.51 = (f32[128]{0:T(128)S(1)}, f32[128]{0:T(128)}, u32[]{:S(2)}) copy-start(f32[128]{0:T(128)} %copy-done.50) | copy-start | bytes 1540
  729.3 528.4 %copy-start.55 = (f32[128]{0:T(128)S(1)}, f32[128]{0:T(128)}, u32[]{:S(2)}) copy-start(f32[128]{0:T(128)} %get-tuple-element.80) | copy-start | bytes 1540
  1259.9 11.1 copy-start.39
  1259.9 11.1 copy-start.41
  1267.2 24.1 %copy-start.16 = (f32[1024,2,128]{0,2,1:T(8,128)S(1)}, f32[1024,2,128]{0,2,1:T(8,128)}, u32[]{:S(2)}) copy-start(f32[1024,2,128]{0,2,1:T(8,128)} %get-tuple-element.85) | copy-start | bytes 3145732
  1267.2 18.9 %all-to-all-start.3 = ((bf16[8,128,256]{1,2,0:T(8,128)(2,1)}), bf16[8,128,256]{1,2,0:T(8,128)(2,1)S(1)}, u32[]{:S(2)}, u32[]{:S(2)}) async-start(bf16[8,128,256]{1,2,0:T(8,128)(2,1)} %bitcast.46), calls=%async_computation.5 | async-start | bytes 1048576 | tf_op jit(solution)/shard_map/all_to_all | solution.py:260
  1270.8 111.6 %reduce-scatter.19.cloned.1.call-start = ((), (), s32[]{:S(2)}) async-start(), calls=%async_computation.20 | async-start | bytes 4718592 | tf_op jit(solution)/shard_map/reduce_scatter | solution.py:307
  1334.1 8.8 copy-start.12
  1334.1 48.3 %copy-start.35 = (f32[2048,1]{0,1:T(1,128)S(1)}, f32[2048,1]{0,1:T(1,128)}, u32[]{:S(2)}) copy-start(f32[2048,1]{0,1:T(1,128)} %copy-done.34) | copy-start | bytes 24580
  1334.1 48.3 %copy-start.49 = (f32[128]{0:T(128)S(1)}, f32[128]{0:T(128)}, u32[]{:S(2)}) copy-start(f32[128]{0:T(128)} %copy-done.48) | copy-start | bytes 1540
  1334.1 93.4 %reduce-scatter.21.cloned.1.call-start = ((), (), s32[]{:S(2)}) async-start(), calls=%async_computation.21 | async-start | bytes 3932160 | tf_op jit(solution)/shard_map/reduce_scatter | solution.py:301
  1342.8 39.5 %copy-start.7 = (bf16[1,128,2048]{2,1,0:T(8,128)(2,1)S(1)}, bf16[1,128,2048]{2,1,0:T(8,128)(2,1)}, u32[]{:S(2)}) copy-start(bf16[1,128,2048]{2,1,0:T(8,128)(2,1)} %param.16) | copy-start | bytes 1572868
  1342.8 42.4 %copy-start.10 = (bf16[8,128,256]{1,2,0:T(8,128)(2,1)S(1)}, bf16[8,128,256]{1,2,0:T(8,128)(2,1)}, u32[]{:S(2)}) copy-start(bf16[8,128,256]{1,2,0:T(8,128)(2,1)} %copy-done.9) | copy-start | bytes 1572868
  1342.9 222.4 %reduce-scatter.29.cloned.1.call-start = ((), (), s32[]{:S(2)}) async-start(), calls=%async_computation.27 | async-start | bytes 1081344
  1385.2 330.4 %reduce-scatter.23.cloned.1.call-start = ((), (), s32[]{:S(2)}) async-start(), calls=%async_computation.22 | async-start | bytes 8650752 | tf_op jit(solution)/shard_map/reduce_scatter | solution.py:255
  1390.9 10.7 copy-start.74
  1391.0 18.4 %slice-start.2 = ((s8[8388608]{0:T(1024)(128)(4,1)}), s8[4194304]{0:T(1024)(128)(4,1)S(1)}, s32[]{:S(2)}) async-start(s8[8388608]{0:T(1024)(128)(4,1)} %bitcast.338), calls=%async_computation.30 | async-start | bytes 8388608
  1401.7 7.7 copy-start.72
  1401.7 12.4 slice-start
  1420.3 12.1 copy-start.78
  1427.5 27.5 %all-to-all-start.4 = ((bf16[8,64,768]{2,1,0:T(8,128)(2,1)}), bf16[8,64,768]{2,1,0:T(8,128)(2,1)}, u32[]{:S(2)}, u32[]{:S(2)}) async-start(bf16[8,64,768]{2,1,0:T(8,128)(2,1)} %bitcast.279), calls=%async_computation.8 | async-start | bytes 1572864 | tf_op jit(solution)/shard_map/all_to_all | solution.py:303
  1460.3 257.0 %copy-start.1 = (bf16[1,512,2048]{2,1,0:T(8,128)(2,1)S(1)}, bf16[1,512,2048]{2,1,0:T(8,128)(2,1)}, u32[]{:S(2)}) copy-start(bf16[1,512,2048]{2,1,0:T(8,128)(2,1)} %param.30) | copy-start | bytes 6291460
  (38 other events, 163.7 us)
Sparse Core Ops, SparseCore 0:
  44.5 43.5 all-gather.14
  90.2 46.9 all-gather.12
  140.2 85.4 all-gather.16
  228.5 75.2 all-gather.22
  306.6 75.9 all-gather.24
  386.1 75.9 all-gather.20
  465.7 75.9 all-gather.18
  651.9 148.6 reduce-scatter.16
  802.9 150.8 reduce-scatter.14
  955.9 148.9 reduce-scatter.24
  1107.3 149.2 reduce-scatter.26
  1334.2 48.1 reduce-scatter.18
  1385.3 42.1 reduce-scatter.20
  1429.6 135.6 reduce-scatter.28
  1567.5 148.0 reduce-scatter.22

commit v2 on v1

--- a/solution.py
+++ b/solution.py
@@ -1,8 +1,11 @@
+import functools
 import math
 
 import jax
 import jax.numpy as jnp
 from jax import lax
+from jax.experimental import pallas as pl
+from jax.experimental.pallas import tpu as pltpu
 from jax.sharding import PartitionSpec as P
 
 HEADS = 16
@@ -12,20 +15,497 @@
 epsilon = 1e-05
 masked_score = -1e30
 BOTH = ("row", "blk")
+MESH = pl.DeviceIdType.MESH
 bf16 = jnp.bfloat16
 f32 = jnp.float32
-
-
-def mm(a, b):
+EXTRA = 128
+
+
+def dot(a, b):
     return jnp.dot(a, b, preferred_element_type=f32)
 
 
-def mm_tn(a, b):
+def dot_nt(a, b):
+    return lax.dot_general(a, b, (((1,), (1,)), ((), ())), preferred_element_type=f32)
+
+
+def dot_tn(a, b):
     return lax.dot_general(a, b, (((0,), (0,)), ((), ())), preferred_element_type=f32)
 
 
-def mm_nt(a, b):
-    return lax.dot_general(a, b, (((1,), (1,)), ((), ())), preferred_element_type=f32)
+def place():
+    row, blk = lax.axis_index("row"), lax.axis_index("blk")
+    return row, blk // 2, blk % 2
+
+
+def partners():
+    row, z, c = place()
+    blk = z * 2 + c
+    return {
+        "sib": (row, z * 2 + (1 - c)),
+        "x": (row ^ 1, blk),
+        "y": (row ^ 2, blk),
+        "z1": (row, ((z + 1) % 4) * 2 + c),
+        "z2": (row, ((z + 2) % 4) * 2 + c),
+        "z3": (row, ((z + 3) % 4) * 2 + c),
+    }
+
+
+def remote(src, dst, send, recv, to):
+    return pltpu.make_async_remote_copy(
+        src_ref=src,
+        dst_ref=dst,
+        send_sem=send,
+        recv_sem=recv,
+        device_id=to,
+        device_id_type=MESH,
+    )
+
+
+def greet(targets):
+    barrier = pltpu.get_barrier_semaphore()
+    for to in targets:
+        pl.semaphore_signal(barrier, inc=1, device_id=to, device_id_type=MESH)
+    pl.semaphore_wait(barrier, len(targets))
+
+
+def moe_kernel(
+    steps,
+    x_ref,
+    c_ref,
+    mask_ref,
+    router_ref,
+    wgu_ref,
+    wd_ref,
+    xall,
+    out_ref,
+    back_ref,
+    dwg_ref,
+    dwu_ref,
+    dwd_ref,
+    xbuf,
+    cbuf,
+    hbuf,
+    gbuf,
+    po,
+    pb,
+    ro,
+    rb,
+    so,
+    sb,
+    p1ao,
+    p1bo,
+    p1ab,
+    p1bb,
+    p2o,
+    p2b,
+    zo,
+    zb,
+    ag_send,
+    ag_recv,
+    rs_send,
+    rs_recv,
+    load_sem,
+):
+    row, z, c = place()
+    to = partners()
+    width = x_ref.shape[-1]
+    half = width // 2
+    hidden = wd_ref.shape[0]
+    me = row * 8 + z * 2 + c
+    expert = me // 2
+
+    greet(list(to.values()))
+
+    def ag(j, k, src, dst, who):
+        return remote(src, dst, ag_send.at[j, k], ag_recv.at[j, k], to[who])
+
+    def own_copy(j):
+        return pltpu.make_async_copy(
+            x_ref.at[j], xall.at[j, row, z, c], load_sem.at[2 + j % 4]
+        )
+
+    def z_copies(j):
+        slot = xall.at[j, row, z, c]
+        return [ag(j, k, x_ref.at[j], slot, "z%d" % (k + 1)) for k in range(3)]
+
+    def line_copies(j):
+        line = xall.at[j, row, :, c]
+        return [
+            ag(j, 3, line, line, "x"),
+            ag(j, 4, line, line, "y"),
+            ag(j, 5, line, line, "sib"),
+        ]
+
+    def relay_copies(j):
+        a = xall.at[j, row ^ 1, :, c, :, pl.ds(0, half)]
+        b = xall.at[j, row ^ 2, :, c, :, pl.ds(half, half)]
+        s1 = xall.at[j, row ^ 1, :, c]
+        s2 = xall.at[j, row ^ 2, :, c]
+        return [
+            ag(j, 6, a, a, "y"),
+            ag(j, 7, b, b, "x"),
+            ag(j, 8, s1, s1, "sib"),
+            ag(j, 9, s2, s2, "sib"),
+        ]
+
+    def last_copies(j):
+        s3 = xall.at[j, row ^ 3, :, c]
+        return [ag(j, 10, s3, s3, "sib")]
+
+    def ag_z(j):
+        own_copy(j).start()
+        for cp in z_copies(j):
+            cp.start()
+
+    def ag_xy(j):
+        own_copy(j).wait()
+        for cp in z_copies(j):
+            cp.wait_recv()
+        for cp in line_copies(j):
+            cp.start()
+
+    def ag_rel(j):
+        for cp in line_copies(j)[:2]:
+            cp.wait_recv()
+        for cp in relay_copies(j):
+            cp.start()
+
+    def ag_fin(j):
+        for cp in relay_copies(j)[:2]:
+            cp.wait_recv()
+        for cp in last_copies(j):
+            cp.start()
+
+    def loads(j):
+        return [
+            pltpu.make_async_copy(xall.at[j], xbuf.at[j % 2], load_sem.at[0]),
+            pltpu.make_async_copy(
+                c_ref.at[:, :, :, j], cbuf.at[j % 2], load_sem.at[1]
+            ),
+        ]
+
+    def ag_done(j):
+        line_copies(j)[2].wait_recv()
+        for cp in relay_copies(j)[2:] + last_copies(j):
+            cp.wait_recv()
+        for cp in loads(j):
+            cp.start()
+
+    def ag_sent(j):
+        for cp in z_copies(j) + line_copies(j) + relay_copies(j) + last_copies(j):
+            cp.wait_send()
+
+    arrays = (
+        (po, ro, so, p1ao, p1bo, p2o, zo, out_ref),
+        (pb, rb, sb, p1ab, p1bb, p2b, zb, back_ref),
+    )
+
+    def rs(i, q, k, src, dst, who):
+        s = i % 2
+        return remote(src, dst, rs_send.at[q, s, k], rs_recv.at[q, s, k], to[who])
+
+    def rs_sib_copy(q, i):
+        p, r = arrays[q][:2]
+        return rs(i, q, 0, p.at[:, :, 1 - c], r.at[i % 2], "sib")
+
+    def p1_copies(q, i):
+        p, r, s, p1a, p1b, p2, zz, out = arrays[q]
+        part = s.at[i % 2, row ^ 3]
+        rest = p.shape[-1] - half
+        return [
+            rs(i, q, 1, part.at[:, :, pl.ds(0, half)], p1a.at[i % 2], "y"),
+            rs(i, q, 2, part.at[:, :, pl.ds(half, rest)], p1b.at[i % 2], "x"),
+        ]
+
+    def p2_copies(q, i):
+        p, r, s, p1a, p1b, p2, zz, out = arrays[q]
+        return [
+            rs(i, q, 3, s.at[i % 2, row ^ 1], p2.at[i % 2, 0], "x"),
+            rs(i, q, 4, s.at[i % 2, row ^ 2], p2.at[i % 2, 1], "y"),
+        ]
+
+    def rsz_copies(q, i):
+        p, r, s, p1a, p1b, p2, zz, out = arrays[q]
+        return [
+            rs(
+                i,
+                q,
+                5 + k,
+                s.at[i % 2, row, (z + k + 1) % 4],
+                zz.at[i % 2, k],
+                "z%d" % (k + 1),
+            )
+            for k in range(3)
+        ]
+
+    def rs_sib(q, i):
+        rs_sib_copy(q, i).start()
+
+    def rs_p1(q, i):
+        p, r, s, p1a, p1b, p2, zz, out = arrays[q]
+        cp = rs_sib_copy(q, i)
+        cp.wait_recv()
+
+        @pl.loop(0, 4)
+        def _(a):
+            s[i % 2, a] = (
+                p[a, :, c].astype(f32) + r[i % 2, a].astype(f32)
+            ).astype(bf16)
+
+        cp.wait_send()
+        for cp in p1_copies(q, i):
+            cp.start()
+
+    def rs_p2(q, i):
+        p, r, s, p1a, p1b, p2, zz, out = arrays[q]
+        rest = p.shape[-1] - half
+        copies = p1_copies(q, i)
+        copies[0].wait_recv()
+        at = s.at[i % 2, row ^ 1]
+        at[:, :, pl.ds(0, half)] = (
+            at[:, :, pl.ds(0, half)].astype(f32) + p1a[i % 2].astype(f32)
+        ).astype(bf16)
+        out_copies = p2_copies(q, i)
+        out_copies[0].start()
+        copies[1].wait_recv()
+        at = s.at[i % 2, row ^ 2]
+        at[:, :, pl.ds(half, rest)] = (
+            at[:, :, pl.ds(half, rest)].astype(f32) + p1b[i % 2].astype(f32)
+        ).astype(bf16)
+        out_copies[1].start()
+
+    def rs_z(q, i):
+        p, r, s, p1a, p1b, p2, zz, out = arrays[q]
+        for cp in p2_copies(q, i):
+            cp.wait_recv()
+        s[i % 2, row] = (
+            s[i % 2, row].astype(f32)
+            + p2[i % 2, 0].astype(f32)
+            + p2[i % 2, 1].astype(f32)
+        ).astype(bf16)
+        for cp in rsz_copies(q, i):
+            cp.start()
+
+    def rs_fin(q, i):
+        p, r, s, p1a, p1b, p2, zz, out = arrays[q]
+        copies = rsz_copies(q, i)
+        for cp in copies:
+            cp.wait_recv()
+        total = s[i % 2, row, z].astype(f32)
+        for k in range(3):
+            total = total + zz[i % 2, k].astype(f32)
+        out[i] = total
+        for cp in copies + p2_copies(q, i) + p1_copies(q, i):
+            cp.wait_send()
+
+    lanes = po.shape[3]
+    rows_here = 16 * lanes
+    cut = 512
+
+    def tile(i, t):
+        s = i % 2
+        xt = xbuf[s, 2 * t : 2 * t + 2].reshape(rows_here, width)
+        mask = mask_ref[i, t * rows_here : (t + 1) * rows_here, :]
+        logits = dot(xt, router_ref[...])[:, : mask.shape[-1]]
+        logits = jnp.where(mask > 0, logits, masked_score)
+        top = jnp.max(logits, axis=-1, keepdims=True)
+        raised = jnp.where(mask > 0, jnp.exp(logits - top), 0.0)
+        lane = lax.broadcasted_iota(jnp.int32, raised.shape, 1)
+        gate = jnp.sum(
+            jnp.where(lane == expert, raised, 0.0), axis=-1, keepdims=True
+        ) / jnp.sum(raised, axis=-1, keepdims=True)
+        both = dot(xt, wgu_ref[...])
+        gp, up = both[:, :hidden], both[:, hidden:]
+        sig = jax.nn.sigmoid(gp)
+        silu = gp * sig
+        hid = (silu * up).astype(bf16)
+        hbuf[t * rows_here : (t + 1) * rows_here, :] = hid
+        slope = up * sig * (1.0 + gp * (1.0 - sig))
+        dots = jnp.zeros((rows_here, 1), f32)
+        ghid = jnp.zeros((rows_here, hidden), f32)
+        for n in range(width // cut):
+            cols = slice(n * cut, (n + 1) * cut)
+            wd = wd_ref[:, cols]
+            part = dot(hid, wd).astype(bf16).astype(f32)
+            cf = cbuf[s, 2 * t : 2 * t + 2, :, :, :, cols]
+            shape = cf.shape
+            cf = cf.reshape(rows_here, cut).astype(f32)
+            dots = dots + jnp.sum(part * cf, axis=-1, keepdims=True)
+            po[2 * t : 2 * t + 2, :, :, :, cols] = (
+                (gate * part).astype(bf16).reshape(shape)
+            )
+            gpart = (gate * cf).astype(bf16)
+            cbuf[s, 2 * t : 2 * t + 2, :, :, :, cols] = gpart.reshape(shape)
+            ghid = ghid + dot_nt(gpart, wd)
+        dgp = (ghid * slope).astype(bf16)
+        dup = (ghid * silu).astype(bf16)
+        grads = jnp.concatenate([dgp, dup], axis=1)
+        gbuf[t * rows_here : (t + 1) * rows_here, :] = grads
+        for n in range(width // cut):
+            cols = slice(n * cut, (n + 1) * cut)
+            bk = dot_nt(grads, wgu_ref[cols, :]).astype(bf16)
+            pb[2 * t : 2 * t + 2, :, :, :, cols] = bk.reshape(shape)
+        high = dots.astype(bf16).astype(f32)
+        low = dots - high
+        lane = lax.broadcasted_iota(jnp.int32, (rows_here, EXTRA), 1)
+        extra = jnp.where(lane == me, high, jnp.where(lane == me + 64, low, 0.0))
+        pb[2 * t : 2 * t + 2, :, :, :, width:] = extra.astype(bf16).reshape(
+            shape[:-1] + (EXTRA,)
+        )
+
+    def weight_grads(i):
+        s = i % 2
+        every = 2 * rows_here
+
+        @pl.loop(0, width // 256)
+        def _(n):
+            cols = pl.ds(pl.multiple_of(n * 256, 256), 256)
+            xt = xbuf[s, :, :, :, :, cols].reshape(every, 256)
+            r = dot_tn(xt, gbuf[...])
+            dwg_ref[cols, :] += r[:, :hidden]
+            dwu_ref[cols, :] += r[:, hidden:]
+
+        @pl.loop(0, width // cut)
+        def _(n):
+            cols = pl.ds(pl.multiple_of(n * cut, cut), cut)
+            gpart = cbuf[s, :, :, :, :, cols].reshape(every, cut)
+            dwd_ref[:, cols] += dot_tn(hbuf[...], gpart)
+
+    dwg_ref[...] = jnp.zeros_like(dwg_ref)
+    dwu_ref[...] = jnp.zeros_like(dwu_ref)
+    dwd_ref[...] = jnp.zeros_like(dwd_ref)
+    for j in range(3):
+        ag_z(j)
+    ag_xy(0)
+    ag_xy(1)
+    ag_rel(0)
+    ag_rel(1)
+    ag_fin(0)
+    ag_done(0)
+    ag_fin(1)
+
+    @pl.loop(0, steps + 2)
+    def _(i):
+        def when(low, high, *work):
+            @pl.when((i >= low) & (i < high))
+            def _():
+                for f in work:
+                    f()
+
+        @pl.when(i + 3 < steps)
+        def _():
+            ag_z(i + 3)
+
+        @pl.when(i + 2 < steps)
+        def _():
+            ag_xy(i + 2)
+
+        when(1, steps + 1, lambda: rs_p2(0, i - 1))
+        when(2, steps + 2, lambda: rs_z(1, i - 2))
+
+        @pl.when(i < steps)
+        def _():
+            for cp in loads(i):
+                cp.wait()
+            tile(i, 0)
+
+        @pl.when(i + 2 < steps)
+        def _():
+            ag_rel(i + 2)
+
+        when(1, steps + 1, lambda: rs_p2(1, i - 1))
+        when(2, steps + 2, lambda: rs_fin(0, i - 2))
+
+        @pl.when(i < steps)
+        def _():
+            tile(i, 1)
+            rs_sib(0, i)
+            rs_sib(1, i)
+
+        @pl.when(i + 2 < steps)
+        def _():
+            ag_fin(i + 2)
+
+        when(0, steps, lambda: rs_p1(0, i))
+        when(1, steps + 1, lambda: rs_z(0, i - 1))
+        when(2, steps + 2, lambda: rs_fin(1, i - 2))
+        when(0, steps, lambda: rs_p1(1, i))
+
+        @pl.when(i < steps)
+        def _():
+            weight_grads(i)
+
+        @pl.when(i + 1 < steps)
+        def _():
+            ag_done(i + 1)
+
+    @pl.loop(0, steps)
+    def _(j):
+        ag_sent(j)
+
+
+def moe(expert_in, upstream_all, mask, router, gate_up, down):
+    tokens, width = expert_in.shape
+    hidden = down.shape[0]
+    steps = tokens // 16
+    wide = width + EXTRA
+    half = width // 2
+    any_, vm = pl.BlockSpec(memory_space=pl.ANY), pl.BlockSpec(memory_space=pltpu.VMEM)
+    dma = pltpu.SemaphoreType.DMA
+    router = jnp.pad(router, ((0, 0), (0, 128 - router.shape[1])))
+    results = pl.pallas_call(
+        functools.partial(moe_kernel, steps),
+        out_shape=(
+            jax.ShapeDtypeStruct((steps, 4, 4, 2, 16, width), bf16),
+            jax.ShapeDtypeStruct((steps, 16, width), f32),
+            jax.ShapeDtypeStruct((steps, 16, wide), f32),
+            jax.ShapeDtypeStruct((width, hidden), f32),
+            jax.ShapeDtypeStruct((width, hidden), f32),
+            jax.ShapeDtypeStruct((hidden, width), f32),
+        ),
+        in_specs=[any_, any_, vm, vm, vm, vm],
+        out_specs=(any_, vm, vm, vm, vm, vm),
+        scratch_shapes=[
+            pltpu.VMEM((2, 4, 4, 2, 16, width), bf16),
+            pltpu.VMEM((2, 4, 4, 2, 16, width), bf16),
+            pltpu.VMEM((512, hidden), bf16),
+            pltpu.VMEM((512, 2 * hidden), bf16),
+            pltpu.VMEM((4, 4, 2, 16, width), bf16),
+            pltpu.VMEM((4, 4, 2, 16, wide), bf16),
+            pltpu.VMEM((2, 4, 4, 16, width), bf16),
+            pltpu.VMEM((2, 4, 4, 16, wide), bf16),
+            pltpu.VMEM((2, 4, 4, 16, width), bf16),
+            pltpu.VMEM((2, 4, 4, 16, wide), bf16),
+            pltpu.VMEM((2, 4, 16, half), bf16),
+            pltpu.VMEM((2, 4, 16, half), bf16),
+            pltpu.VMEM((2, 4, 16, half), bf16),
+            pltpu.VMEM((2, 4, 16, wide - half), bf16),
+            pltpu.VMEM((2, 2, 4, 16, width), bf16),
+            pltpu.VMEM((2, 2, 4, 16, wide), bf16),
+            pltpu.VMEM((2, 3, 16, width), bf16),
+            pltpu.VMEM((2, 3, 16, wide), bf16),
+            dma((steps, 11)),
+            dma((steps, 11)),
+            dma((2, 2, 8)),
+            dma((2, 2, 8)),
+            dma((6,)),
+        ],
+        compiler_params=pltpu.CompilerParams(
+            collective_id=1, has_side_effects=True, vmem_limit_bytes=60 * 2**20
+        ),
+        cost_estimate=pl.CostEstimate(
+            flops=78 * 10**9, bytes_accessed=10**8, transcendentals=0
+        ),
+    )(
+        expert_in.reshape(steps, 16, width),
+        upstream_all.reshape(4, 4, 2, steps, 16, width),
+        mask,
+        router,
+        gate_up,
+        down,
+    )
+    return results[1:]
 
 
 def rope_tables(count):
@@ -45,6 +525,104 @@
 
 def norm_back(v, r, g, c, mean_vgc):
     return r * g * c - v * (r * r * r) * mean_vgc
+
+
+def experts_by_scan(expert_in, upstream, gates, gate_local, up_local, down_local):
+    tokens, width = expert_in.shape
+    experts = gates.shape[1]
+    rows, blocks = lax.axis_size("row"), lax.axis_size("blk")
+    devices = rows * blocks
+    me = lax.axis_index("row") * blocks + lax.axis_index("blk")
+    parts = devices * tokens // 2048
+    step = tokens // parts
+    all_gates = lax.all_gather(gates, BOTH, axis=0, tiled=False)
+    own_gate = jnp.sum(
+        jnp.where(
+            jnp.arange(experts, dtype=jnp.int32)[None, None, :] == me // 2,
+            all_gates,
+            0.0,
+        ),
+        axis=-1,
+    )
+
+    def expert_part(sums, items):
+        own_rows, own_upstream, gate_col = items
+        got = lax.all_gather(own_rows, BOTH, axis=0, tiled=True)
+        up_stream = lax.all_gather(own_upstream, BOTH, axis=0, tiled=True)
+        gate_col = gate_col.reshape(devices * step, 1)
+        gate_pre = dot(got, gate_local)
+        up_pre = dot(got, up_local)
+        sig = jax.nn.sigmoid(gate_pre)
+        silu = gate_pre * sig
+        hidden = (silu * up_pre).astype(bf16)
+        part_f = dot(hidden, down_local).astype(bf16).astype(f32)
+        up_f = up_stream.astype(f32)
+        dots = jnp.sum(part_f * up_f, axis=-1).reshape(devices, step)
+        mixed = (gate_col * part_f).astype(bf16)
+        out = lax.psum_scatter(mixed, BOTH, scatter_dimension=0, tiled=True)
+        grad_part = (gate_col * up_f).astype(bf16)
+        grad_hidden = dot_nt(grad_part, down_local)
+        grad_gate_pre = (
+            grad_hidden * up_pre * sig * (1.0 + gate_pre * (1.0 - sig))
+        ).astype(bf16)
+        grad_up_pre = (grad_hidden * silu).astype(bf16)
+        grad_rows = (
+            dot_nt(grad_gate_pre, gate_local) + dot_nt(grad_up_pre, up_local)
+        ).astype(bf16)
+        back = lax.psum_scatter(grad_rows, BOTH, scatter_dimension=0, tiled=True)
+        sums = (
+            sums[0] + dot_tn(got, grad_gate_pre),
+            sums[1] + dot_tn(got, grad_up_pre),
+            sums[2] + dot_tn(hidden, grad_part),
+        )
+        return sums, (out, back, dots)
+
+    sums = (
+        jnp.zeros(gate_local.shape, f32),
+        jnp.zeros(up_local.shape, f32),
+        jnp.zeros(down_local.shape, f32),
+    )
+    items = (
+        expert_in.reshape(parts, step, width),
+        upstream.reshape(parts, step, width),
+        own_gate.reshape(devices, parts, step).transpose(1, 0, 2),
+    )
+    if parts > 2:
+        sums, (outs, backs, dots) = lax.scan(expert_part, sums, items)
+    else:
+        made = []
+        for part in range(parts):
+            sums, result = expert_part(sums, tuple(item[part] for item in items))
+            made.append(result)
+        outs, backs, dots = (jnp.stack(some) for some in zip(*made))
+    dots = dots.transpose(1, 0, 2).reshape(devices, tokens)
+    outs = outs.reshape(tokens, width)
+    backs = backs.reshape(tokens, width)
+    dots = lax.all_to_all(dots, BOTH, split_axis=0, concat_axis=0, tiled=True)
+    grad_gates = jnp.sum(dots.reshape(experts, 2, tokens), axis=1).T
+    return outs.astype(f32), backs.astype(f32), grad_gates, sums
+
+
+def experts_in_kernel(
+    expert_in, upstream, routed, router, gate_local, up_local, down_local
+):
+    tokens, width = expert_in.shape
+    experts = router.shape[1]
+    steps = tokens // 16
+    upstream_all = lax.all_gather(upstream, BOTH, axis=0, tiled=False)
+    mask = lax.all_gather(routed.astype(bf16), BOTH, axis=0, tiled=False).astype(f32)
+    mask = mask.reshape(-1, steps, 16, experts).transpose(1, 0, 2, 3)
+    mask = mask.reshape(steps, -1, experts)
+    gate_up = jnp.concatenate([gate_local, up_local], axis=1)
+    outs, backs, *sums = moe(
+        expert_in, upstream_all, mask, router, gate_up, down_local
+    )
+    outs = outs.reshape(tokens, width)
+    backs = backs.reshape(tokens, width + EXTRA)
+    dots = backs[:, width : width + 2 * experts]
+    dots = dots + backs[:, width + 64 : width + 64 + 2 * experts]
+    grad_gates = jnp.sum(dots.reshape(tokens, experts, 2), axis=2)
+    return outs, backs[:, :width], grad_gates, sums
 
 
 def body(
@@ -109,7 +687,7 @@
     qkv_cols = lax.all_gather(cols, "row", axis=0, tiled=True)
     full_output = lax.all_gather(output_weight, BOTH, axis=0, tiled=True)
 
-    qkv = mm(normed_row, qkv_cols)
+    qkv = dot(normed_row, qkv_cols)
     query_pre = qkv[:, :head_cols]
     key_pre = qkv[:, head_cols : 2 * head_cols]
     value = qkv[:, 2 * head_cols :].astype(bf16)
@@ -145,12 +723,12 @@
     )
     attended_low = attended_low.transpose(1, 0, 2).reshape(tokens, width)
 
-    residual_mid = x + mm(attended_low, full_output)
+    residual_mid = x + dot(attended_low, full_output)
     r_exp = lax.rsqrt(
         jnp.mean(residual_mid * residual_mid, axis=-1, keepdims=True) + epsilon
     )
     expert_in = (residual_mid * r_exp * gain_expert).astype(bf16)
-    logits = mm(expert_in, router)
+    logits = dot(expert_in, router)
     routes = expert_ids[0]
     routed = jnp.any(
         routes[:, :, None] == jnp.arange(experts, dtype=jnp.int32)[None, None, :],
@@ -163,85 +741,25 @@
     gates = gates / jnp.sum(gates, axis=-1, keepdims=True)
 
     gate_local, up_local, down_local = gate_weight[0], up_weight[0], down_weight[0]
-    parts = devices * tokens // 2048
-    step = tokens // parts
-    all_gates = lax.all_gather(gates, BOTH, axis=0, tiled=False)
-    own_gate = jnp.sum(
-        jnp.where(
-            jnp.arange(experts, dtype=jnp.int32)[None, None, :] == me // 2,
-            all_gates,
-            0.0,
-        ),
-        axis=-1,
-    )
-
-    def expert_part(sums, items):
-        own_rows, own_upstream, gate_col = items
-        got = lax.all_gather(own_rows, BOTH, axis=0, tiled=True)
-        up_stream = lax.all_gather(own_upstream, BOTH, axis=0, tiled=True)
-        gate_col = gate_col.reshape(devices * step, 1)
-        gate_pre = mm(got, gate_local)
-        up_pre = mm(got, up_local)
-        sig = jax.nn.sigmoid(gate_pre)
-        silu = gate_pre * sig
-        hidden = (silu * up_pre).astype(bf16)
-        part_f = mm(hidden, down_local).astype(bf16).astype(f32)
-        up_f = up_stream.astype(f32)
-        dots = jnp.sum(part_f * up_f, axis=-1).reshape(devices, step)
-        mixed = (gate_col * part_f).astype(bf16)
-        out = lax.psum_scatter(mixed, BOTH, scatter_dimension=0, tiled=True)
-        grad_part = (gate_col * up_f).astype(bf16)
-        grad_hidden = mm_nt(grad_part, down_local)
-        grad_gate_pre = (
-            grad_hidden * up_pre * sig * (1.0 + gate_pre * (1.0 - sig))
-        ).astype(bf16)
-        grad_up_pre = (grad_hidden * silu).astype(bf16)
-        grad_rows = (
-            mm_nt(grad_gate_pre, gate_local) + mm_nt(grad_up_pre, up_local)
-        ).astype(bf16)
-        back = lax.psum_scatter(grad_rows, BOTH, scatter_dimension=0, tiled=True)
-        sums = (
-            sums[0] + mm_tn(got, grad_gate_pre),
-            sums[1] + mm_tn(got, grad_up_pre),
-            sums[2] + mm_tn(hidden, grad_part),
+    if (rows, blocks, 2 * experts, heads_here) == (4, 8, 32, 2):
+        outs, backs, grad_gates, sums = experts_in_kernel(
+            expert_in, grad_out[0], routed, router, gate_local, up_local, down_local
         )
-        return sums, (out, back, dots)
-
-    sums = (
-        jnp.zeros(gate_local.shape, f32),
-        jnp.zeros(up_local.shape, f32),
-        jnp.zeros(down_local.shape, f32),
-    )
-    items = (
-        expert_in.reshape(parts, step, width),
-        grad_out[0].reshape(parts, step, width),
-        own_gate.reshape(devices, parts, step).transpose(1, 0, 2),
-    )
-    if parts > 2:
-        sums, (outs, backs, dots) = lax.scan(expert_part, sums, items)
     else:
-        made = []
-        for part in range(parts):
-            sums, result = expert_part(sums, tuple(item[part] for item in items))
-            made.append(result)
-        outs, backs, dots = (jnp.stack(some) for some in zip(*made))
+        outs, backs, grad_gates, sums = experts_by_scan(
+            expert_in, grad_out[0], gates, gate_local, up_local, down_local
+        )
     grad_gate_local, grad_up_local, grad_down_local = sums
-    dots = dots.transpose(1, 0, 2).reshape(devices, tokens)
-    outs = outs.reshape(tokens, width)
-    backs = backs.reshape(tokens, width)
-    dots = lax.all_to_all(dots, BOTH, split_axis=0, concat_axis=0, tiled=True)
-    grad_gates = jnp.sum(dots.reshape(experts, 2, tokens), axis=1).T
-    moe_out = outs.astype(f32)
-    layer_out = (residual_mid + moe_out).astype(bf16)
+    layer_out = (residual_mid + outs).astype(bf16)
     upstream = grad_out[0].astype(f32)
     grad_picked = gates * (
         grad_gates - jnp.sum(gates * grad_gates, axis=-1, keepdims=True)
     )
     grad_logits = jnp.where(routed, grad_picked, 0.0).astype(bf16)
-    grad_expert_in = backs.astype(f32) + mm_nt(
+    grad_expert_in = backs + dot_nt(
         grad_logits, router
     )
-    grad_router = mm_tn(expert_in, grad_logits)
+    grad_router = dot_tn(expert_in, grad_logits)
     grad_gain_expert = jnp.sum(grad_expert_in * residual_mid * r_exp, axis=0)
     grad_mid = upstream + norm_back(
         residual_mid,
@@ -251,11 +769,11 @@
         jnp.mean(residual_mid * gain_expert * grad_expert_in, axis=-1, keepdims=True),
     )
     grad_proj = grad_mid.astype(bf16)
-    grad_output_w = mm_tn(attended_low, grad_proj).astype(bf16)
+    grad_output_w = dot_tn(attended_low, grad_proj).astype(bf16)
     grad_output_w = lax.psum_scatter(
         grad_output_w, BOTH, scatter_dimension=0, tiled=True
     ).astype(f32)
-    grad_attended = mm_nt(grad_proj, full_output).astype(bf16)
+    grad_attended = dot_nt(grad_proj, full_output).astype(bf16)
     grad_attended = grad_attended.reshape(tokens, blocks, head_cols).transpose(1, 0, 2)
     grad_attended = lax.all_to_all(
         grad_attended, "blk", split_axis=0, concat_axis=0, tiled=True
@@ -297,13 +815,13 @@
         ],
         axis=1,
     )
-    grad_w = mm_tn(normed_row, grad_qkv).astype(bf16)
+    grad_w = dot_tn(normed_row, grad_qkv).astype(bf16)
     grad_w = lax.psum_scatter(grad_w, "row", scatter_dimension=0, tiled=True)
     grad_w = grad_w.reshape(blocks, wrows, 3 * head_cols)
     grad_w = lax.all_to_all(grad_w, "blk", split_axis=0, concat_axis=0, tiled=True)
     grad_w = grad_w.reshape(blocks, wrows, 3, head_cols).transpose(2, 1, 0, 3)
     grad_w = grad_w.reshape(3, wrows, width).astype(f32)
-    grad_normed = mm_nt(grad_qkv, qkv_cols).astype(bf16)
+    grad_normed = dot_nt(grad_qkv, qkv_cols).astype(bf16)
     grad_normed = lax.psum_scatter(
         grad_normed, "blk", scatter_dimension=0, tiled=True
     ).astype(f32)

time: 1730 us -> 1100 us (0.64)
  waiting for transfers between devices: 1140 us -> 459 us
  Pallas kernels: 0 us -> 260 us
  matrix products: 224 us -> 62.2 us
  local copies, waits for them, and re-layouts: 95.6 us -> 74.5 us
  other arithmetic: 60.6 us -> 43.1 us
    reduce_scatter x4 -> x0, waiting for transfers between devices: 526 us -> none  [the longest x2 301 us: expert_part(): out = lax.psum_scatter(mixed, BOTH, scatter_dimension=0, tiled=True)]
    pallas_call x0 -> x1, Pallas kernels: none -> 260 us  [moe(): pl.pallas_call(functools.partial(moe_kernel, steps), out_shape=(jax.Shape...]
    all_gather x4 -> x1, waiting for transfers between devices: 259 us -> 68.2 us  [experts_in_kernel(): upstream_all = lax.all_gather(upstream, BOTH, axis=0, tiled=False)]
    dot_general x27 -> x9, matrix products: 199 us -> 37 us  [the longest x3 14.4 us: dot_tn(): lax.dot_general(a, b, (((0,), (0,)), ((), ())), preferred_element_type=f32)]
    reduce_scatter x1, waiting for transfers between devices: 1.18 us -> 35.8 us  [body(): grad_w = lax.psum_scatter(grad_w, 'row', scatter_dimension=0, tiled=True)]
    all_to_all x1 -> x0, blocking collectives: 26.9 us -> none  [body(): lax.all_to_all(attended_low_cols, 'blk', split_axis=0, concat_axis=0, til...]
    all_gather x2 -> x0, local copies, waits for them, and re-layouts: 24.5 us -> none  [expert_part(): up_stream = lax.all_gather(own_upstream, BOTH, axis=0, tiled=True)]
    convert_element_type x2 -> x1, other arithmetic: 19.6 us -> 0.01 us  [experts_in_kernel(): routed.astype(bf16)]
  transfers between devices with their start and end apart: 18 -> 11, of which waited for: 17 -> 8; matrix products, arithmetic and copies ran while one was open for 15% -> 9% of each run, Pallas kernels for 0% -> 0%
where the time goes in v2:
time: 1100 us; the launch traced here: 1090 us
  waiting for transfers between devices  459 us (42%)
  Pallas kernels  260 us (24%)
  blocking collectives  159 us (14%)
  local copies, waits for them, and re-layouts  74.5 us (7%)
  matrix products  62.2 us (6%)
  other arithmetic  43.1 us (4%)
  starting transfers between devices  15.6 us (1%)
  between operations  15.3 us (1%)
    pallas_call x1, Pallas kernels, moe(): pl.pallas_call(functools.partial(moe_kernel, steps), out_shape=(jax.Shape...  260 us
    reduce_scatter x1, waiting for transfers between devices, body(): lax.psum_scatter(grad_output_w, BOTH, scatter_dimension=0, tiled=True)  145 us
    unnamed x9, waiting for transfers between devices  100 us
    all_gather x1, waiting for transfers between devices, experts_in_kernel(): upstream_all = lax.all_gather(upstream, BOTH, axis=0, tiled=False)  68.2 us
    all_gather x1, blocking collectives, experts_in_kernel(): lax.all_gather(routed.astype(bf16), BOTH, axis=0, tiled=False).astype(f32)  52.8 us
    all_gather x1, blocking collectives, body(): small = lax.all_gather(small, BOTH, axis=0, tiled=True)  40.8 us
    reduce_scatter x1, waiting for transfers between devices, body(): lax.psum_scatter(grad_normed, 'blk', scatter_dimension=0, tiled=True)  38.4 us
    unnamed x106, local copies, waits for them, and re-layouts  38.2 us
  transfers between devices with their start and end apart: 11, of which 8 were waited for; matrix products, arithmetic and copies ran while one was open for 9% of the time, Pallas kernels for 0%

profile of v2, /device:TPU:0, one launch (start us, length us, event | category | flops | bytes accessed | tf_op | source)
XLA Modules:
  0.0 1088.9 jit_solution(12406238443737672410)
XLA Ops:
  11.6 1.8 maximum_bitcast_fusion
  14.3 27.2 %all_to_all.20 = bf16[8,64,768]{2,1,0:T(8,128)(2,1)} all-to-all(bf16[8,64,768]{2,1,0:T(8,128)(2,1)S(1)} %reshape.307), channel_id=1, replica_groups=mesh['row'=4,'blk'=8] {'blk'}, dimensions={0} | all-to-all | bytes 1572864 | tf_op jit(solution)/shard_map/all_to_all | solution.py:685
  41.7 40.8 %all-gather.2 = bf16[32,64,20]{1,2,0:T(8,128)(2,1)S(1)} all-gather(bf16[1,64,20]{1,2,0:T(8,128)(2,1)S(1)} %bitcast.208), channel_id=1, replica_groups=mesh['row'=4,'blk'=8] {'row','blk'}, dimensions={0}, use_global_device_ids=true | all-gather | bytes 84480 | tf_op jit(solution)/shard_map/all_gather | solution.py:668
  83.7 1.4 fusion.51
  88.1 8.7 all-gather
  97.0 2.9 fusion.36
  99.9 1.6 fusion.4
  101.5 32.9 %all-gather.8.cloned.1.call-done = bf16[1024,2048]{1,0:T(8,128)(2,1)} async-done(((bf16[128,2048]{1,0:T(8,128)(2,1)}), bf16[1024,2048]{1,0:T(8,128)(2,1)}) %all-gather.8.cloned.1.call-update) | async-done | bytes 4194320 | tf_op jit(solution)/shard_map/all_gather | solution.py:678
  134.4 6.2 fusion.57
  141.7 15.1 %psum.14 = f32[2,1024]{1,0:T(2,128)S(1)} all-reduce(f32[2,1024]{1,0:T(2,128)S(1)} %pad_maximum_fusion.8), channel_id=1, replica_groups=mesh['row'=4,'blk'=8] {'blk'}, use_global_device_ids=true, to_apply=%region_3.0 | all-reduce | flops 2048 | bytes 16384 | tf_op jit(solution)/shard_map/psum | solution.py:697
  159.1 2.4 copy.181
  161.5 2.4 copy.180
  163.8 2.3 fusion.52
  166.1 2.4 copy.182
  168.4 2.4 copy.183
  170.8 4.2 subtract_convert_fusion.1
  175.0 10.6 fusion.55
  185.6 4.7 fusion.6
  190.3 2.0 copy-done.1
  192.3 1.7 fusion.56
  195.0 4.2 all-to-all-start.1
  199.2 52.8 %all-gather.1 = bf16[4096,16]{0,1:T(8,128)(2,1)S(1)} all-gather(bf16[128,16]{0,1:T(8,128)(2,1)S(1)} %convert_element_type.131), channel_id=3, replica_groups=mesh['row'=4,'blk'=8] {'row','blk'}, dimensions={0}, use_global_device_ids=true | all-gather | bytes 135168 | tf_op jit(solution)/shard_map/all_gather | solution.py:613
  252.0 2.1 reshape.336
  254.1 3.2 copy.147
  257.2 2.0 pad.4.router_ref
  259.2 4.8 pad_maximum_fusion.wgu_ref
  264.0 5.0 multiply_reduce_fusion.3
  271.0 68.2 %all-gather.14.cloned.1.call-done = bf16[32,128,2048]{2,1,0:T(8,128)(2,1)} async-done(((bf16[1,128,2048]{2,1,0:T(8,128)(2,1)}), bf16[32,128,2048]{2,1,0:T(8,128)(2,1)}) %all-gather.14.cloned.1.call-update) | async-done | bytes 16777232 | tf_op jit(solution)/shard_map/all_gather | solution.py:612
  339.2 260.1 %shard_map.263 = (bf16[8,4,4,2,16,2048]{5,4,3,2,1,0:T(8,128)(2,1)}, f32[8,16,2048]{2,1,0:T(8,128)}, f32[8,16,2176]{2,1,0:T(8,128)}, f32[2048,512]{1,0:T(8,128)},...) custom-call(bf16[8,16,2048]{2,1,0:T(8,128)(2,1)} %bitcast.162, bf16[4,4,2,8,16,2048]{5,4,3,2,1,0:T(8,128)(2,1)} %bitcast.227, ...), custom_call_target="tpu_custom_call" | custom-call | flops 77999996928 | bytes 100000000 | tf_op jit(solution)/shard_map/pallas_call | solution.py:457
  600.5 2.4 multiply_reduce_fusion
  602.9 3.3 convert_add_fusion
  607.2 3.7 convolution_convert_fusion.3
  610.9 2.0 copy.177
  612.9 6.0 all-to-all-start.2
  619.2 15.2 %all-to-all-done.2 = bf16[8,128,256]{1,2,0:T(8,128)(2,1)} async-done(((bf16[8,128,256]{1,2,0:T(8,128)(2,1)}), bf16[8,128,256]{1,2,0:T(8,128)(2,1)}, u32[]{:S(2)}, u32[]{:S(2)}) %all-to-all-start.2) | async-done | bytes 524320 | tf_op jit(solution)/shard_map/all_to_all | solution.py:778
  634.4 2.2 copy.150
  636.6 2.1 reshape.323
  638.6 4.8 convolution_convert_fusion.4
  643.6 4.8 multiply_convert_fusion
  648.5 2.0 fusion.8
  651.9 2.0 multiply_subtract_fusion.1
  655.2 2.5 copy.157
  657.7 2.9 pad_maximum_fusion.3
  660.6 2.5 copy.161
  663.1 2.1 fusion.23
  665.2 14.8 %psum.15 = f32[2,1024]{1,0:T(2,128)S(1)} all-reduce(f32[2,1024]{1,0:T(2,128)S(1)} %pad_maximum_fusion.9), channel_id=1, replica_groups=mesh['row'=4,'blk'=8] {'blk'}, use_global_device_ids=true, to_apply=%region_16.17 | all-reduce | flops 2048 | bytes 16384 | tf_op jit(solution)/shard_map/psum | solution.py:805
  680.0 2.1 fusion.25
  683.1 5.0 convolution_convert_fusion.1
  689.5 7.5 convolution_convert_fusion.2
  697.3 38.4 %reduce-scatter.7.cloned.1.call-done = bf16[128,2048]{1,0:T(8,128)(2,1)} async-done(((bf16[1024,2048]{1,0:T(8,128)(2,1)}), bf16[128,2048]{1,0:T(8,128)(2,1)}) %reduce-scatter.7.cloned.1.call-update) | async-done | bytes 524304 | tf_op jit(solution)/shard_map/reduce_scatter | solution.py:825
  738.7 6.7 convolution_convert_fusion
  745.4 35.8 %reduce-scatter.9.cloned.1.call-done = bf16[512,768]{1,0:T(8,128)(2,1)} async-done(((bf16[2048,768]{1,0:T(8,128)(2,1)}), bf16[512,768]{1,0:T(8,128)(2,1)}) %reduce-scatter.9.cloned.1.call-update) | async-done | bytes 786448 | tf_op jit(solution)/shard_map/reduce_scatter | solution.py:819
  781.2 4.6 all-to-all-start.3
  785.9 22.6 %all-to-all-done.3 = bf16[8,64,768]{2,1,0:T(8,128)(2,1)S(1)} async-done(((bf16[8,64,768]{2,1,0:T(8,128)(2,1)}), bf16[8,64,768]{2,1,0:T(8,128)(2,1)S(1)}, u32[]{:S(2)}, u32[]{:S(2)}) %all-to-all-start.3) | async-done | bytes 786464 | tf_op jit(solution)/shard_map/all_to_all | solution.py:821
  808.4 1.8 reshape.334
  810.3 4.7 fusion.49
  820.1 99.0 %reduce-scatter.13.cloned.1.call-done = f32[64,20]{1,0:T(8,128)} async-done(((f32[2048,20]{1,0:T(8,128)}), f32[64,20]{1,0:T(8,128)}) %reduce-scatter.13.cloned.1.call-update) | async-done | bytes 5136
  922.5 1.4 copy.188
  923.9 145.4 %reduce-scatter.11.cloned.1.call-done = bf16[64,2048]{1,0:T(8,128)(2,1)} async-done(((bf16[2048,2048]{1,0:T(8,128)(2,1)}), bf16[64,2048]{1,0:T(8,128)(2,1)}) %reduce-scatter.11.cloned.1.call-update) | async-done | bytes 262160 | tf_op jit(solution)/shard_map/reduce_scatter | solution.py:773
  1069.3 1.8 convert_element_type.129
  1071.1 4.8 copy.202
  1075.9 2.1 copy.203
  1078.1 1.6 copy-done.13
  1079.6 2.0 copy.204
  (167 shorter events, 35.2 us)
Async XLA Ops:
  7.2 94.3 %all-gather.10.cloned.1.call-start = ((), (), s32[]{:S(2)}) async-start(), calls=%async_computation.9 | async-start | bytes 3932160 | tf_op jit(solution)/shard_map/all_gather | solution.py:687
  10.1 31.6 %copy-start.34 = (bf16[64,16]{0,1:T(8,128)(2,1)S(1)}, bf16[64,16]{0,1:T(8,128)(2,1)}, u32[]{:S(2)}) copy-start(bf16[64,16]{0,1:T(8,128)(2,1)} %param.27) | copy-start | bytes 6148
  10.1 31.6 %copy-start.37 = (bf16[64]{0:T(256)(128)(2,1)S(1)}, bf16[64]{0:T(256)(128)(2,1)}, u32[]{:S(2)}) copy-start(bf16[64]{0:T(256)(128)(2,1)} %param.19) | copy-start | bytes 388
  10.1 31.5 %copy-start.38 = (bf16[64]{0:T(256)(128)(2,1)S(1)}, bf16[64]{0:T(256)(128)(2,1)}, u32[]{:S(2)}) copy-start(bf16[64]{0:T(256)(128)(2,1)} %param.20) | copy-start | bytes 388
  10.1 31.5 %copy-start.39 = (bf16[64]{0:T(256)(128)(2,1)S(1)}, bf16[64]{0:T(256)(128)(2,1)}, u32[]{:S(2)}) copy-start(bf16[64]{0:T(256)(128)(2,1)} %param.21) | copy-start | bytes 388
  10.1 31.5 %copy-start.40 = (bf16[64]{0:T(256)(128)(2,1)S(1)}, bf16[64]{0:T(256)(128)(2,1)}, u32[]{:S(2)}) copy-start(bf16[64]{0:T(256)(128)(2,1)} %param.22) | copy-start | bytes 388
  11.1 71.6 %copy-start.5 = (bf16[1,128,2048]{2,1,0:T(8,128)(2,1)S(1)}, bf16[1,128,2048]{2,1,0:T(8,128)(2,1)}, u32[]{:S(2)}) copy-start(bf16[1,128,2048]{2,1,0:T(8,128)(2,1)} %param.16) | copy-start | bytes 1572868
  41.6 92.9 %all-gather.8.cloned.1.call-start = ((), (), s32[]{:S(2)}) async-start(), calls=%async_computation.8 | async-start | bytes 4718592 | tf_op jit(solution)/shard_map/all_gather | solution.py:678
  82.8 2.4 copy-start.7
  83.5 3.3 copy-start.32
  83.7 4.4 copy-start.41
  85.2 0.6 copy-start.30
  86.8 177.2 %all-gather.12.cloned.1.call-start = ((), (), s32[]{:S(2)}) async-start(), calls=%async_computation.10 | async-start | bytes 8650752 | tf_op jit(solution)/shard_map/all_gather | solution.py:688
  87.5 251.7 %all-gather.14.cloned.1.call-start = ((), (), s32[]{:S(2)}) async-start(), calls=%async_computation.11 | async-start | bytes 17301504 | tf_op jit(solution)/shard_map/all_gather | solution.py:612
  185.6 6.7 copy-start.22
  190.3 2.0 copy-start.1
  192.3 6.8 copy-start.35
  195.0 69.0 %all-to-all-start.1 = ((bf16[8,128,256]{1,2,0:T(8,128)(2,1)}), bf16[8,128,256]{1,2,0:T(8,128)(2,1)}, u32[]{:S(2)}, u32[]{:S(2)}) async-start(bf16[8,128,256]{1,2,0:T(8,128)(2,1)} %copy.146), calls=%async_computation.1 | async-start | bytes 1048576 | tf_op jit(solution)/shard_map/all_to_all | solution.py:721
  264.0 6.2 copy-start.8
  269.0 1.0 copy-start.4
  270.2 0.8 copy-start.11
  600.5 6.7 copy-start
  606.2 1.0 copy-start.2
  612.9 21.5 %all-to-all-start.2 = ((bf16[8,128,256]{1,2,0:T(8,128)(2,1)}), bf16[8,128,256]{1,2,0:T(8,128)(2,1)}, u32[]{:S(2)}, u32[]{:S(2)}) async-start(bf16[8,128,256]{1,2,0:T(8,128)(2,1)} %bitcast.173), calls=%async_computation.2 | async-start | bytes 1048576 | tf_op jit(solution)/shard_map/all_to_all | solution.py:778
  618.9 116.8 %reduce-scatter.7.cloned.1.call-start = ((), (), s32[]{:S(2)}) async-start(), calls=%async_computation.12 | async-start | bytes 4718592 | tf_op jit(solution)/shard_map/reduce_scatter | solution.py:825
  638.6 4.8 copy-start.10
  638.6 4.8 copy-start.15
  638.6 5.0 copy-start.23
  643.6 4.9 copy-start.18
  643.6 4.9 copy-start.19
  648.5 2.0 copy-start.16
  648.5 2.0 copy-start.17
  650.6 1.4 copy-start.9
  650.6 1.4 copy-start.21
  680.0 3.2 copy-start.24
  680.0 3.2 copy-start.42
  682.2 0.8 copy-start.26
  682.2 1.0 copy-start.28
  688.2 1.0 copy-start.25
  688.2 1.2 copy-start.27
  688.2 1.4 copy-start.29
  688.2 8.9 copy-start.12
  688.2 47.5 %copy-start.31 = (f32[2048]{0:T(1024)S(1)}, f32[2048]{0:T(1024)}, u32[]{:S(2)}) copy-start(f32[2048]{0:T(1024)} %copy-done.30) | copy-start | bytes 24580
  688.2 47.5 %copy-start.33 = (f32[128]{0:T(128)S(1)}, f32[128]{0:T(128)}, u32[]{:S(2)}) copy-start(f32[128]{0:T(128)} %copy-done.32) | copy-start | bytes 1540
  688.2 93.0 %reduce-scatter.9.cloned.1.call-start = ((), (), s32[]{:S(2)}) async-start(), calls=%async_computation.13 | async-start | bytes 3932160 | tf_op jit(solution)/shard_map/reduce_scatter | solution.py:819
  697.0 38.7 %copy-start.6 = (bf16[1,128,2048]{2,1,0:T(8,128)(2,1)S(1)}, bf16[1,128,2048]{2,1,0:T(8,128)(2,1)}, u32[]{:S(2)}) copy-start(bf16[1,128,2048]{2,1,0:T(8,128)(2,1)} %param.16) | copy-start | bytes 1572868
  697.0 41.7 %copy-start.3 = (f32[128,2048]{1,0:T(8,128)S(1)}, f32[128,2048]{1,0:T(8,128)}, u32[]{:S(2)}) copy-start(f32[128,2048]{1,0:T(8,128)} %copy-done.2) | copy-start | bytes 3145732
  697.0 222.1 %reduce-scatter.13.cloned.1.call-start = ((), (), s32[]{:S(2)}) async-start(), calls=%async_computation.15 | async-start | bytes 1081344
  738.6 330.7 %reduce-scatter.11.cloned.1.call-start = ((), (), s32[]{:S(2)}) async-start(), calls=%async_computation.14 | async-start | bytes 8650752 | tf_op jit(solution)/shard_map/reduce_scatter | solution.py:773
  781.2 27.2 %all-to-all-start.3 = ((bf16[8,64,768]{2,1,0:T(8,128)(2,1)}), bf16[8,64,768]{2,1,0:T(8,128)(2,1)S(1)}, u32[]{:S(2)}, u32[]{:S(2)}) async-start(bf16[8,64,768]{2,1,0:T(8,128)(2,1)} %bitcast.186), calls=%async_computation.5 | async-start | bytes 1572864 | tf_op jit(solution)/shard_map/all_to_all | solution.py:821
  810.3 8.5 copy-start.20
  810.3 8.5 copy-start.36
  1071.1 4.8 copy-start.14
  1075.9 3.7 copy-start.13
Sparse Core Ops, SparseCore 0:
  41.7 43.5 all-gather.9
  87.4 46.9 all-gather.7
  137.4 85.9 all-gather.11
  226.2 112.9 all-gather.13
  688.3 47.3 reduce-scatter.6
  739.1 42.0 reduce-scatter.8
  783.5 135.6 reduce-scatter.12
  921.5 147.7 reduce-scatter.10

commit v3 on v2

--- a/solution.py
+++ b/solution.py
@@ -3,6 +3,7 @@
 
 import jax
 import jax.numpy as jnp
+import numpy as np
 from jax import lax
 from jax.experimental import pallas as pl
 from jax.experimental.pallas import tpu as pltpu
@@ -75,11 +76,17 @@
     c_ref,
     mask_ref,
     router_ref,
-    wgu_ref,
-    wd_ref,
+    gate_ref,
+    up_ref,
+    down_ref,
     xall,
     out_ref,
     back_ref,
+    dwg_out,
+    dwu_out,
+    dwd_out,
+    wgu_ref,
+    wd_ref,
     dwg_ref,
     dwu_ref,
     dwd_ref,
@@ -106,6 +113,7 @@
     rs_send,
     rs_recv,
     load_sem,
+    weight_sem,
 ):
     row, z, c = place()
     to = partners()
@@ -115,6 +123,24 @@
     me = row * 8 + z * 2 + c
     expert = me // 2
 
+    weights = [
+        pltpu.make_async_copy(src, dst, weight_sem.at[k])
+        for k, (src, dst) in enumerate(
+            (
+                (gate_ref, wgu_ref.at[:, pl.ds(0, hidden)]),
+                (up_ref, wgu_ref.at[:, pl.ds(hidden, hidden)]),
+                (down_ref, wd_ref),
+            )
+        )
+    ]
+    sums = [
+        pltpu.make_async_copy(src, dst, weight_sem.at[3 + k])
+        for k, (src, dst) in enumerate(
+            ((dwg_ref, dwg_out), (dwu_ref, dwu_out), (dwd_ref, dwd_out))
+        )
+    ]
+    for cp in weights:
+        cp.start()
     greet(list(to.values()))
 
     def ag(j, k, src, dst, who):
@@ -180,9 +206,7 @@
     def loads(j):
         return [
             pltpu.make_async_copy(xall.at[j], xbuf.at[j % 2], load_sem.at[0]),
-            pltpu.make_async_copy(
-                c_ref.at[:, :, :, j], cbuf.at[j % 2], load_sem.at[1]
-            ),
+            pltpu.make_async_copy(c_ref.at[j], cbuf.at[j % 2], load_sem.at[1]),
         ]
 
     def ag_done(j):
@@ -372,13 +396,15 @@
             gpart = cbuf[s, :, :, :, :, cols].reshape(every, cut)
             dwd_ref[:, cols] += dot_tn(hbuf[...], gpart)
 
-    dwg_ref[...] = jnp.zeros_like(dwg_ref)
-    dwu_ref[...] = jnp.zeros_like(dwu_ref)
-    dwd_ref[...] = jnp.zeros_like(dwd_ref)
     for j in range(3):
         ag_z(j)
     ag_xy(0)
     ag_xy(1)
+    dwg_ref[...] = jnp.zeros_like(dwg_ref)
+    dwu_ref[...] = jnp.zeros_like(dwu_ref)
+    dwd_ref[...] = jnp.zeros_like(dwd_ref)
+    for cp in weights:
+        cp.wait()
     ag_rel(0)
     ag_rel(1)
     ag_fin(0)
@@ -436,6 +462,11 @@
         def _():
             weight_grads(i)
 
+        @pl.when(i == steps - 1)
+        def _():
+            for cp in sums:
+                cp.start()
+
         @pl.when(i + 1 < steps)
         def _():
             ag_done(i + 1)
@@ -444,8 +475,11 @@
     def _(j):
         ag_sent(j)
 
-
-def moe(expert_in, upstream_all, mask, router, gate_up, down):
+    for cp in sums:
+        cp.wait()
+
+
+def moe(expert_in, upstream_all, mask, router, gate, up, down):
     tokens, width = expert_in.shape
     hidden = down.shape[0]
     steps = tokens // 16
@@ -464,9 +498,14 @@
             jax.ShapeDtypeStruct((width, hidden), f32),
             jax.ShapeDtypeStruct((hidden, width), f32),
         ),
-        in_specs=[any_, any_, vm, vm, vm, vm],
-        out_specs=(any_, vm, vm, vm, vm, vm),
+        in_specs=[any_, any_, vm, vm, any_, any_, any_],
+        out_specs=(any_, vm, vm, any_, any_, any_),
         scratch_shapes=[
+            pltpu.VMEM((width, 2 * hidden), bf16),
+            pltpu.VMEM((hidden, width), bf16),
+            pltpu.VMEM((width, hidden), f32),
+            pltpu.VMEM((width, hidden), f32),
+            pltpu.VMEM((hidden, width), f32),
             pltpu.VMEM((2, 4, 4, 2, 16, width), bf16),
             pltpu.VMEM((2, 4, 4, 2, 16, width), bf16),
             pltpu.VMEM((512, hidden), bf16),
@@ -490,6 +529,7 @@
             dma((2, 2, 8)),
             dma((2, 2, 8)),
             dma((6,)),
+            dma((6,)),
         ],
         compiler_params=pltpu.CompilerParams(
             collective_id=1, has_side_effects=True, vmem_limit_bytes=60 * 2**20
@@ -499,13 +539,1047 @@
         ),
     )(
         expert_in.reshape(steps, 16, width),
-        upstream_all.reshape(4, 4, 2, steps, 16, width),
+        upstream_all,
         mask,
         router,
-        gate_up,
+        gate,
+        up,
         down,
     )
     return results[1:]
+
+
+class Copies:
+    def __init__(self, send, recv):
+        self.send, self.recv, self.count, self.made = send, recv, 0, []
+
+    def __call__(self, src, dst, who):
+        k = self.count
+        self.count += 1
+        return remote(src, dst, self.send.at[k], self.recv.at[k], who)
+
+
+def row_mates():
+    row, z, c = place()
+    mates = [(row, z * 2 + (1 - c))]
+    for k in (1, 3, 2):
+        for flip in (0, 1):
+            mates.append((row, ((z + k) % 4) * 2 + (c ^ flip)))
+    return mates
+
+
+def gather_stages(copy, src, slots, cut, own_sem):
+    row, z, c = place()
+    to = partners()
+    own = slots.at[row, z, c]
+    line = slots.at[row, :, c]
+    width = src.shape[-1]
+    if cut:
+        a = slots.at[row ^ 1, :, c, :, pl.ds(0, cut)]
+        b = slots.at[row ^ 2, :, c, :, pl.ds(cut, width - cut)]
+    else:
+        a = slots.at[row ^ 1, pl.ds(0, 2), c]
+        b = slots.at[row ^ 2, pl.ds(2, 2), c]
+    s1, s2, s3 = (slots.at[row ^ k, :, c] for k in (1, 2, 3))
+    local = pltpu.make_async_copy(src, own, own_sem)
+    along_z = [copy(src, own, to["z%d" % k]) for k in (1, 3, 2)]
+    over = [copy(line, line, to[k]) for k in ("x", "y", "sib")]
+    relay = [copy(a, a, to["y"]), copy(b, b, to["x"])]
+    inside = [copy(s1, s1, to["sib"]), copy(s2, s2, to["sib"])]
+    last = [copy(s3, s3, to["sib"])]
+
+    def start(some):
+        for cp in some:
+            cp.start()
+
+    def arrived(some):
+        for cp in some:
+            cp.wait_recv()
+
+    def first():
+        local.start()
+        start(along_z)
+
+    def second():
+        local.wait()
+        arrived(along_z)
+        start(over)
+
+    def third():
+        arrived(over[:2])
+        start(relay + inside)
+
+    def fourth():
+        arrived(relay)
+        start(last)
+
+    def fifth():
+        arrived(over[2:] + inside + last)
+        for cp in along_z + over + relay + inside + last:
+            cp.wait_send()
+
+    return first, second, third, fourth, fifth
+
+
+def norm_rows(v):
+    return lax.rsqrt(jnp.mean(v * v, axis=-1, keepdims=True) + epsilon)
+
+
+def turned(v, cosine, sine):
+    heads = []
+    for h in range(v.shape[1] // HEAD_DIM):
+        one = v[:, h * HEAD_DIM : (h + 1) * HEAD_DIM]
+        heads.append(one * cosine + pltpu.roll(one, HEAD_DIM // 2, 1) * sine)
+    return jnp.concatenate(heads, axis=1)
+
+
+def row_pairs(cols):
+    row = lax.broadcasted_iota(jnp.int32, (8, 2 * cols), 0)
+    lane = lax.broadcasted_iota(jnp.int32, (8, 2 * cols), 1)
+    return jnp.where((lane // cols) == row, 1.0, 0.0).astype(f32)
+
+
+def sums_by_row(pairs, v):
+    return lax.dot_general(
+        pairs,
+        v,
+        (((1,), (1,)), ((), ())),
+        precision=lax.Precision.HIGHEST,
+        preferred_element_type=f32,
+    )
+
+
+def slot_stages(copy, src, slot, k, cut, own_sem):
+    row, z, c = place()
+    to = partners()
+    there = (z + k) % 4
+    own = slot(row, z)
+    s0, s1, s2, s3 = (slot(row ^ r, there) for r in range(4))
+    width = src.shape[-1]
+    a = slot(row ^ 1, there).at[:, :, pl.ds(0, cut)]
+    b = slot(row ^ 2, there).at[:, :, pl.ds(cut, width - cut)]
+    if k:
+        along_z = [copy(src, own, to["z%d" % (4 - k)])]
+        over = [copy(s0, s0, to[w]) for w in ("x", "y", "sib")]
+    else:
+        along_z = []
+        local = pltpu.make_async_copy(src, own, own_sem)
+        over = [copy(src, own, to[w]) for w in ("x", "y", "sib")]
+    relay = [copy(a, a, to["y"]), copy(b, b, to["x"])]
+    inside = [copy(s1, s1, to["sib"]), copy(s2, s2, to["sib"])]
+    last = [copy(s3, s3, to["sib"])]
+
+    def start(some):
+        for cp in some:
+            cp.start()
+
+    def arrived(some):
+        for cp in some:
+            cp.wait_recv()
+
+    def first():
+        if k:
+            start(along_z)
+        else:
+            local.start()
+
+    def second():
+        arrived(along_z)
+        start(over)
+
+    def third():
+        arrived(over[:2])
+        start(relay + inside)
+
+    def fourth():
+        arrived(relay)
+        start(last)
+
+    def fifth():
+        if not k:
+            local.wait()
+        arrived(over[2:] + inside + last)
+        for cp in along_z + over + relay + inside + last:
+            cp.wait_send()
+
+    return first, second, third, fourth, fifth
+
+
+def front_kernel(
+    h_ref,
+    wq_ref,
+    wk_ref,
+    wv_ref,
+    wo_ref,
+    up_ref,
+    pack_ref,
+    cos_ref,
+    sin_ref,
+    woall,
+    call,
+    packs,
+    normed_out,
+    wcols_out,
+    low_out,
+    pre_out,
+    att_out,
+    stat_ref,
+    home_ref,
+    mid_ref,
+    expert_ref,
+    hrow,
+    normed_ref,
+    wcols,
+    low_ref,
+    pre_ref,
+    att_ref,
+    wo_buf,
+    gains_ref,
+    sums_ref,
+    sums_land,
+    att_low,
+    send,
+    recv,
+    local_sem,
+):
+    row, z, c = place()
+    blk = z * 2 + c
+    to = partners()
+    mates = row_mates()
+    greet(mates + [to["x"], to["y"]])
+    copy = Copies(send, recv)
+    cols_here = wcols.shape[3] // 3
+    tokens, width = h_ref.shape
+    seq = 8 * tokens
+    wrows = wq_ref.shape[0]
+
+    pack_stages = gather_stages(copy, pack_ref, packs, 0, local_sem.at[0])
+    parts = up_ref.shape[0] // 4
+    streams = []
+    for k in (0, 1, 3, 2):
+        streams.append(
+            slot_stages(
+                copy,
+                wo_ref,
+                lambda r, q: woall.at[r, q, c],
+                k,
+                width // 2,
+                local_sem.at[9 + len(streams)],
+            )
+        )
+        for j in range(parts):
+            part = pl.ds(j * 4, 4)
+            streams.append(
+                slot_stages(
+                    copy,
+                    up_ref.at[part],
+                    lambda r, q, part=part: call.at[part, r, q, c],
+                    k,
+                    width // 2,
+                    local_sem.at[9 + len(streams)],
+                )
+            )
+    for_output = streams[:: parts + 1]
+    for_upstream = [one for one in streams if one not in for_output]
+    saves = [
+        pltpu.make_async_copy(src, dst, local_sem.at[9 + len(streams) + k])
+        for k, (src, dst) in enumerate(
+            (
+                (wcols, wcols_out),
+                (normed_ref, normed_out),
+                (pre_ref, pre_out),
+                (low_ref, low_out),
+                (att_ref, att_out),
+            )
+        )
+    ]
+    wo_load = pltpu.make_async_copy(woall, wo_buf, local_sem.at[9 + len(streams) + 5])
+    ticks = [0]
+
+    def tick():
+        t = ticks[0]
+        ticks[0] += 1
+        for stage, lag in ((0, 0), (1, 1), (2, 2), (3, 3)):
+            if 0 <= t - lag < len(streams):
+                streams[t - lag][stage]()
+
+    own_rows = pltpu.make_async_copy(h_ref, hrow.at[blk], local_sem.at[5])
+    up_to, down_to = (row, blk + 2), (row, blk - 2)
+    sib = to["sib"]
+    own_sib = copy(h_ref, hrow.at[blk], sib)
+    ups, downs = [], []
+    for t in range(3):
+        src = h_ref if t == 0 else hrow.at[blk - 2 * t]
+        up = copy(src, hrow.at[blk - 2 * t], up_to)
+        got = hrow.at[blk - 2 - 2 * t]
+        ups.append((up, copy(got, got, sib), (z < 3) & (z >= t), z >= t + 1))
+        src = h_ref if t == 0 else hrow.at[blk + 2 * t]
+        down = copy(src, hrow.at[blk + 2 * t], down_to)
+        got = hrow.at[blk + 2 + 2 * t]
+        downs.append((down, copy(got, got, sib), (z > 0) & (z + t <= 3), z + t + 1 <= 3))
+
+    def line_start(t):
+        for cp, hand, sends, gets in (ups[t], downs[t]):
+            pl.when(sends)(cp.start)
+
+    def line_arrived(t):
+        for cp, hand, sends, gets in (ups[t], downs[t]):
+
+            @pl.when(gets)
+            def _():
+                cp.wait_recv()
+                hand.start()
+
+    def line_done():
+        own_rows.wait()
+        own_sib.wait()
+        for t in range(3):
+            for cp, hand, sends, gets in (ups[t], downs[t]):
+                pl.when(sends)(cp.wait_send)
+                pl.when(gets)(hand.wait)
+
+    def columns(b):
+        return pl.ds(pl.multiple_of(b * cols_here, cols_here), cols_here)
+
+    own_cols, col_copies = [], []
+    for j, w in enumerate((wq_ref, wk_ref, wv_ref)):
+        there = pl.ds(j * cols_here, cols_here)
+        own_cols.append(
+            pltpu.make_async_copy(
+                w.at[:, columns(blk)], wcols.at[row, blk, :, there], local_sem.at[6 + j]
+            )
+        )
+        for mate in mates:
+            col_copies.append(
+                copy(w.at[:, columns(mate[1])], wcols.at[row, blk, :, there], mate)
+            )
+    half = wcols.shape[1] // 2
+    col_over = [copy(wcols.at[row], wcols.at[row], to[k]) for k in ("x", "y")]
+    a = wcols.at[row ^ 1, pl.ds(0, half)]
+    b = wcols.at[row ^ 2, pl.ds(half, half)]
+    col_relay = [copy(a, a, to["y"]), copy(b, b, to["x"])]
+    sum_copies = [
+        copy(sums_ref, sums_land.at[k], mate) for k, mate in enumerate(mates)
+    ]
+    home_copies = [
+        copy(att_low.at[mate[1]], home_ref.at[:, columns(blk)], mate) for mate in mates
+    ]
+
+    def start(some):
+        for cp in some:
+            cp.start()
+
+    def arrived(some):
+        for cp in some:
+            cp.wait_recv()
+
+    own_rows.start()
+    start(own_cols)
+    line_start(0)
+    own_sib.start()
+    tick()
+    tick()
+    pack_stages[0]()
+    start(col_copies)
+    tick()
+    pack_stages[1]()
+    tick()
+    line_arrived(0)
+    line_start(1)
+    tick()
+    pack_stages[2]()
+    for cp in own_cols:
+        cp.wait()
+    arrived(col_copies)
+    start(col_over)
+    pack_stages[3]()
+    line_arrived(1)
+    line_start(2)
+    tick()
+    arrived(col_over)
+    start(col_relay)
+    tick()
+    line_arrived(2)
+    pack_stages[4]()
+    arrived(col_relay)
+    line_done()
+    tick()
+    start(saves[:1])
+
+    pieces = []
+    for r in range(4):
+        for q in range(4):
+            pieces.append(
+                packs[r, q, 0, 48:64, :].astype(f32) + packs[r, q, 1, 48:64, :].astype(f32)
+            )
+    gains_ref[...] = jnp.concatenate(pieces, axis=1)[0:8]
+    gain_attn = gains_ref[0:1, :]
+    segments = jnp.concatenate(
+        [
+            packs[row, q, k, 16:32, :].astype(f32)[0:1]
+            for q in range(4)
+            for k in range(2)
+        ],
+        axis=1,
+    )
+    pairs = row_pairs(cols_here)
+    block = 256
+    blocks = seq // block
+
+    for t in range(blocks):
+        rows = slice(t * block, (t + 1) * block)
+        per = block // tokens
+        v = hrow[t * per : (t + 1) * per].reshape(block, width).astype(f32)
+        normed = (v * norm_rows(v) * gain_attn).astype(bf16)
+        normed_ref[rows, :] = normed
+        pre = dot(normed, wcols[...].reshape(width, 3 * cols_here))
+        pre_ref[rows, :] = pre[:, : 2 * cols_here]
+        low_ref[rows, 2 * cols_here :] = pre[:, 2 * cols_here :].astype(bf16)
+        both = pre[:, : 2 * cols_here]
+        squares = sums_by_row(pairs, both * both)
+        sums_ref[2 * t : 2 * t + 2, :] = squares[0:2]
+        if t % 2:
+            tick()
+    start(saves[1:3])
+    start(sum_copies)
+    tick()
+    total = sums_ref[...]
+    for k, cp in enumerate(sum_copies):
+        cp.wait_recv()
+        total = total + sums_land[k]
+    scales = lax.rsqrt(total * (1.0 / width) + epsilon)
+    gain_q = gains_ref[1:2, columns(blk)]
+    gain_k = gains_ref[2:3, columns(blk)]
+    for t in range(blocks):
+        rows = slice(t * block, (t + 1) * block)
+        turned_scales = jnp.concatenate(
+            [scales[2 * t : 2 * t + 2], segments[:, rows], jnp.zeros((5, block), f32)],
+            axis=0,
+        ).T
+        stat_ref[rows, :] = jnp.concatenate(
+            [turned_scales, jnp.zeros((block, 120), f32)], axis=1
+        )
+        cosine, sine = cos_ref[rows, :], sin_ref[rows, :]
+        q = pre_ref[rows, :cols_here] * turned_scales[:, 0:1] * gain_q
+        low_ref[rows, :cols_here] = turned(q, cosine, sine).astype(bf16)
+        k = pre_ref[rows, cols_here : 2 * cols_here] * turned_scales[:, 1:2] * gain_k
+        low_ref[rows, cols_here : 2 * cols_here] = turned(k, cosine, sine).astype(bf16)
+    tick()
+
+    for t in range(blocks):
+        rows = slice(t * block, (t + 1) * block)
+        keys = (t + 1) * block
+        stat = stat_ref[rows, :]
+        place_q = lax.broadcasted_iota(jnp.int32, (block, keys), 0) + t * block
+        place_k = lax.broadcasted_iota(jnp.int32, (block, keys), 1)
+        allowed = (place_k <= place_q) & (segments[:, :keys] == stat[:, 2:3])
+        lane = lax.broadcasted_iota(jnp.int32, stat.shape, 1)
+        for h in range(cols_here // HEAD_DIM):
+            cols = slice(h * HEAD_DIM, (h + 1) * HEAD_DIM)
+            q = low_ref[rows, cols]
+            k = low_ref[0:keys, cols_here + h * HEAD_DIM : cols_here + (h + 1) * HEAD_DIM]
+            v = low_ref[
+                0:keys, 2 * cols_here + h * HEAD_DIM : 2 * cols_here + (h + 1) * HEAD_DIM
+            ]
+            scores = jnp.where(allowed, dot_nt(q, k) * HEAD_DIM**-0.5, masked_score)
+            top = jnp.max(scores, axis=-1, keepdims=True)
+            raised = jnp.where(allowed, jnp.exp(scores - top), 0.0)
+            share = 1.0 / jnp.sum(raised, axis=-1, keepdims=True)
+            out = dot((raised * share).astype(bf16), v)
+            att_ref[rows, cols] = out
+            per = block // tokens
+            att_low[t * per : (t + 1) * per, :, cols] = out.astype(bf16).reshape(
+                per, tokens, HEAD_DIM
+            )
+            stat = jnp.where(lane == 3 + h, top, jnp.where(lane == 5 + h, share, stat))
+        stat_ref[rows, :] = stat
+        if t % 2:
+            tick()
+    start(saves[3:])
+    home_ref[:, columns(blk)] = att_low[blk]
+    start(home_copies)
+    tick()
+    while ticks[0] < len(streams) - parts + 3:
+        tick()
+    for stages in for_output:
+        stages[4]()
+    wo_load.start()
+    arrived(home_copies)
+    wo_load.wait()
+    mid = hrow[blk].astype(f32)
+    cut = 512
+    for n in range(width // cut):
+        cols = slice(n * cut, (n + 1) * cut)
+        mid_ref[:, cols] = mid[:, cols] + dot(
+            home_ref[...], wo_buf[:, :, :, :, :, cols].reshape(width, cut)
+        )
+    mid = mid_ref[...]
+    expert_ref[...] = (mid * norm_rows(mid) * gains_ref[3:4, :]).astype(bf16)
+    while ticks[0] < len(streams) + 3:
+        tick()
+    for stages in for_upstream:
+        stages[4]()
+    for cp in col_copies + col_over + col_relay + sum_copies + home_copies:
+        cp.wait_send()
+    for cp in saves:
+        cp.wait()
+
+
+def front(hidden, wq, wk, wv, wo, upstream, pack, cosine, sine):
+    any_, vm = pl.BlockSpec(memory_space=pl.ANY), pl.BlockSpec(memory_space=pltpu.VMEM)
+    tokens, width = hidden.shape
+    wrows = wq.shape[0]
+    seq, cols = 8 * tokens, width // 8
+    dma = pltpu.SemaphoreType.DMA
+    streams = 4 * (1 + tokens // 64)
+    count = 11 + 9 * streams + 13 + 21 + 4 + 14
+    shape = jax.ShapeDtypeStruct
+    return pl.pallas_call(
+        front_kernel,
+        out_shape=(
+            shape((4, 4, 2, wrows // 16, 16, width), bf16),
+            shape((tokens // 16, 4, 4, 2, 16, width), bf16),
+            shape((4, 4, 2) + pack.shape, bf16),
+            shape((seq, width), bf16),
+            shape((4, 8, wrows, 3 * cols), bf16),
+            shape((seq, 3 * cols), bf16),
+            shape((seq, 2 * cols), f32),
+            shape((seq, cols), f32),
+            shape((seq, 128), f32),
+            shape((tokens, width), bf16),
+            shape((tokens, width), f32),
+            shape((tokens, width), bf16),
+        ),
+        in_specs=[any_] * 7 + [vm] * 2,
+        out_specs=(any_, any_, vm) + (any_,) * 5 + (vm,) * 4,
+        scratch_shapes=[
+            pltpu.VMEM((8, tokens, width), bf16),
+            pltpu.VMEM((seq, width), bf16),
+            pltpu.VMEM((4, 8, wrows, 3 * cols), bf16),
+            pltpu.VMEM((seq, 3 * cols), bf16),
+            pltpu.VMEM((seq, 2 * cols), f32),
+            pltpu.VMEM((seq, cols), f32),
+            pltpu.VMEM((4, 4, 2, wrows // 16, 16, width), bf16),
+            pltpu.VMEM((8, width), f32),
+            pltpu.VMEM((8, seq // 4), f32),
+            pltpu.VMEM((7, 8, seq // 4), f32),
+            pltpu.VMEM((8, tokens, cols), bf16),
+            dma((count,)),
+            dma((count,)),
+            dma((16 + streams,)),
+        ],
+        compiler_params=pltpu.CompilerParams(
+            collective_id=2, has_side_effects=True, vmem_limit_bytes=56 * 2**20
+        ),
+        cost_estimate=pl.CostEstimate(
+            flops=10**10, bytes_accessed=2 * 10**8, transcendentals=0
+        ),
+    )(
+        hidden,
+        wq,
+        wk,
+        wv,
+        wo.reshape(-1, 16, width),
+        upstream.reshape(-1, 16, width),
+        pack,
+        cosine,
+        sine,
+    )
+
+
+def added(total, *extra):
+    total = total.astype(f32)
+    for one in extra:
+        total = total + one.astype(f32)
+    return total.astype(bf16)
+
+
+def reduce_stages(copy, src, got, p1a, p1b, p2, land, out):
+    row, z, c = place()
+    to = partners()
+    half = src.shape[-1] // 2
+
+    def own(r):
+        return src.at[r, :, c]
+
+    inside = copy(src.at[:, :, 1 - c], got, to["sib"])
+    far = [
+        copy(own(row ^ 3).at[:, :, pl.ds(0, half)], p1a, to["y"]),
+        copy(own(row ^ 3).at[:, :, pl.ds(half, half)], p1b, to["x"]),
+    ]
+    near = [
+        copy(own(row ^ 1), p2.at[0], to["x"]),
+        copy(own(row ^ 2), p2.at[1], to["y"]),
+    ]
+    home = [
+        copy(src.at[row, (z + k) % 4, c], land.at[k - 1], to["z%d" % k])
+        for k in (1, 3, 2)
+    ]
+
+    def first():
+        inside.start()
+
+    def second():
+        inside.wait_recv()
+        for k in (3, 1, 2, 0):
+            at = own(row ^ k)
+            at[...] = added(at[...], got[row ^ k])
+            if k == 3:
+                for cp in far:
+                    cp.start()
+
+    def third():
+        far[0].wait_recv()
+        at = own(row ^ 1).at[:, :, pl.ds(0, half)]
+        at[...] = added(at[...], p1a[...])
+        near[0].start()
+        far[1].wait_recv()
+        at = own(row ^ 2).at[:, :, pl.ds(half, half)]
+        at[...] = added(at[...], p1b[...])
+        near[1].start()
+
+    def fourth():
+        for cp in near:
+            cp.wait_recv()
+        at = own(row)
+        at[...] = added(at[...], p2[0], p2[1])
+        for cp in home:
+            cp.start()
+
+    def fifth():
+        for cp in home:
+            cp.wait_recv()
+        total = src[row, z, c].astype(f32)
+        for k in range(3):
+            total = total + land[k].astype(f32)
+        out[...] = total
+        for cp in [inside] + far + near + home:
+            cp.wait_send()
+
+    return first, second, third, fourth, fifth
+
+
+def back_kernel(
+    ga_home,
+    attended_ref,
+    proj_ref,
+    low_ref,
+    pre_ref,
+    att_ref,
+    stat_ref,
+    seg_ref,
+    gain_ref,
+    cos_ref,
+    sin_ref,
+    normed_in,
+    wcols_in,
+    small_ref,
+    gn_out,
+    q_out,
+    k_out,
+    v_out,
+    wo_out,
+    small_out,
+    normed_ref,
+    wcols,
+    ga,
+    dq_ref,
+    dk_ref,
+    dv_ref,
+    grads_ref,
+    sums_ref,
+    sums_land,
+    gn,
+    gn_sib,
+    gn_land,
+    gw,
+    gw_p1,
+    gw_p2,
+    gw_land,
+    small,
+    sm_sib,
+    sm_p1a,
+    sm_p1b,
+    sm_p2,
+    sm_land,
+    dwo_ref,
+    wo_got,
+    wo_p1a,
+    wo_p1b,
+    wo_p2,
+    wo_land,
+    send,
+    recv,
+    local_sem,
+):
+    row, z, c = place()
+    blk = z * 2 + c
+    to = partners()
+    mates = row_mates()
+    greet(mates + [to["x"], to["y"]])
+    copy = Copies(send, recv)
+    tokens, width = ga_home.shape
+    seq = 8 * tokens
+    cols_here = att_ref.shape[1]
+    wrows = wo_out.shape[0]
+    scale = HEAD_DIM**-0.5
+    block = 256
+    blocks = seq // block
+    per = block // tokens
+
+    def start(some):
+        for cp in some:
+            cp.start()
+
+    def arrived(some):
+        for cp in some:
+            cp.wait_recv()
+
+    def columns(b):
+        return pl.ds(pl.multiple_of(b * cols_here, cols_here), cols_here)
+
+    streams = []
+    for j in range(wrows // 16):
+        part = pl.ds(j * 16, 16)
+        streams.append(
+            reduce_stages(
+                copy,
+                dwo_ref.at[:, :, :, part],
+                wo_got.at[j],
+                wo_p1a.at[j],
+                wo_p1b.at[j],
+                wo_p2.at[j],
+                wo_land.at[j],
+                wo_out.at[part],
+            )
+        )
+    ticks = [0]
+
+    def tick():
+        t = ticks[0]
+        ticks[0] += 1
+        for stage in range(5):
+            if 0 <= t - stage < len(streams):
+                streams[t - stage][stage]()
+
+    own_ga = pltpu.make_async_copy(
+        ga_home.at[:, columns(blk)], ga.at[blk], local_sem.at[0]
+    )
+    ga_copies = [copy(ga_home.at[:, columns(mate[1])], ga.at[blk], mate) for mate in mates]
+    sum_copies = [
+        copy(sums_ref, sums_land.at[k], mate) for k, mate in enumerate(mates)
+    ]
+    half = gw.shape[1] // 2
+    w_far = [
+        copy(gw.at[row ^ 3, pl.ds(0, half)], gw_p1.at[0], to["y"]),
+        copy(gw.at[row ^ 3, pl.ds(half, half)], gw_p1.at[1], to["x"]),
+    ]
+    w_near = [
+        copy(gw.at[row ^ 1], gw_p2.at[0], to["x"]),
+        copy(gw.at[row ^ 2], gw_p2.at[1], to["y"]),
+    ]
+    w_home = [copy(gw.at[row, mate[1]], gw_land.at[blk], mate) for mate in mates]
+    d0, d1 = 3 - z, (3 * z + 2) % 5
+    d2 = 3 - d1
+    inner, outer = (z == 1) | (z == 2), (z == 0) | (z == 3)
+    n_sib = [
+        copy(gn.at[chip, 1 - c], gn_sib.at[chip], to["sib"]) for chip in (d0, d1, d2, z)
+    ]
+    n_relay = copy(gn.at[d0, c], gn_land.at[0], (row, (1 + z // 2) * 2 + c))
+    n_inner = copy(gn.at[d0, c], gn_land.at[1], (row, (2 - z // 2) * 2 + c))
+    n_home = [
+        copy(gn.at[d1, c], gn_land.at[2], (row, d1 * 2 + c)),
+        copy(gn.at[d2, c], gn_land.at[3], (row, d2 * 2 + c)),
+    ]
+    s_sib = copy(small.at[0], sm_sib, to["sib"])
+    s_far = [
+        copy(small.at[1, row ^ 3, 0:2], sm_p1a, to["y"]),
+        copy(small.at[1, row ^ 3, 2:4], sm_p1b, to["x"]),
+    ]
+    s_near = [
+        copy(small.at[1, row ^ 1], sm_p2.at[0], to["x"]),
+        copy(small.at[1, row ^ 2], sm_p2.at[1], to["y"]),
+    ]
+    s_home = [
+        copy(small.at[1, row, (z + k) % 4], sm_land.at[k - 1], to["z%d" % k])
+        for k in (1, 3, 2)
+    ]
+
+    late = [
+        pltpu.make_async_copy(src, dst, local_sem.at[1 + len(streams) + k])
+        for k, (src, dst) in enumerate(
+            ((normed_in, normed_ref), (wcols_in, wcols))
+        )
+    ]
+    own_ga.start()
+    start(ga_copies)
+    start(late)
+
+    @pl.loop(0, 8)
+    def _(n):
+        some = attended_ref[:, pl.ds(pl.multiple_of(n * block, block), block)]
+        made = dot_tn(some, proj_ref[...]).astype(bf16)
+        dwo_ref[n // 2, pl.ds(2 * (n % 2), 2)] = made.reshape(2, 2, wrows, width)
+
+    tick()
+    dk_ref[...] = jnp.zeros_like(dk_ref)
+    dv_ref[...] = jnp.zeros_like(dv_ref)
+    small[0] = small_ref[...]
+    own_ga.wait()
+    arrived(ga_copies)
+
+    segments = seg_ref[0:1, :]
+    for t in range(blocks):
+        rows = slice(t * block, (t + 1) * block)
+        keys = (t + 1) * block
+        stat = stat_ref[rows, :]
+        place_q = lax.broadcasted_iota(jnp.int32, (block, keys), 0) + t * block
+        place_k = lax.broadcasted_iota(jnp.int32, (block, keys), 1)
+        allowed = (place_k <= place_q) & (segments[:, :keys] == stat[:, 2:3])
+        for h in range(cols_here // HEAD_DIM):
+            cols = slice(h * HEAD_DIM, (h + 1) * HEAD_DIM)
+            q = low_ref[rows, cols]
+            k = low_ref[0:keys, cols_here + h * HEAD_DIM : cols_here + (h + 1) * HEAD_DIM]
+            v = low_ref[
+                0:keys, 2 * cols_here + h * HEAD_DIM : 2 * cols_here + (h + 1) * HEAD_DIM
+            ]
+            g = ga[t * per : (t + 1) * per, :, cols].reshape(block, HEAD_DIM)
+            scores = jnp.where(allowed, dot_nt(q, k) * scale, masked_score)
+            raised = jnp.exp(scores - stat[:, 3 + h : 4 + h])
+            probs = jnp.where(allowed, raised, 0.0) * stat[:, 5 + h : 6 + h]
+            delta = jnp.sum(g.astype(f32) * att_ref[rows, cols], axis=-1, keepdims=True)
+            ds = (probs * (dot_nt(g, v) - delta)).astype(bf16)
+            dq_ref[rows, cols] = dot(ds, k) * scale
+            dk_ref[0:keys, cols] += dot_tn(ds, q) * scale
+            dv_ref[0:keys, cols] += dot_tn(probs.astype(bf16), g)
+        tick()
+
+    pairs = row_pairs(cols_here)
+    gain_q, gain_k = gain_ref[0:1, :], gain_ref[1:2, :]
+    for_q = jnp.zeros((1, cols_here), f32)
+    for_k = jnp.zeros((1, cols_here), f32)
+    for t in range(blocks):
+        rows = slice(t * block, (t + 1) * block)
+        cosine, sine = cos_ref[rows, :], -sin_ref[rows, :]
+        q_pre, k_pre = pre_ref[rows, :cols_here], pre_ref[rows, cols_here:]
+        dq = turned(dq_ref[rows, :], cosine, sine)
+        dk = turned(dk_ref[rows, :], cosine, sine)
+        dq_ref[rows, :] = dq
+        dk_ref[rows, :] = dk
+        vq, vk = dq * q_pre, dk * k_pre
+        for_q = for_q + jnp.sum(vq * stat_ref[rows, 0:1], axis=0, keepdims=True)
+        for_k = for_k + jnp.sum(vk * stat_ref[rows, 1:2], axis=0, keepdims=True)
+        sums = sums_by_row(pairs, jnp.concatenate([vq * gain_q, vk * gain_k], axis=1))
+        sums_ref[2 * t : 2 * t + 2, :] = sums[0:2]
+    start(sum_copies)
+    tick()
+    total = sums_ref[...]
+    for k, cp in enumerate(sum_copies):
+        cp.wait_recv()
+        total = total + sums_land[k]
+    means = total * (1.0 / width)
+    for t in range(blocks):
+        rows = slice(t * block, (t + 1) * block)
+        mean = jnp.concatenate(
+            [means[2 * t : 2 * t + 2], jnp.zeros((6, block), f32)], axis=0
+        ).T
+        for j, (d_ref, gain) in enumerate(((dq_ref, gain_q), (dk_ref, gain_k))):
+            cols = slice(j * cols_here, (j + 1) * cols_here)
+            r = stat_ref[rows, j : j + 1]
+            grads_ref[rows, cols] = (
+                r * gain * d_ref[rows, :]
+                - pre_ref[rows, cols] * (r * r * r) * mean[:, j : j + 1]
+            ).astype(bf16)
+        grads_ref[rows, 2 * cols_here :] = dv_ref[rows, :].astype(bf16)
+
+    deep = 8 * wrows
+    for cp in late:
+        cp.wait()
+
+    def weight_rows(k):
+        there = row ^ k
+        some = normed_ref[:, pl.ds(pl.multiple_of(there * deep, deep), deep)]
+        gw[there] = (
+            dot_tn(some, grads_ref[...]).astype(bf16).reshape(8, wrows, 3 * cols_here)
+        )
+
+    weight_rows(3)
+    start(w_far)
+    weights = wcols[...].reshape(width, 3 * cols_here)
+    for_attn = jnp.zeros((1, width), f32)
+    chips = (d0, d1, d2, z)
+    for n, chip in enumerate(chips):
+        tok = pl.ds(pl.multiple_of(chip * block, block), block)
+        made = dot_nt(grads_ref[tok, :], weights)
+        gn[chip] = made.astype(bf16).reshape(per, tokens, width)
+        n_sib[n].start()
+        for_attn = for_attn + jnp.sum(
+            made * normed_ref[tok, :].astype(f32), axis=0, keepdims=True
+        )
+        if n:
+            before = chips[n - 1]
+            n_sib[n - 1].wait_recv()
+            n_sib[n - 1].wait_send()
+            gn[before, c] = added(gn[before, c], gn_sib[before])
+            if n == 1:
+                pl.when(outer)(n_relay.start)
+                pl.when(inner)(n_inner.start)
+            elif n == 2:
+                n_home[0].start()
+    weight_rows(1)
+    weight_rows(2)
+
+    @pl.when(inner)
+    def _():
+        n_relay.wait_recv()
+        gn[d2, c] = added(gn[d2, c], gn_land[0])
+
+    n_home[1].start()
+    weight_rows(0)
+    tick()
+    for r in range(4):
+        for q in range(4):
+            at = (r * 4 + q) * 128
+            small[0, r, q, 16:17, :] = for_attn[:, at : at + 128]
+    for j in range(cols_here // 128):
+        at = blk * (cols_here // 128) + j
+        small[0, at // 4, at % 4, 17:18, :] = for_q[:, j * 128 : (j + 1) * 128]
+        small[0, at // 4, at % 4, 18:19, :] = for_k[:, j * 128 : (j + 1) * 128]
+    s_sib.start()
+
+    arrived(w_far[:1])
+    gw[row ^ 1, 0:half] = added(gw[row ^ 1, 0:half], gw_p1[0])
+    w_near[0].start()
+    arrived(w_far[1:])
+    gw[row ^ 2, half:] = added(gw[row ^ 2, half:], gw_p1[1])
+    w_near[1].start()
+    s_sib.wait_recv()
+    small[1] = small[0] + sm_sib[...]
+    start(s_far)
+    tick()
+    arrived(s_far)
+    small[1, row ^ 1, 0:2] = small[1, row ^ 1, 0:2] + sm_p1a[...]
+    small[1, row ^ 2, 2:4] = small[1, row ^ 2, 2:4] + sm_p1b[...]
+    start(s_near)
+    arrived(w_near)
+    for b in range(8):
+        gw[row, b] = added(gw[row, b], gw_p2[0, b], gw_p2[1, b])
+    start(w_home)
+    arrived(s_near)
+    small[1, row] = small[1, row] + sm_p2[0] + sm_p2[1]
+    start(s_home)
+    while ticks[0] < len(streams) + 4:
+        tick()
+
+    n_sib[3].wait_recv()
+    gn_out[...] = gn[z, c].astype(f32) + gn_sib[z].astype(f32)
+    arrived(n_home)
+    gn_out[...] += gn_land[2].astype(f32) + gn_land[3].astype(f32)
+
+    @pl.when(inner)
+    def _():
+        n_inner.wait_recv()
+        n_inner.wait_send()
+        gn_out[...] += gn_land[1].astype(f32)
+
+    @pl.when(outer)
+    def _():
+        n_relay.wait_send()
+
+    arrived(s_home)
+    small_out[...] = small[1, row, z] + sm_land[0] + sm_land[1] + sm_land[2]
+    gw_land[blk] = gw[row, blk]
+    arrived(w_home)
+    for b in range(8):
+        for j, out in enumerate((q_out, k_out, v_out)):
+            out[:, b * cols_here : (b + 1) * cols_here] = gw_land[
+                b, :, j * cols_here : (j + 1) * cols_here
+            ].astype(f32)
+    n_sib[3].wait_send()
+    for cp in ga_copies + sum_copies + w_far + w_near + w_home + n_home:
+        cp.wait_send()
+    for cp in [s_sib] + s_far + s_near + s_home:
+        cp.wait_send()
+
+
+def back(ga, att_low, proj, low, pre, att, stat, seg, gain, cosine, sine, normed, wcols, small):
+    any_, vm = pl.BlockSpec(memory_space=pl.ANY), pl.BlockSpec(memory_space=pltpu.VMEM)
+    tokens, width = ga.shape
+    seq, cols = 8 * tokens, width // 8
+    wrows = wcols.shape[2]
+    fields = small.shape[2:]
+    dma = pltpu.SemaphoreType.DMA
+    streams = wrows // 16
+    count = 8 * streams + 7 + 7 + 2 + 2 + 7 + 4 + 4 + 1 + 2 + 2 + 3
+    shape, vmem = jax.ShapeDtypeStruct, pltpu.VMEM
+    weight = shape((wrows, width), f32)
+    return pl.pallas_call(
+        back_kernel,
+        out_shape=(
+            shape((tokens, width), f32),
+            weight,
+            weight,
+            weight,
+            weight,
+            shape(fields, f32),
+        ),
+        in_specs=[any_] + [vm] * 10 + [any_] * 2 + [vm],
+        out_specs=(vm,) * 6,
+        scratch_shapes=[
+            vmem((seq, width), bf16),
+            vmem((4, 8, wrows, 3 * cols), bf16),
+            vmem((8, tokens, cols), bf16),
+            vmem((seq, cols), f32),
+            vmem((seq, cols), f32),
+            vmem((seq, cols), f32),
+            vmem((seq, 3 * cols), bf16),
+            vmem((8, seq // 4), f32),
+            vmem((7, 8, seq // 4), f32),
+            vmem((4, 2, tokens, width), bf16),
+            vmem((4, tokens, width), bf16),
+            vmem((4, tokens, width), bf16),
+            vmem((4, 8, wrows, 3 * cols), bf16),
+            vmem((2, 4, wrows, 3 * cols), bf16),
+            vmem((2, 8, wrows, 3 * cols), bf16),
+            vmem((8, wrows, 3 * cols), bf16),
+            vmem((2, 4, 4) + fields, f32),
+            vmem((4, 4) + fields, f32),
+            vmem((2,) + fields, f32),
+            vmem((2,) + fields, f32),
+            vmem((2, 4) + fields, f32),
+            vmem((3,) + fields, f32),
+            vmem((4, 4, 2, wrows, width), bf16),
+            vmem((streams, 4, 4, 16, width), bf16),
+            vmem((streams, 4, 16, width // 2), bf16),
+            vmem((streams, 4, 16, width // 2), bf16),
+            vmem((streams, 2, 4, 16, width), bf16),
+            vmem((streams, 3, 16, width), bf16),
+            dma((count,)),
+            dma((count,)),
+            dma((4 + streams,)),
+        ],
+        compiler_params=pltpu.CompilerParams(
+            collective_id=7, has_side_effects=True, vmem_limit_bytes=60 * 2**20
+        ),
+        cost_estimate=pl.CostEstimate(
+            flops=10**10, bytes_accessed=2 * 10**8, transcendentals=0
+        ),
+    )(
+        ga,
+        att_low,
+        proj,
+        low,
+        pre,
+        att,
+        stat,
+        seg,
+        gain,
+        cosine,
+        sine,
+        normed,
+        wcols,
+        small,
+    )
 
 
 def rope_tables(count):
@@ -514,7 +1588,7 @@
         -math.log(10000.0) * 2.0 * jnp.arange(half, dtype=f32) / HEAD_DIM
     )
     angles = jnp.arange(count, dtype=f32)[:, None] * frequency[None, :]
-    return jnp.cos(angles)[:, None, :], jnp.sin(angles)[:, None, :]
+    return jnp.cos(angles), jnp.sin(angles)
 
 
 def rope(values, cosine, sine):
@@ -603,29 +1677,197 @@
     return outs.astype(f32), backs.astype(f32), grad_gates, sums
 
 
-def experts_in_kernel(
-    expert_in, upstream, routed, router, gate_local, up_local, down_local
+def own_mesh_body(
+    hidden_in,
+    segment_ids,
+    expert_ids,
+    attention_gain,
+    query_gain,
+    key_gain,
+    expert_gain,
+    query_weight,
+    key_weight,
+    value_weight,
+    output_weight,
+    router_weight,
+    gate_weight,
+    up_weight,
+    down_weight,
+    grad_out,
 ):
-    tokens, width = expert_in.shape
-    experts = router.shape[1]
+    tokens, width = hidden_in.shape[1:]
+    wrows = query_weight.shape[0]
+    experts = router_weight.shape[1]
+    blocks = lax.axis_size("blk")
+    seq = tokens * blocks
+    head_cols = width // blocks
+    blk = lax.axis_index("blk")
+    upstream_low = grad_out[0]
+
+    experts_in_order = jnp.arange(experts, dtype=jnp.int32)
+    routed = jnp.any(
+        expert_ids[0][:, :, None] == experts_in_order[None, None, :], axis=1
+    )
+    routed_t = jnp.any(
+        expert_ids[0].T[None, :, :] == experts_in_order[:, None, None], axis=1
+    )
+    gains = jnp.stack([attention_gain, query_gain, key_gain, expert_gain])
+    spare = tokens - wrows
+    gains = jnp.concatenate([gains, gains], axis=1)
+    lane = jnp.arange(2 * wrows, dtype=jnp.int32)[None]
+    gains = jnp.where(lane // wrows == blk % 2, gains, 0)
+
+    def rows_at(first, values, lanes):
+        return jnp.pad(values.astype(f32), ((first, 64 - first - values.shape[0]), (0, lanes)))
+
+    pack = (
+        rows_at(0, routed_t, 0)
+        + rows_at(16, segment_ids, 0)
+        + rows_at(32, router_weight.T, spare)
+        + rows_at(32 + experts, gains, 0)
+    ).astype(bf16)
+    half = HEAD_DIM // 2
+    frequency = np.exp(-math.log(10000.0) * 2.0 * np.arange(half) / HEAD_DIM)
+    angles = np.arange(seq)[:, None] * frequency.astype(np.float32)[None, :]
+    angles = angles.astype(np.float32)
+    cosine, sine = np.cos(angles), np.sin(angles)
+    cosine = jnp.asarray(np.concatenate([cosine, cosine], axis=1), f32)
+    sine = jnp.asarray(np.concatenate([-sine, sine], axis=1), f32)
+    (
+        full_output,
+        upstream_all,
+        packs,
+        normed_row,
+        qkv_cols,
+        low,
+        pre,
+        attended,
+        stats,
+        attended_low,
+        residual_mid,
+        expert_in,
+    ) = front(
+        hidden_in[0],
+        query_weight,
+        key_weight,
+        value_weight,
+        output_weight,
+        upstream_low,
+        pack,
+        cosine,
+        sine,
+    )
+    full_output = full_output.reshape(width, width)
+    packs = packs.reshape(-1, pack.shape[0], tokens)
+    router = packs[:, 32 : 32 + experts, :wrows].transpose(0, 2, 1).reshape(width, -1)
+    gains = packs[:, 32 + experts : 36 + experts].reshape(-1, 2, 4, tokens).sum(axis=1)
+    gains = gains.transpose(1, 0, 2).reshape(4, width).astype(f32)
+    gain_attn, gain_expert = gains[0], gains[3]
+    own_q_gain = lax.dynamic_slice_in_dim(gains[1], blk * head_cols, head_cols)
+    own_k_gain = lax.dynamic_slice_in_dim(gains[2], blk * head_cols, head_cols)
     steps = tokens // 16
-    upstream_all = lax.all_gather(upstream, BOTH, axis=0, tiled=False)
-    mask = lax.all_gather(routed.astype(bf16), BOTH, axis=0, tiled=False).astype(f32)
-    mask = mask.reshape(-1, steps, 16, experts).transpose(1, 0, 2, 3)
-    mask = mask.reshape(steps, -1, experts)
-    gate_up = jnp.concatenate([gate_local, up_local], axis=1)
-    outs, backs, *sums = moe(
-        expert_in, upstream_all, mask, router, gate_up, down_local
+    mask = packs[:, :experts].astype(f32).reshape(-1, experts, steps, 16)
+    mask = mask.transpose(2, 0, 3, 1).reshape(steps, -1, experts)
+    x = hidden_in[0].astype(f32)
+    r_attn = lax.rsqrt(jnp.mean(x * x, axis=-1, keepdims=True) + epsilon)
+    r_exp = lax.rsqrt(
+        jnp.mean(residual_mid * residual_mid, axis=-1, keepdims=True) + epsilon
+    )
+    logits = dot(expert_in, router)
+    top_logit = jnp.max(
+        jnp.where(routed, logits, masked_score), axis=-1, keepdims=True
+    )
+    gates = jnp.where(routed, jnp.exp(logits - top_logit), 0.0)
+    gates = gates / jnp.sum(gates, axis=-1, keepdims=True)
+
+    outs, backs, grad_gate_local, grad_up_local, grad_down_local = moe(
+        expert_in,
+        upstream_all,
+        mask,
+        router,
+        gate_weight[0],
+        up_weight[0],
+        down_weight[0],
     )
     outs = outs.reshape(tokens, width)
     backs = backs.reshape(tokens, width + EXTRA)
     dots = backs[:, width : width + 2 * experts]
     dots = dots + backs[:, width + 64 : width + 64 + 2 * experts]
     grad_gates = jnp.sum(dots.reshape(tokens, experts, 2), axis=2)
-    return outs, backs[:, :width], grad_gates, sums
-
-
-def body(
+    layer_out = (residual_mid + outs).astype(bf16)
+    upstream = upstream_low.astype(f32)
+    grad_picked = gates * (
+        grad_gates - jnp.sum(gates * grad_gates, axis=-1, keepdims=True)
+    )
+    grad_logits = jnp.where(routed, grad_picked, 0.0).astype(bf16)
+    grad_expert_in = backs[:, :width] + dot_nt(grad_logits, router)
+    grad_router = dot_tn(grad_logits, expert_in)
+    grad_gain_expert = jnp.sum(grad_expert_in * residual_mid * r_exp, axis=0)
+    grad_mid = upstream + norm_back(
+        residual_mid,
+        r_exp,
+        gain_expert,
+        grad_expert_in,
+        jnp.mean(residual_mid * gain_expert * grad_expert_in, axis=-1, keepdims=True),
+    )
+    grad_proj = grad_mid.astype(bf16)
+    grad_attended = dot_nt(grad_proj, full_output).astype(bf16)
+    small = jnp.concatenate(
+        [
+            grad_router,
+            jnp.zeros((3, width), f32),
+            grad_gain_expert[None],
+            jnp.zeros((20 - experts, width), f32),
+        ],
+        axis=0,
+    )
+    fields = small.shape[0]
+    small = small.reshape(fields, 4, 4, 2 * wrows).transpose(1, 2, 0, 3)
+    grad_normed, grad_q, grad_k, grad_v, grad_output_w, small = back(
+        grad_attended,
+        attended_low,
+        grad_proj,
+        low,
+        pre,
+        attended,
+        stats,
+        jnp.broadcast_to(stats[:, 2][None], (8, seq)),
+        jnp.concatenate(
+            [own_q_gain[None], own_k_gain[None], jnp.zeros((6, head_cols), f32)], axis=0
+        ),
+        cosine,
+        sine,
+        normed_row,
+        qkv_cols,
+        small,
+    )
+    input_grad = grad_mid + norm_back(
+        x,
+        r_attn,
+        gain_attn,
+        grad_normed,
+        jnp.mean(x * gain_attn * grad_normed, axis=-1, keepdims=True),
+    )
+    small = lax.dynamic_slice_in_dim(small, (blk % 2) * wrows, wrows, axis=1)
+    return (
+        layer_out[None],
+        input_grad[None],
+        small[experts] / attention_gain.astype(f32),
+        small[experts + 1],
+        small[experts + 2],
+        small[experts + 3],
+        grad_q,
+        grad_k,
+        grad_v,
+        grad_output_w,
+        small[:experts].T,
+        grad_gate_local[None],
+        grad_up_local[None],
+        grad_down_local[None],
+    )
+
+
+def any_mesh_body(
     hidden_in,
     segment_ids,
     expert_ids,
@@ -697,7 +1939,7 @@
     squares = lax.psum(squares, "blk") / width
     r_q = lax.rsqrt(squares[0] + epsilon)[:, None]
     r_k = lax.rsqrt(squares[1] + epsilon)[:, None]
-    cosine, sine = rope_tables(seq)
+    cosine, sine = (table[:, None] for table in rope_tables(seq))
 
     def heads(v):
         return v.reshape(seq, heads_here, HEAD_DIM)
@@ -741,14 +1983,9 @@
     gates = gates / jnp.sum(gates, axis=-1, keepdims=True)
 
     gate_local, up_local, down_local = gate_weight[0], up_weight[0], down_weight[0]
-    if (rows, blocks, 2 * experts, heads_here) == (4, 8, 32, 2):
-        outs, backs, grad_gates, sums = experts_in_kernel(
-            expert_in, grad_out[0], routed, router, gate_local, up_local, down_local
-        )
-    else:
-        outs, backs, grad_gates, sums = experts_by_scan(
-            expert_in, grad_out[0], gates, gate_local, up_local, down_local
-        )
+    outs, backs, grad_gates, sums = experts_by_scan(
+        expert_in, grad_out[0], gates, gate_local, up_local, down_local
+    )
     grad_gate_local, grad_up_local, grad_down_local = sums
     layer_out = (residual_mid + outs).astype(bf16)
     upstream = grad_out[0].astype(f32)
@@ -871,8 +2108,9 @@
 def solution(mesh):
     tokens3 = P("row", "blk", None)
     vector, matrix, cube = P(BOTH), P(BOTH, None), P(BOTH, None, None)
+    own = (mesh.shape["row"], mesh.shape["blk"]) == (4, 8)
     return jax.shard_map(
-        body,
+        own_mesh_body if own else any_mesh_body,
         mesh=mesh,
         in_specs=(
             tokens3,

time: 1100 us -> 604 us (0.55)
  waiting for transfers between devices: 459 us -> 0 us
  Pallas kernels: 260 us -> 549 us
  blocking collectives: 159 us -> 0 us
  local copies, waits for them, and re-layouts: 74.5 us -> 21 us
  matrix products: 62.2 us -> 9.54 us
  other arithmetic: 43.1 us -> 14.6 us
  starting transfers between devices: 15.6 us -> 0 us
  between operations: 15.3 us -> 1.32 us
    pallas_call x0 -> x2, Pallas kernels: none -> 289 us  [the longest x1 167 us: front(): pl.pallas_call(front_kernel, out_shape=(shape((4, 4, 2, wrows // 16, 16,...]
    reduce_scatter x3 -> x0, waiting for transfers between devices: 220 us -> none  [the longest x1 145 us: body(): lax.psum_scatter(grad_output_w, BOTH, scatter_dimension=0, tiled=True)]
    all_gather x3 -> x0, blocking collectives: 102 us -> none  [the longest x1 52.8 us: experts_in_kernel(): lax.all_gather(routed.astype(bf16), BOTH, axis=0, tiled=False).astype(f32)]
    all_gather x4 -> x0, waiting for transfers between devices: 101 us -> none  [the longest x1 68.2 us: experts_in_kernel(): upstream_all = lax.all_gather(upstream, BOTH, axis=0, tiled=False)]
    unnamed x9 -> x0, waiting for transfers between devices: 100 us -> none
    all_to_all x3 -> x0, waiting for transfers between devices: 37.8 us -> none  [the longest x1 22.6 us: body(): lax.all_to_all(grad_w, 'blk', split_axis=0, concat_axis=0, tiled=True)]
    psum x2 -> x0, blocking collectives: 29.9 us -> none  [the longest x1 15.1 us: body(): squares = lax.psum(squares, 'blk') / width]
    all_to_all x1 -> x0, blocking collectives: 27.2 us -> none  [body(): lax.all_to_all(stacked, 'blk', split_axis=0, concat_axis=0, tiled=True)]
  transfers between devices with their start and end apart: 11 -> 0, of which waited for: 8 -> 0; matrix products, arithmetic and copies ran while one was open for 9% -> 0% of each run, Pallas kernels for 0% -> 0%
where the time goes in v3:
time: 604 us; the launch traced here: 595 us
  Pallas kernels  549 us (91%)
  local copies, waits for them, and re-layouts  21 us (3%)
  other arithmetic  14.6 us (2%)
  matrix products  9.54 us (2%)
    pallas_call x1, Pallas kernels, moe(): pl.pallas_call(functools.partial(moe_kernel, steps), out_shape=(jax.Shape...  260 us
    pallas_call x1, Pallas kernels, front(): pl.pallas_call(front_kernel, out_shape=(shape((4, 4, 2, wrows // 16, 16,...  167 us
    pallas_call x1, Pallas kernels, back(): pl.pallas_call(back_kernel, out_shape=(shape((tokens, width), f32), weigh...  122 us
    unnamed x43, local copies, waits for them, and re-layouts  13.2 us

profile of v3, /device:TPU:0, one launch (start us, length us, event | category | flops | bytes accessed | tf_op | source)
XLA Modules:
  0.0 595.4 jit_solution(11769235936229547912)
XLA Ops:
  0.6 0.7 convert_element_type.58
  1.3 0.7 fusion.8
  2.0 0.9 maximum_select_fusion
  2.9 1.3 add_convert_fusion.pack_ref
  4.2 166.8 %shard_map.281 = (bf16[4,4,2,4,16,2048]{5,4,3,2,1,0:T(8,128)(2,1)}, bf16[8,4,4,2,16,2048]{5,4,3,2,1,0:T(8,128)(2,1)}, bf16[4,4,2,64,128]{4,3,2,1,0:T(8,128)(2,1)...) custom-call(bf16[128,2048]{1,0:T(8,128)(2,1)} %bitcast.87, ...), custom_call_target="tpu_custom_call" | custom-call | flops 10000000000 | bytes 200000000 | tf_op jit(solution)/shard_map/pallas_call | solution.py:1037
  171.0 1.4 multiply_reduce_fusion.2
  172.4 0.9 bitcast_reduce_fusion
  173.3 0.0 copy-done.14
  173.3 0.9 slice.74
  174.3 0.3 copy.51
  174.6 0.1 convert_bitcast_fusion
  174.7 2.4 copy.47
  177.0 0.9 slice.75
  178.0 0.3 copy.52
  178.2 0.9 pad.36.router_ref
  179.1 259.7 %shard_map.282 = (bf16[8,4,4,2,16,2048]{5,4,3,2,1,0:T(8,128)(2,1)}, f32[8,16,2048]{2,1,0:T(8,128)}, f32[8,16,2176]{2,1,0:T(8,128)}, f32[2048,512]{1,0:T(8,128)},...) custom-call(bf16[8,16,2048]{2,1,0:T(8,128)(2,1)} %bitcast.86, bf16[8,4,4,2,16,2048]{5,4,3,2,1,0:T(8,128)(2,1)} %get-tuple-element.39.c_ref, ...), custom_call_target="tpu_custom_call" | custom-call | flops 77999996928 | bytes 100000000 | tf_op jit(solution)/shard_map/pallas_call | solution.py:491
  438.9 0.0 copy-start.8
  438.9 1.0 slice_add_fusion
  439.9 0.1 copy.49
  440.0 0.0 copy-done.5
  440.0 0.0 copy-start.7
  440.0 0.3 select_reduce_fusion
  440.4 0.0 copy-done
  440.4 1.8 multiply_reduce_fusion
  442.2 0.0 copy-done.8
  442.2 0.0 copy-done.7
  442.2 1.2 fusion.14
  443.5 7.3 %convolution_convert_fusion.ga_home = bf16[128,2048]{1,0:T(8,128)(2,1)} fusion(bf16[128,2048]{1,0:T(8,128)(2,1)S(1)} %get-tuple-element.64.proj_ref, bf16[2048,2048]{1,0:T(8,128)(2,1)} %bitcast.77), kind=kOutput, calls=%fused_computation.1 | convolution fusion | flops 1074003968 | bytes 9437184 | tf_op jit(solution)/shard_map/dot_general | solution.py:30
  450.8 0.0 copy-done.4
  450.8 0.0 copy-done.9
  450.8 0.4 slice_reduce_fusion
  451.2 0.6 broadcast_in_dim.71.seg_ref
  451.8 0.1 pad.43.clone
  451.9 0.7 maximum_maximum_fusion.gain_ref
  452.5 0.2 fusion.16
  452.7 0.1 concatenate.16
  452.9 0.1 pad.40.clone
  453.0 0.1 pad.38.clone
  453.0 0.8 maximum_bitcast_fusion.small_ref
  453.8 122.4 %shard_map.283 = (f32[128,2048]{1,0:T(8,128)}, f32[64,2048]{1,0:T(8,128)}, f32[64,2048]{1,0:T(8,128)}, f32[64,2048]{1,0:T(8,128)}, f32[64,2048]{1,0:T(8,128)}, /*index=5*/f32[24,128]{1,0:T(8,128)}) custom-call(bf16[128,2048]{1,0:T(8,128)(2,1)} %convolution_convert_fusion.ga_home, bf16[128,2048]{1,0:T(8,128)(2,1)} %get-tuple-element.44.attended_ref, ...), custom_call_target="tpu_custom_call" | custom-call | flops 10000000000 | bytes 200000000 | tf_op jit(solution)/shard_map/pallas_call | solution.py:1516
  576.3 0.0 copy-start.15
  576.3 0.0 copy-start.16
  576.3 0.0 copy-start.13
  576.3 0.0 copy-start.12
  576.3 0.0 copy-start.11
  576.3 0.0 copy-done.6
  576.3 0.0 copy-start.10
  576.3 1.7 fusion
  578.0 2.6 fusion.4
  580.6 0.0 copy-done.15
  580.6 0.6 fusion.13
  581.2 0.6 dynamic-slice_bitcast_fusion.1
  581.8 0.7 dynamic-slice_bitcast_fusion
  582.4 0.8 copy.60
  583.2 0.8 copy.61
  584.0 0.8 copy.62
  584.8 0.0 copy-done.10
  584.8 0.8 copy.63
  585.6 0.0 copy-done.3
  585.6 2.1 copy.64
  587.7 1.6 copy-done.2
  589.3 2.1 copy.65
  591.5 1.6 copy-done.1
  593.0 2.0 copy.66
  (30 shorter events, 0.3 us)
Async XLA Ops:
  4.2 169.1 %copy-start.14 = (s32[1,128,8]{1,2,0:T(8,128)S(1)}, s32[1,128,8]{1,2,0:T(8,128)}, u32[]{:S(2)}) copy-start(s32[1,128,8]{1,2,0:T(8,128)} %param.20) | copy-start | bytes 12292
  179.1 260.9 %copy-start.5 = (bf16[128,2048]{1,0:T(8,128)(2,1)S(1)}, bf16[128,2048]{1,0:T(8,128)(2,1)}, u32[]{:S(2)}) copy-start(bf16[128,2048]{1,0:T(8,128)(2,1)} %get-tuple-element.38) | copy-start | bytes 1572868
  179.1 261.3 %copy-start = (f32[128,2048]{1,0:T(8,128)S(1)}, f32[128,2048]{1,0:T(8,128)}, u32[]{:S(2)}) copy-start(f32[128,2048]{1,0:T(8,128)} %get-tuple-element.37) | copy-start | bytes 3145732
  438.9 3.3 copy-start.8
  440.0 2.2 copy-start.7
  443.5 7.3 %copy-start.4 = (bf16[128,2048]{1,0:T(8,128)(2,1)}, bf16[128,2048]{1,0:T(8,128)(2,1)S(1)}, u32[]{:S(2)}) copy-start(bf16[128,2048]{1,0:T(8,128)(2,1)S(1)} %get-tuple-element.64.proj_ref) | copy-start | bytes 1572868
  443.5 7.3 %copy-start.9 = (f32[1024,128]{1,0:T(8,128)S(1)}, f32[1024,128]{1,0:T(8,128)}, u32[]{:S(2)}) copy-start(f32[1024,128]{1,0:T(8,128)} %get-tuple-element.48.stat_ref) | copy-start | bytes 1572868
  453.8 122.5 %copy-start.6 = (bf16[1,128,2048]{2,1,0:T(8,128)(2,1)S(1)}, bf16[1,128,2048]{2,1,0:T(8,128)(2,1)}, u32[]{:S(2)}) copy-start(bf16[1,128,2048]{2,1,0:T(8,128)(2,1)} %param.18) | copy-start | bytes 1572868
  576.3 4.3 copy-start.15
  576.3 4.3 copy-start.16
  576.3 6.2 %copy-start.13 = (f32[64,2048]{1,0:T(8,128)S(1)}, f32[64,2048]{1,0:T(8,128)}, u32[]{:S(2)}) copy-start(f32[64,2048]{1,0:T(8,128)} %get-tuple-element.103) | copy-start | bytes 1572868
  576.3 6.9 %copy-start.12 = (f32[64,2048]{1,0:T(8,128)S(1)}, f32[64,2048]{1,0:T(8,128)}, u32[]{:S(2)}) copy-start(f32[64,2048]{1,0:T(8,128)} %get-tuple-element.104) | copy-start | bytes 1572868
  576.3 7.7 %copy-start.11 = (f32[64,2048]{1,0:T(8,128)S(1)}, f32[64,2048]{1,0:T(8,128)}, u32[]{:S(2)}) copy-start(f32[64,2048]{1,0:T(8,128)} %get-tuple-element.105) | copy-start | bytes 1572868
  576.3 8.5 %copy-start.10 = (f32[64,2048]{1,0:T(8,128)S(1)}, f32[64,2048]{1,0:T(8,128)}, u32[]{:S(2)}) copy-start(f32[64,2048]{1,0:T(8,128)} %get-tuple-element.106) | copy-start | bytes 1572868
  581.2 4.5 copy-start.3
  585.6 3.7 copy-start.2
  589.3 3.7 copy-start.1

commit v4 on v3

--- a/solution.py
+++ b/solution.py
@@ -3,7 +3,6 @@
 
 import jax
 import jax.numpy as jnp
-import numpy as np
 from jax import lax
 from jax.experimental import pallas as pl
 from jax.experimental.pallas import tpu as pltpu
@@ -20,6 +19,7 @@
 bf16 = jnp.bfloat16
 f32 = jnp.float32
 EXTRA = 128
+ZCOLS = 256
 
 
 def dot(a, b):
@@ -108,6 +108,9 @@
     p2b,
     zo,
     zb,
+    gz,
+    gp1,
+    gp2,
     ag_send,
     ag_recv,
     rs_send,
@@ -224,6 +227,8 @@
         (po, ro, so, p1ao, p1bo, p2o, zo, out_ref),
         (pb, rb, sb, p1ab, p1bb, p2b, zb, back_ref),
     )
+    near_z, near_cut = ZCOLS, ZCOLS // 2
+    mid = near_z + p1ao.shape[-1]
 
     def rs(i, q, k, src, dst, who):
         s = i % 2
@@ -236,33 +241,64 @@
     def p1_copies(q, i):
         p, r, s, p1a, p1b, p2, zz, out = arrays[q]
         part = s.at[i % 2, row ^ 3]
-        rest = p.shape[-1] - half
+        rest = p.shape[-1] - mid
         return [
-            rs(i, q, 1, part.at[:, :, pl.ds(0, half)], p1a.at[i % 2], "y"),
-            rs(i, q, 2, part.at[:, :, pl.ds(half, rest)], p1b.at[i % 2], "x"),
+            rs(i, q, 1, part.at[:, :, pl.ds(near_z, mid - near_z)], p1a.at[i % 2], "y"),
+            rs(i, q, 2, part.at[:, :, pl.ds(mid, rest)], p1b.at[i % 2], "x"),
         ]
 
     def p2_copies(q, i):
         p, r, s, p1a, p1b, p2, zz, out = arrays[q]
+        cols = pl.ds(near_z, p.shape[-1] - near_z)
         return [
-            rs(i, q, 3, s.at[i % 2, row ^ 1], p2.at[i % 2, 0], "x"),
-            rs(i, q, 4, s.at[i % 2, row ^ 2], p2.at[i % 2, 1], "y"),
+            rs(i, q, 3, s.at[i % 2, row ^ 1, :, :, cols], p2.at[i % 2, 0], "x"),
+            rs(i, q, 4, s.at[i % 2, row ^ 2, :, :, cols], p2.at[i % 2, 1], "y"),
         ]
 
     def rsz_copies(q, i):
         p, r, s, p1a, p1b, p2, zz, out = arrays[q]
+        cols = pl.ds(near_z, p.shape[-1] - near_z)
         return [
             rs(
                 i,
                 q,
                 5 + k,
-                s.at[i % 2, row, (z + k + 1) % 4],
+                s.at[i % 2, row, (z + k + 1) % 4, :, cols],
                 zz.at[i % 2, k],
                 "z%d" % (k + 1),
             )
             for k in range(3)
         ]
 
+    def first_z_copies(q, i):
+        s = arrays[q][2]
+        return [
+            rs(
+                i,
+                q,
+                8 + k,
+                s.at[i % 2, :, (z + k + 1) % 4, :, pl.ds(0, near_z)],
+                gz.at[q, i % 2, k],
+                "z%d" % (k + 1),
+            )
+            for k in range(3)
+        ]
+
+    def first_p1_copies(q, i):
+        part = arrays[q][2].at[i % 2, row ^ 3, z]
+        return [
+            rs(i, q, 11, part.at[:, pl.ds(0, near_cut)], gp1.at[q, i % 2, 0], "y"),
+            rs(i, q, 12, part.at[:, pl.ds(near_cut, near_cut)], gp1.at[q, i % 2, 1], "x"),
+        ]
+
+    def first_p2_copies(q, i):
+        s = arrays[q][2]
+        cols = pl.ds(0, near_z)
+        return [
+            rs(i, q, 13, s.at[i % 2, row ^ 1, z, :, cols], gp2.at[q, i % 2, 0], "x"),
+            rs(i, q, 14, s.at[i % 2, row ^ 2, z, :, cols], gp2.at[q, i % 2, 1], "y"),
+        ]
+
     def rs_sib(q, i):
         rs_sib_copy(q, i).start()
 
@@ -278,37 +314,44 @@
             ).astype(bf16)
 
         cp.wait_send()
-        for cp in p1_copies(q, i):
+        for cp in p1_copies(q, i) + first_z_copies(q, i):
             cp.start()
 
     def rs_p2(q, i):
         p, r, s, p1a, p1b, p2, zz, out = arrays[q]
-        rest = p.shape[-1] - half
+        rest = p.shape[-1] - mid
         copies = p1_copies(q, i)
         copies[0].wait_recv()
-        at = s.at[i % 2, row ^ 1]
-        at[:, :, pl.ds(0, half)] = (
-            at[:, :, pl.ds(0, half)].astype(f32) + p1a[i % 2].astype(f32)
-        ).astype(bf16)
+        at = s.at[i % 2, row ^ 1, :, :, pl.ds(near_z, mid - near_z)]
+        at[...] = added(at[...], p1a[i % 2])
         out_copies = p2_copies(q, i)
         out_copies[0].start()
         copies[1].wait_recv()
-        at = s.at[i % 2, row ^ 2]
-        at[:, :, pl.ds(half, rest)] = (
-            at[:, :, pl.ds(half, rest)].astype(f32) + p1b[i % 2].astype(f32)
-        ).astype(bf16)
+        at = s.at[i % 2, row ^ 2, :, :, pl.ds(mid, rest)]
+        at[...] = added(at[...], p1b[i % 2])
         out_copies[1].start()
+        for cp in first_z_copies(q, i):
+            cp.wait_recv()
+        at = s.at[i % 2, :, z, :, pl.ds(0, near_z)]
+        at[...] = added(at[...], gz[q, i % 2, 0], gz[q, i % 2, 1], gz[q, i % 2, 2])
+        for cp in first_p1_copies(q, i):
+            cp.start()
 
     def rs_z(q, i):
         p, r, s, p1a, p1b, p2, zz, out = arrays[q]
         for cp in p2_copies(q, i):
             cp.wait_recv()
-        s[i % 2, row] = (
-            s[i % 2, row].astype(f32)
-            + p2[i % 2, 0].astype(f32)
-            + p2[i % 2, 1].astype(f32)
-        ).astype(bf16)
+        at = s.at[i % 2, row, :, :, pl.ds(near_z, p.shape[-1] - near_z)]
+        at[...] = added(at[...], p2[i % 2, 0], p2[i % 2, 1])
         for cp in rsz_copies(q, i):
+            cp.start()
+        for cp in first_p1_copies(q, i):
+            cp.wait_recv()
+        at = s.at[i % 2, row ^ 1, z, :, pl.ds(0, near_cut)]
+        at[...] = added(at[...], gp1[q, i % 2, 0])
+        at = s.at[i % 2, row ^ 2, z, :, pl.ds(near_cut, near_cut)]
+        at[...] = added(at[...], gp1[q, i % 2, 1])
+        for cp in first_p2_copies(q, i):
             cp.start()
 
     def rs_fin(q, i):
@@ -316,11 +359,20 @@
         copies = rsz_copies(q, i)
         for cp in copies:
             cp.wait_recv()
-        total = s[i % 2, row, z].astype(f32)
+        total = s[i % 2, row, z, :, near_z:].astype(f32)
         for k in range(3):
             total = total + zz[i % 2, k].astype(f32)
-        out[i] = total
+        out[i, :, near_z:] = total
+        first = first_p2_copies(q, i)
+        for cp in first:
+            cp.wait_recv()
+        total = s[i % 2, row, z, :, :near_z].astype(f32)
+        for k in range(2):
+            total = total + gp2[q, i % 2, k].astype(f32)
+        out[i, :, :near_z] = total
         for cp in copies + p2_copies(q, i) + p1_copies(q, i):
+            cp.wait_send()
+        for cp in first + first_p1_copies(q, i) + first_z_copies(q, i):
             cp.wait_send()
 
     lanes = po.shape[3]
@@ -484,7 +536,7 @@
     hidden = down.shape[0]
     steps = tokens // 16
     wide = width + EXTRA
-    half = width // 2
+    mid = ZCOLS + (width - ZCOLS) // 2
     any_, vm = pl.BlockSpec(memory_space=pl.ANY), pl.BlockSpec(memory_space=pltpu.VMEM)
     dma = pltpu.SemaphoreType.DMA
     router = jnp.pad(router, ((0, 0), (0, 128 - router.shape[1])))
@@ -516,18 +568,21 @@
             pltpu.VMEM((2, 4, 4, 16, wide), bf16),
             pltpu.VMEM((2, 4, 4, 16, width), bf16),
             pltpu.VMEM((2, 4, 4, 16, wide), bf16),
-            pltpu.VMEM((2, 4, 16, half), bf16),
-            pltpu.VMEM((2, 4, 16, half), bf16),
-            pltpu.VMEM((2, 4, 16, half), bf16),
-            pltpu.VMEM((2, 4, 16, wide - half), bf16),
-            pltpu.VMEM((2, 2, 4, 16, width), bf16),
-            pltpu.VMEM((2, 2, 4, 16, wide), bf16),
-            pltpu.VMEM((2, 3, 16, width), bf16),
-            pltpu.VMEM((2, 3, 16, wide), bf16),
+            pltpu.VMEM((2, 4, 16, mid - ZCOLS), bf16),
+            pltpu.VMEM((2, 4, 16, width - mid), bf16),
+            pltpu.VMEM((2, 4, 16, mid - ZCOLS), bf16),
+            pltpu.VMEM((2, 4, 16, wide - mid), bf16),
+            pltpu.VMEM((2, 2, 4, 16, width - ZCOLS), bf16),
+            pltpu.VMEM((2, 2, 4, 16, wide - ZCOLS), bf16),
+            pltpu.VMEM((2, 3, 16, width - ZCOLS), bf16),
+            pltpu.VMEM((2, 3, 16, wide - ZCOLS), bf16),
+            pltpu.VMEM((2, 2, 3, 4, 16, ZCOLS), bf16),
+            pltpu.VMEM((2, 2, 2, 16, ZCOLS // 2), bf16),
+            pltpu.VMEM((2, 2, 2, 16, ZCOLS), bf16),
             dma((steps, 11)),
             dma((steps, 11)),
-            dma((2, 2, 8)),
-            dma((2, 2, 8)),
+            dma((2, 2, 15)),
+            dma((2, 2, 15)),
             dma((6,)),
             dma((6,)),
         ],
@@ -1726,13 +1781,9 @@
         + rows_at(32, router_weight.T, spare)
         + rows_at(32 + experts, gains, 0)
     ).astype(bf16)
-    half = HEAD_DIM // 2
-    frequency = np.exp(-math.log(10000.0) * 2.0 * np.arange(half) / HEAD_DIM)
-    angles = np.arange(seq)[:, None] * frequency.astype(np.float32)[None, :]
-    angles = angles.astype(np.float32)
-    cosine, sine = np.cos(angles), np.sin(angles)
-    cosine = jnp.asarray(np.concatenate([cosine, cosine], axis=1), f32)
-    sine = jnp.asarray(np.concatenate([-sine, sine], axis=1), f32)
+    cosine, sine = rope_tables(seq)
+    cosine = jnp.concatenate([cosine, cosine], axis=1)
+    sine = jnp.concatenate([-sine, sine], axis=1)
     (
         full_output,
         upstream_all,

time: 604 us -> 593 us (0.982)
  Pallas kernels: 549 us -> 534 us
    pallas_call x1, Pallas kernels: 260 us -> 246 us  [moe(): pl.pallas_call(functools.partial(moe_kernel, steps), out_shape=(jax.Shape...]
where the time goes in v4:
time: 593 us; the launch traced here: 584 us
  Pallas kernels  534 us (90%)
  local copies, waits for them, and re-layouts  21 us (4%)
  other arithmetic  17.8 us (3%)
  matrix products  9.54 us (2%)
    pallas_call x1, Pallas kernels, moe(): pl.pallas_call(functools.partial(moe_kernel, steps), out_shape=(jax.Shape...  246 us
    pallas_call x1, Pallas kernels, front(): pl.pallas_call(front_kernel, out_shape=(shape((4, 4, 2, wrows // 16, 16,...  167 us
    pallas_call x1, Pallas kernels, back(): pl.pallas_call(back_kernel, out_shape=(shape((tokens, width), f32), weigh...  121 us
    unnamed x43, local copies, waits for them, and re-layouts  13.2 us

profile of v4, /device:TPU:0, one launch (start us, length us, event | category | flops | bytes accessed | tf_op | source)
XLA Modules:
  0.0 584.1 jit_solution(13382515076338680240)
XLA Ops:
  0.6 0.7 convert_element_type.58
  1.3 0.7 fusion.11
  2.0 0.9 maximum_select_fusion
  2.9 1.3 add_convert_fusion.pack_ref
  4.2 2.0 fusion.10
  6.2 1.3 pad_maximum_fusion
  7.5 166.8 %shard_map.263 = (bf16[4,4,2,4,16,2048]{5,4,3,2,1,0:T(8,128)(2,1)}, bf16[8,4,4,2,16,2048]{5,4,3,2,1,0:T(8,128)(2,1)}, bf16[4,4,2,64,128]{4,3,2,1,0:T(8,128)(2,1)...) custom-call(bf16[128,2048]{1,0:T(8,128)(2,1)} %bitcast.87, ...), custom_call_target="tpu_custom_call" | custom-call | flops 10000000000 | bytes 200000000 | tf_op jit(solution)/shard_map/pallas_call | solution.py:1092
  174.3 1.4 multiply_reduce_fusion.2
  175.7 0.9 bitcast_reduce_fusion
  176.6 0.0 copy-done.14
  176.6 0.9 slice.74
  177.5 0.3 copy.49
  177.8 0.1 convert_bitcast_fusion
  178.0 2.4 copy.45
  180.3 0.9 slice.75
  181.2 0.3 copy.50
  181.5 0.9 pad.36.router_ref
  182.4 246.5 %shard_map.264 = (bf16[8,4,4,2,16,2048]{5,4,3,2,1,0:T(8,128)(2,1)}, f32[8,16,2048]{2,1,0:T(8,128)}, f32[8,16,2176]{2,1,0:T(8,128)}, f32[2048,512]{1,0:T(8,128)},...) custom-call(bf16[8,16,2048]{2,1,0:T(8,128)(2,1)} %bitcast.86, bf16[8,4,4,2,16,2048]{5,4,3,2,1,0:T(8,128)(2,1)} %get-tuple-element.39.c_ref, ...), custom_call_target="tpu_custom_call" | custom-call | flops 77999996928 | bytes 100000000 | tf_op jit(solution)/shard_map/pallas_call | solution.py:543
  428.9 0.0 copy-start.8
  428.9 1.0 slice_add_fusion
  429.9 0.1 copy.47
  430.0 0.0 copy-done.5
  430.0 0.0 copy-start.7
  430.1 0.3 select_reduce_fusion
  430.4 0.0 copy-done
  430.5 1.8 multiply_reduce_fusion
  432.2 0.0 copy-done.8
  432.2 0.0 copy-done.7
  432.2 1.2 fusion.17
  433.5 7.3 %convolution_convert_fusion.ga_home = bf16[128,2048]{1,0:T(8,128)(2,1)} fusion(bf16[128,2048]{1,0:T(8,128)(2,1)S(1)} %get-tuple-element.64.proj_ref, bf16[2048,2048]{1,0:T(8,128)(2,1)} %bitcast.77), kind=kOutput, calls=%fused_computation.1 | convolution fusion | flops 1074003968 | bytes 9437184 | tf_op jit(solution)/shard_map/dot_general | solution.py:30
  440.8 0.0 copy-done.4
  440.8 0.0 copy-done.9
  440.8 0.4 slice_reduce_fusion
  441.2 0.6 broadcast_in_dim.73.seg_ref
  441.8 0.1 pad.43.clone
  441.9 0.7 maximum_maximum_fusion.gain_ref
  442.5 0.2 fusion.19
  442.7 0.1 concatenate.24
  442.9 0.1 pad.40.clone
  443.0 0.1 pad.38.clone
  443.1 0.8 maximum_bitcast_fusion.small_ref
  443.8 121.1 %shard_map.265 = (f32[128,2048]{1,0:T(8,128)}, f32[64,2048]{1,0:T(8,128)}, f32[64,2048]{1,0:T(8,128)}, f32[64,2048]{1,0:T(8,128)}, f32[64,2048]{1,0:T(8,128)}, /*index=5*/f32[24,128]{1,0:T(8,128)}) custom-call(bf16[128,2048]{1,0:T(8,128)(2,1)} %convolution_convert_fusion.ga_home, bf16[128,2048]{1,0:T(8,128)(2,1)} %get-tuple-element.44.attended_ref, ...), custom_call_target="tpu_custom_call" | custom-call | flops 10000000000 | bytes 200000000 | tf_op jit(solution)/shard_map/pallas_call | solution.py:1571
  564.9 0.0 copy-start.15
  564.9 0.0 copy-start.16
  564.9 0.0 copy-start.13
  564.9 0.0 copy-start.12
  564.9 0.0 copy-start.11
  564.9 0.0 copy-done.6
  565.0 1.7 fusion
  566.6 2.6 fusion.4
  569.2 0.0 copy-done.15
  569.2 0.6 fusion.16
  569.8 0.6 dynamic-slice_bitcast_fusion.1
  570.4 0.7 dynamic-slice_bitcast_fusion
  571.1 0.8 copy.58
  571.9 0.8 copy.59
  572.7 0.8 copy.60
  573.4 0.0 copy-done.10
  573.4 0.8 copy.61
  574.2 2.1 copy.62
  576.4 1.6 copy-done.2
  578.0 2.1 copy.63
  580.1 1.6 copy-done.1
  581.7 2.0 copy.64
  (34 shorter events, 0.3 us)
Async XLA Ops:
  7.5 169.1 %copy-start.14 = (s32[1,128,8]{1,2,0:T(8,128)S(1)}, s32[1,128,8]{1,2,0:T(8,128)}, u32[]{:S(2)}) copy-start(s32[1,128,8]{1,2,0:T(8,128)} %param.18) | copy-start | bytes 12292
  182.4 247.6 %copy-start.5 = (bf16[128,2048]{1,0:T(8,128)(2,1)S(1)}, bf16[128,2048]{1,0:T(8,128)(2,1)}, u32[]{:S(2)}) copy-start(bf16[128,2048]{1,0:T(8,128)(2,1)} %get-tuple-element.38) | copy-start | bytes 1572868
  182.4 248.0 %copy-start = (f32[128,2048]{1,0:T(8,128)S(1)}, f32[128,2048]{1,0:T(8,128)}, u32[]{:S(2)}) copy-start(f32[128,2048]{1,0:T(8,128)} %get-tuple-element.37) | copy-start | bytes 3145732
  428.9 3.3 copy-start.8
  430.0 2.2 copy-start.7
  433.5 7.3 %copy-start.4 = (bf16[128,2048]{1,0:T(8,128)(2,1)}, bf16[128,2048]{1,0:T(8,128)(2,1)S(1)}, u32[]{:S(2)}) copy-start(bf16[128,2048]{1,0:T(8,128)(2,1)S(1)} %get-tuple-element.64.proj_ref) | copy-start | bytes 1572868
  433.5 7.3 %copy-start.9 = (f32[1024,128]{1,0:T(8,128)S(1)}, f32[1024,128]{1,0:T(8,128)}, u32[]{:S(2)}) copy-start(f32[1024,128]{1,0:T(8,128)} %get-tuple-element.48.stat_ref) | copy-start | bytes 1572868
  443.8 121.1 %copy-start.6 = (bf16[1,128,2048]{2,1,0:T(8,128)(2,1)S(1)}, bf16[1,128,2048]{2,1,0:T(8,128)(2,1)}, u32[]{:S(2)}) copy-start(bf16[1,128,2048]{2,1,0:T(8,128)(2,1)} %param.16) | copy-start | bytes 1572868
  564.9 4.3 copy-start.15
  564.9 4.3 copy-start.16
  564.9 6.2 %copy-start.13 = (f32[64,2048]{1,0:T(8,128)S(1)}, f32[64,2048]{1,0:T(8,128)}, u32[]{:S(2)}) copy-start(f32[64,2048]{1,0:T(8,128)} %get-tuple-element.106) | copy-start | bytes 1572868
  564.9 6.9 %copy-start.12 = (f32[64,2048]{1,0:T(8,128)S(1)}, f32[64,2048]{1,0:T(8,128)}, u32[]{:S(2)}) copy-start(f32[64,2048]{1,0:T(8,128)} %get-tuple-element.107) | copy-start | bytes 1572868
  564.9 7.7 %copy-start.11 = (f32[64,2048]{1,0:T(8,128)S(1)}, f32[64,2048]{1,0:T(8,128)}, u32[]{:S(2)}) copy-start(f32[64,2048]{1,0:T(8,128)} %get-tuple-element.108) | copy-start | bytes 1572868
  564.9 8.5 %copy-start.10 = (f32[64,2048]{1,0:T(8,128)S(1)}, f32[64,2048]{1,0:T(8,128)}, u32[]{:S(2)}) copy-start(f32[64,2048]{1,0:T(8,128)} %get-tuple-element.109) | copy-start | bytes 1572868
  569.8 4.5 copy-start.3
  574.2 3.7 copy-start.2
  577.9 3.7 copy-start.1

commit v5 on v4

--- a/solution.py
+++ b/solution.py
@@ -382,7 +382,7 @@
     def tile(i, t):
         s = i % 2
         xt = xbuf[s, 2 * t : 2 * t + 2].reshape(rows_here, width)
-        mask = mask_ref[i, t * rows_here : (t + 1) * rows_here, :]
+        mask = mask_ref[i, t * rows_here : (t + 1) * rows_here, :].astype(f32)
         logits = dot(xt, router_ref[...])[:, : mask.shape[-1]]
         logits = jnp.where(mask > 0, logits, masked_score)
         top = jnp.max(logits, axis=-1, keepdims=True)
@@ -448,18 +448,19 @@
             gpart = cbuf[s, :, :, :, :, cols].reshape(every, cut)
             dwd_ref[:, cols] += dot_tn(hbuf[...], gpart)
 
-    for j in range(3):
-        ag_z(j)
-    ag_xy(0)
-    ag_xy(1)
+    ag_z(0)
+    ag_z(1)
     dwg_ref[...] = jnp.zeros_like(dwg_ref)
     dwu_ref[...] = jnp.zeros_like(dwu_ref)
     dwd_ref[...] = jnp.zeros_like(dwd_ref)
     for cp in weights:
         cp.wait()
+    ag_xy(0)
+    ag_z(2)
+    ag_xy(1)
     ag_rel(0)
+    ag_fin(0)
     ag_rel(1)
-    ag_fin(0)
     ag_done(0)
     ag_fin(1)
 
@@ -1381,6 +1382,7 @@
     dv_ref[...] = jnp.zeros_like(dv_ref)
     small[0] = small_ref[...]
     own_ga.wait()
+    tick()
     arrived(ga_copies)
 
     segments = seg_ref[0:1, :]
@@ -1817,7 +1819,7 @@
     own_q_gain = lax.dynamic_slice_in_dim(gains[1], blk * head_cols, head_cols)
     own_k_gain = lax.dynamic_slice_in_dim(gains[2], blk * head_cols, head_cols)
     steps = tokens // 16
-    mask = packs[:, :experts].astype(f32).reshape(-1, experts, steps, 16)
+    mask = packs[:, :experts].reshape(-1, experts, steps, 16)
     mask = mask.transpose(2, 0, 3, 1).reshape(steps, -1, experts)
     x = hidden_in[0].astype(f32)
     r_attn = lax.rsqrt(jnp.mean(x * x, axis=-1, keepdims=True) + epsilon)

time: 593 us -> 586 us (0.988)
    unnamed x43 -> x45, local copies, waits for them, and re-layouts: 13.2 us -> 14 us
where the time goes in v5:
time: 586 us; the launch traced here: 577 us
  Pallas kernels  531 us (91%)
  local copies, waits for them, and re-layouts  21.6 us (4%)
  other arithmetic  17.7 us (3%)
  matrix products  6.06 us (1%)
    pallas_call x1, Pallas kernels, moe(): pl.pallas_call(functools.partial(moe_kernel, steps), out_shape=(jax.Shape...  244 us
    pallas_call x1, Pallas kernels, front(): pl.pallas_call(front_kernel, out_shape=(shape((4, 4, 2, wrows // 16, 16,...  167 us
    pallas_call x1, Pallas kernels, back(): pl.pallas_call(back_kernel, out_shape=(shape((tokens, width), f32), weigh...  120 us
    unnamed x45, local copies, waits for them, and re-layouts  14 us

profile of v5, /device:TPU:0, one launch (start us, length us, event | category | flops | bytes accessed | tf_op | source)
XLA Modules:
  0.0 577.0 jit_solution(5418408379458895989)
XLA Ops:
  0.6 0.7 convert_element_type.57
  1.3 0.7 fusion.11
  2.0 0.9 maximum_select_fusion
  2.9 1.3 add_convert_fusion.pack_ref
  4.2 2.0 fusion.10
  6.2 1.3 pad_maximum_fusion
  7.5 166.8 %shard_map.263 = (bf16[4,4,2,4,16,2048]{5,4,3,2,1,0:T(8,128)(2,1)}, bf16[8,4,4,2,16,2048]{5,4,3,2,1,0:T(8,128)(2,1)}, bf16[4,4,2,64,128]{4,3,2,1,0:T(8,128)(2,1)...) custom-call(bf16[128,2048]{1,0:T(8,128)(2,1)} %bitcast.85, ...), custom_call_target="tpu_custom_call" | custom-call | flops 10000000000 | bytes 200000000 | tf_op jit(solution)/shard_map/pallas_call | solution.py:1093
  174.3 1.4 multiply_reduce_fusion.2
  175.7 0.9 bitcast_reduce_fusion
  176.6 0.0 copy-done.15
  176.6 0.9 slice.74
  177.5 0.3 copy.49
  177.8 2.2 copy.45
  180.0 0.9 slice.75
  180.9 0.3 copy.50
  181.2 0.9 pad.36.router_ref
  182.1 244.0 %shard_map.264 = (bf16[8,4,4,2,16,2048]{5,4,3,2,1,0:T(8,128)(2,1)}, f32[8,16,2048]{2,1,0:T(8,128)}, f32[8,16,2176]{2,1,0:T(8,128)}, f32[2048,512]{1,0:T(8,128)},...) custom-call(bf16[8,16,2048]{2,1,0:T(8,128)(2,1)} %bitcast.84, bf16[8,4,4,2,16,2048]{5,4,3,2,1,0:T(8,128)(2,1)} %get-tuple-element.39.c_ref, ...), custom_call_target="tpu_custom_call" | custom-call | flops 77999996928 | bytes 100000000 | tf_op jit(solution)/shard_map/pallas_call | solution.py:544
  426.1 0.0 copy-start.9
  426.1 1.0 slice_add_fusion
  427.1 0.1 copy.47
  427.2 0.0 copy-done.6
  427.2 0.0 copy-start.8
  427.2 0.3 select_reduce_fusion
  427.6 0.0 copy-done
  427.6 0.0 copy-start.1
  427.7 1.9 multiply_reduce_fusion
  429.6 0.0 copy-done.9
  429.6 0.0 copy-done.8
  429.6 1.2 fusion.17
  430.8 0.8 copy-done.1
  431.6 3.7 convolution_convert_fusion.ga_home
  435.3 0.0 copy-done.5
  435.3 0.0 copy-done.10
  435.3 0.4 slice_reduce_fusion
  435.7 0.6 broadcast_in_dim.73.seg_ref
  436.3 0.1 pad.43.clone
  436.4 0.7 maximum_maximum_fusion.gain_ref
  437.0 0.2 fusion.19
  437.2 0.1 concatenate.24
  437.4 0.1 pad.40.clone
  437.5 0.1 pad.38.clone
  437.5 0.8 maximum_bitcast_fusion.small_ref
  438.3 119.8 %shard_map.265 = (f32[128,2048]{1,0:T(8,128)}, f32[64,2048]{1,0:T(8,128)}, f32[64,2048]{1,0:T(8,128)}, f32[64,2048]{1,0:T(8,128)}, f32[64,2048]{1,0:T(8,128)}, /*index=5*/f32[24,128]{1,0:T(8,128)}) custom-call(bf16[128,2048]{1,0:T(8,128)(2,1)} %convolution_convert_fusion.ga_home, bf16[128,2048]{1,0:T(8,128)(2,1)} %get-tuple-element.44.attended_ref, ...), custom_call_target="tpu_custom_call" | custom-call | flops 10000000000 | bytes 200000000 | tf_op jit(solution)/shard_map/pallas_call | solution.py:1573
  558.1 0.0 copy-start.16
  558.1 0.0 copy-start.17
  558.1 0.0 copy-start.14
  558.1 0.0 copy-start.13
  558.1 0.0 copy-start.12
  558.2 1.7 fusion
  559.8 2.6 fusion.4
  562.4 0.0 copy-done.17
  562.4 0.6 fusion.16
  563.0 0.6 dynamic-slice_bitcast_fusion.1
  563.6 0.7 dynamic-slice_bitcast_fusion
  564.3 0.8 copy.58
  565.1 0.0 copy-done.13
  565.1 0.8 copy.59
  565.9 0.8 copy.60
  566.7 0.8 copy.61
  567.5 2.1 copy.62
  569.6 1.6 copy-done.3
  571.2 2.1 copy.63
  573.3 1.6 copy-done.2
  574.9 2.0 copy.64
  (35 shorter events, 0.3 us)
Async XLA Ops:
  7.5 169.1 %copy-start.15 = (s32[1,128,8]{1,2,0:T(8,128)S(1)}, s32[1,128,8]{1,2,0:T(8,128)}, u32[]{:S(2)}) copy-start(s32[1,128,8]{1,2,0:T(8,128)} %param.18) | copy-start | bytes 12292
  182.1 245.1 %copy-start.6 = (bf16[128,2048]{1,0:T(8,128)(2,1)S(1)}, bf16[128,2048]{1,0:T(8,128)(2,1)}, u32[]{:S(2)}) copy-start(bf16[128,2048]{1,0:T(8,128)(2,1)} %get-tuple-element.38) | copy-start | bytes 1572868
  182.1 245.5 %copy-start = (f32[128,2048]{1,0:T(8,128)S(1)}, f32[128,2048]{1,0:T(8,128)}, u32[]{:S(2)}) copy-start(f32[128,2048]{1,0:T(8,128)} %get-tuple-element.37) | copy-start | bytes 3145732
  426.1 3.5 copy-start.9
  427.2 2.3 copy-start.8
  427.6 4.0 copy-start.1
  430.8 4.4 copy-start.5
  431.6 3.7 copy-start.10
  438.3 119.8 %copy-start.7 = (bf16[1,128,2048]{2,1,0:T(8,128)(2,1)S(1)}, bf16[1,128,2048]{2,1,0:T(8,128)(2,1)}, u32[]{:S(2)}) copy-start(bf16[1,128,2048]{2,1,0:T(8,128)(2,1)} %param.16) | copy-start | bytes 1572868
  558.1 4.3 copy-start.16
  558.1 4.3 copy-start.17
  558.1 6.2 %copy-start.14 = (f32[64,2048]{1,0:T(8,128)S(1)}, f32[64,2048]{1,0:T(8,128)}, u32[]{:S(2)}) copy-start(f32[64,2048]{1,0:T(8,128)} %get-tuple-element.106) | copy-start | bytes 1572868
  558.1 6.9 %copy-start.13 = (f32[64,2048]{1,0:T(8,128)S(1)}, f32[64,2048]{1,0:T(8,128)}, u32[]{:S(2)}) copy-start(f32[64,2048]{1,0:T(8,128)} %get-tuple-element.107) | copy-start | bytes 1572868
  558.1 7.7 %copy-start.12 = (f32[64,2048]{1,0:T(8,128)S(1)}, f32[64,2048]{1,0:T(8,128)}, u32[]{:S(2)}) copy-start(f32[64,2048]{1,0:T(8,128)} %get-tuple-element.108) | copy-start | bytes 1572868
  558.2 8.5 %copy-start.11 = (f32[64,2048]{1,0:T(8,128)S(1)}, f32[64,2048]{1,0:T(8,128)}, u32[]{:S(2)}) copy-start(f32[64,2048]{1,0:T(8,128)} %get-tuple-element.109) | copy-start | bytes 1572868
  563.0 4.5 copy-start.4
  567.5 3.7 copy-start.3
  571.2 3.7 copy-start.2

commit v6 on v5

--- a/solution.py
+++ b/solution.py
@@ -1049,8 +1049,6 @@
             )
             stat = jnp.where(lane == 3 + h, top, jnp.where(lane == 5 + h, share, stat))
         stat_ref[rows, :] = stat
-        if t % 2:
-            tick()
     start(saves[3:])
     home_ref[:, columns(blk)] = att_low[blk]
     start(home_copies)

time: 586 us -> 585 us (level)
  no operation moved by 1% of the time
where the time goes in v6:
time: 585 us; the launch traced here: 576 us
  Pallas kernels  529 us (90%)
  local copies, waits for them, and re-layouts  21.6 us (4%)
  other arithmetic  17.7 us (3%)
  matrix products  6.06 us (1%)
    pallas_call x1, Pallas kernels, moe(): pl.pallas_call(functools.partial(moe_kernel, steps), out_shape=(jax.Shape...  243 us
    pallas_call x1, Pallas kernels, front(): pl.pallas_call(front_kernel, out_shape=(shape((4, 4, 2, wrows // 16, 16,...  168 us
    pallas_call x1, Pallas kernels, back(): pl.pallas_call(back_kernel, out_shape=(shape((tokens, width), f32), weigh...  119 us
    unnamed x45, local copies, waits for them, and re-layouts  14 us

profile of v6, /device:TPU:0, one launch (start us, length us, event | category | flops | bytes accessed | tf_op | source)
XLA Modules:
  0.0 575.5 jit_solution(1450407828577581182)
XLA Ops:
  0.6 0.7 convert_element_type.57
  1.3 0.7 fusion.11
  2.0 0.9 maximum_select_fusion
  2.9 1.3 add_convert_fusion.pack_ref
  4.2 2.0 fusion.10
  6.2 1.3 pad_maximum_fusion
  7.5 167.6 %shard_map.263 = (bf16[4,4,2,4,16,2048]{5,4,3,2,1,0:T(8,128)(2,1)}, bf16[8,4,4,2,16,2048]{5,4,3,2,1,0:T(8,128)(2,1)}, bf16[4,4,2,64,128]{4,3,2,1,0:T(8,128)(2,1)...) custom-call(bf16[128,2048]{1,0:T(8,128)(2,1)} %bitcast.85, ...), custom_call_target="tpu_custom_call" | custom-call | flops 10000000000 | bytes 200000000 | tf_op jit(solution)/shard_map/pallas_call | solution.py:1091
  175.1 1.4 multiply_reduce_fusion.2
  176.5 0.9 bitcast_reduce_fusion
  177.4 0.0 copy-done.15
  177.4 0.9 slice.74
  178.4 0.3 copy.49
  178.7 2.2 copy.45
  180.8 0.9 slice.75
  181.8 0.3 copy.50
  182.0 0.9 pad.36.router_ref
  182.9 242.5 %shard_map.264 = (bf16[8,4,4,2,16,2048]{5,4,3,2,1,0:T(8,128)(2,1)}, f32[8,16,2048]{2,1,0:T(8,128)}, f32[8,16,2176]{2,1,0:T(8,128)}, f32[2048,512]{1,0:T(8,128)},...) custom-call(bf16[8,16,2048]{2,1,0:T(8,128)(2,1)} %bitcast.84, bf16[8,4,4,2,16,2048]{5,4,3,2,1,0:T(8,128)(2,1)} %get-tuple-element.39.c_ref, ...), custom_call_target="tpu_custom_call" | custom-call | flops 77999996928 | bytes 100000000 | tf_op jit(solution)/shard_map/pallas_call | solution.py:544
  425.5 0.0 copy-start.9
  425.5 1.0 slice_add_fusion
  426.5 0.1 copy.47
  426.6 0.0 copy-done.6
  426.6 0.0 copy-start.8
  426.6 0.3 select_reduce_fusion
  427.0 0.0 copy-done
  427.0 0.0 copy-start.1
  427.0 1.9 multiply_reduce_fusion
  429.0 0.0 copy-done.9
  429.0 0.0 copy-done.8
  429.0 1.2 fusion.17
  430.2 0.8 copy-done.1
  431.0 3.7 convolution_convert_fusion.ga_home
  434.7 0.0 copy-done.5
  434.7 0.0 copy-done.10
  434.7 0.4 slice_reduce_fusion
  435.1 0.6 broadcast_in_dim.73.seg_ref
  435.7 0.1 pad.43.clone
  435.8 0.7 maximum_maximum_fusion.gain_ref
  436.4 0.2 fusion.19
  436.6 0.1 concatenate.24
  436.8 0.1 pad.40.clone
  436.9 0.1 pad.38.clone
  436.9 0.8 maximum_bitcast_fusion.small_ref
  437.7 118.9 %shard_map.265 = (f32[128,2048]{1,0:T(8,128)}, f32[64,2048]{1,0:T(8,128)}, f32[64,2048]{1,0:T(8,128)}, f32[64,2048]{1,0:T(8,128)}, f32[64,2048]{1,0:T(8,128)}, /*index=5*/f32[24,128]{1,0:T(8,128)}) custom-call(bf16[128,2048]{1,0:T(8,128)(2,1)} %convolution_convert_fusion.ga_home, bf16[128,2048]{1,0:T(8,128)(2,1)} %get-tuple-element.44.attended_ref, ...), custom_call_target="tpu_custom_call" | custom-call | flops 10000000000 | bytes 200000000 | tf_op jit(solution)/shard_map/pallas_call | solution.py:1571
  556.6 0.0 copy-start.16
  556.6 0.0 copy-start.17
  556.6 0.0 copy-start.14
  556.6 0.0 copy-start.13
  556.7 0.0 copy-start.12
  556.7 1.7 fusion
  558.4 2.6 fusion.4
  560.9 0.6 fusion.16
  561.5 0.6 dynamic-slice_bitcast_fusion.1
  562.1 0.7 dynamic-slice_bitcast_fusion
  562.8 0.0 copy-done.14
  562.8 0.8 copy.58
  563.6 0.8 copy.59
  564.4 0.8 copy.60
  565.2 0.8 copy.61
  566.0 0.0 copy-done.4
  566.0 2.1 copy.62
  568.1 1.6 copy-done.3
  569.7 2.1 copy.63
  571.8 1.6 copy-done.2
  573.4 2.0 copy.64
  (35 shorter events, 0.3 us)
Async XLA Ops:
  7.5 169.9 %copy-start.15 = (s32[1,128,8]{1,2,0:T(8,128)S(1)}, s32[1,128,8]{1,2,0:T(8,128)}, u32[]{:S(2)}) copy-start(s32[1,128,8]{1,2,0:T(8,128)} %param.18) | copy-start | bytes 12292
  182.9 243.7 %copy-start.6 = (bf16[128,2048]{1,0:T(8,128)(2,1)S(1)}, bf16[128,2048]{1,0:T(8,128)(2,1)}, u32[]{:S(2)}) copy-start(bf16[128,2048]{1,0:T(8,128)(2,1)} %get-tuple-element.38) | copy-start | bytes 1572868
  182.9 244.1 %copy-start = (f32[128,2048]{1,0:T(8,128)S(1)}, f32[128,2048]{1,0:T(8,128)}, u32[]{:S(2)}) copy-start(f32[128,2048]{1,0:T(8,128)} %get-tuple-element.37) | copy-start | bytes 3145732
  425.5 3.5 copy-start.9
  426.6 2.3 copy-start.8
  427.0 4.0 copy-start.1
  430.2 4.5 copy-start.5
  431.0 3.7 copy-start.10
  437.7 119.0 %copy-start.7 = (bf16[1,128,2048]{2,1,0:T(8,128)(2,1)S(1)}, bf16[1,128,2048]{2,1,0:T(8,128)(2,1)}, u32[]{:S(2)}) copy-start(bf16[1,128,2048]{2,1,0:T(8,128)(2,1)} %param.16) | copy-start | bytes 1572868
  556.6 4.3 copy-start.16
  556.6 4.3 copy-start.17
  556.6 6.2 %copy-start.14 = (f32[64,2048]{1,0:T(8,128)S(1)}, f32[64,2048]{1,0:T(8,128)}, u32[]{:S(2)}) copy-start(f32[64,2048]{1,0:T(8,128)} %get-tuple-element.106) | copy-start | bytes 1572868
  556.6 6.9 %copy-start.13 = (f32[64,2048]{1,0:T(8,128)S(1)}, f32[64,2048]{1,0:T(8,128)}, u32[]{:S(2)}) copy-start(f32[64,2048]{1,0:T(8,128)} %get-tuple-element.107) | copy-start | bytes 1572868
  556.7 7.7 %copy-start.12 = (f32[64,2048]{1,0:T(8,128)S(1)}, f32[64,2048]{1,0:T(8,128)}, u32[]{:S(2)}) copy-start(f32[64,2048]{1,0:T(8,128)} %get-tuple-element.108) | copy-start | bytes 1572868
  556.7 8.5 %copy-start.11 = (f32[64,2048]{1,0:T(8,128)S(1)}, f32[64,2048]{1,0:T(8,128)}, u32[]{:S(2)}) copy-start(f32[64,2048]{1,0:T(8,128)} %get-tuple-element.109) | copy-start | bytes 1572868
  561.5 4.5 copy-start.4
  566.0 3.7 copy-start.3
  569.7 3.7 copy-start.2
